TPU v7x, 32 devices: a whole 2x2x4 slice. The times are simulated.
32 devices in a mesh: rows: 8 (over z, y), seq: 4 (over x, core).
Axes of the slice: x: 2, y: 2, z: 4, core: 2. Of those that a mesh axis runs over, the one named last changes fastest.
Arguments:
- block_input: bfloat16 [8, 1024, 768], P('rows', 'seq'), may hold values from -6 to 6
- output_cotangent: bfloat16 [8, 1024, 768], P('rows', 'seq'), may hold values from -6 to 6
- doc_ids: int32 [8, 1024], P('rows'), may hold values from 0 to 510, as said below
- w_qkv: bfloat16 [2, 768, 2304], P(None, 'seq'), may hold values from -0.21875 to 0.21875
- w_o: bfloat16 [2, 768, 768], P(None, 'seq'), may hold values from -0.875 to 0.875
- w_fc: bfloat16 [2, 768, 3072], P(None, 'seq'), may hold values from -0.21875 to 0.21875
- w_proj: bfloat16 [2, 3072, 768], P(None, 'seq'), may hold values from -0.21875 to 0.21875
- norm_gain: bfloat16 [2, 2, 768], P(None, None, 'seq'), may hold values from 0.5 to 1.5
- norm_bias: bfloat16 [2, 2, 768], P(None, None, 'seq'), may hold values from -4 to 4
- qv_bias: bfloat16 [2, 2, 768], P(None, None, 'seq'), may hold values from -4 to 4
- out_bias: bfloat16 [2, 2, 768], P(None, None, 'seq'), may hold values from -6 to 6
- fc_bias: bfloat16 [2, 3072], P(None, 'seq'), may hold values from -4 to 4
Outputs:
- block_output: float32 [8, 1024, 768], P('rows', 'seq')
- input_grad: float32 [8, 1024, 768], P('rows', 'seq')
- grad_w_qkv: float32 [2, 768, 2304], P(None, 'seq')
- grad_w_o: float32 [2, 768, 768], P(None, 'seq')
- grad_w_fc: float32 [2, 768, 3072], P(None, 'seq')
- grad_w_proj: float32 [2, 3072, 768], P(None, 'seq')
- grad_norm_gain: float32 [2, 2, 768], P(None, None, 'seq')
- grad_norm_bias: float32 [2, 2, 768], P(None, None, 'seq')
- grad_qv_bias: float32 [2, 2, 768], P(None, None, 'seq')
- grad_out_bias: float32 [2, 2, 768], P(None, None, 'seq')
- grad_fc_bias: float32 [2, 3072], P(None, 'seq')
Inputs may be any that keep to these rules, and one draw needn't show every extreme that they name: `doc_ids`: along each row the ids start at 0 and rise by 0 or 1 from one token to the next; in every row one document has tokens in the first quarter and in the last quarter of the row; in one row every token outside that document is a document of its own.
All inputs are finite; a program needn't handle non-finite values.
Results may differ from a plain program's by a relative error of at most 0.015.
Values may be sent and summed in bfloat16 or wider, within the bound.
No kernel may reach another device: no remote copies, remote signals or barrier semaphores. Data moves between devices by JAX's collectives and lax.ppermute only.
A program may use at most 320 MiB of HBM per device.

v0:
```python
import jax
import jax.numpy as jnp
from jax import lax
from jax.sharding import PartitionSpec as P

H = 12
HD = 64


branch_scale = 48.0 ** (-0.5)
norm_eps = 1e-05
masked_score = -1e30


def layer_norm(values, norm_scale, norm_shift):
    centre = values - jnp.mean(values, axis=-1, keepdims=True)
    spread = jnp.mean(centre * centre, axis=-1, keepdims=True)
    return centre * lax.rsqrt(spread + norm_eps) * norm_scale + norm_shift


def gelu_tanh(values):
    return jax.nn.gelu(values, approximate=True)


def matmul(left, right):
    return jnp.dot(left, right, preferred_element_type=jnp.float32)


def matmul_tn(left, right):
    return lax.dot_general(
        left, right, (((0,), (0,)), ((), ())), preferred_element_type=jnp.float32
    )


def matmul_nt(left, right):
    return lax.dot_general(
        left, right, (((1,), (1,)), ((), ())), preferred_element_type=jnp.float32
    )


def fetch_params(sharded, layer_index):
    w_qkv, w_o, w_fc, w_proj, norm_gain, norm_bias, qv_bias, out_bias, fc_bias = sharded
    return (
        lax.all_gather(w_qkv[layer_index], "seq", axis=0, tiled=True),
        lax.all_gather(w_o[layer_index], "seq", axis=0, tiled=True),
        lax.all_gather(w_fc[layer_index], "seq", axis=0, tiled=True),
        lax.all_gather(w_proj[layer_index], "seq", axis=0, tiled=True),
        lax.all_gather(norm_gain[layer_index], "seq", axis=1, tiled=True),
        lax.all_gather(norm_bias[layer_index], "seq", axis=1, tiled=True),
        lax.all_gather(qv_bias[layer_index], "seq", axis=1, tiled=True),
        lax.all_gather(out_bias[layer_index], "seq", axis=1, tiled=True),
        lax.all_gather(fc_bias[layer_index], "seq", axis=0, tiled=True),
    )


def fetch_again(sharded, layer_index):
    w_qkv, w_o, w_fc, w_proj, norm_gain, norm_bias, qv_bias, out_bias, fc_bias = sharded
    return (
        lax.all_gather(w_qkv[layer_index], "seq", axis=0, tiled=True),
        lax.all_gather(w_o[layer_index], "seq", axis=0, tiled=True),
        lax.all_gather(w_fc[layer_index], "seq", axis=0, tiled=True),
        lax.all_gather(w_proj[layer_index], "seq", axis=0, tiled=True),
        lax.all_gather(norm_gain[layer_index], "seq", axis=1, tiled=True),
        lax.all_gather(norm_bias[layer_index], "seq", axis=1, tiled=True),
        lax.all_gather(qv_bias[layer_index], "seq", axis=1, tiled=True),
        lax.all_gather(out_bias[layer_index], "seq", axis=1, tiled=True),
        lax.all_gather(fc_bias[layer_index], "seq", axis=0, tiled=True),
    )


def block_scores(block_q, key_rows, doc_row, first_row, score_scale):
    block_rows = block_q.shape[0]
    length = doc_row.shape[0]
    scores = (
        jnp.einsum("qhd,khd->hqk", block_q, key_rows, preferred_element_type=jnp.float32)
        * score_scale
    )
    key_pos = lax.broadcasted_iota(jnp.int32, (block_rows, length), 1)
    query_pos = first_row + lax.broadcasted_iota(jnp.int32, (block_rows, length), 0)
    query_doc = lax.dynamic_slice_in_dim(doc_row, first_row, block_rows)
    allowed = (key_pos <= query_pos) & (doc_row[None, :] == query_doc[:, None])
    return jnp.where(allowed[None], scores, masked_score)


def attention_forward(head_rows, doc_row):
    length, _, local_heads, head_size = head_rows.shape
    score_scale = head_size ** (-0.5)
    block_rows = min(512, length)
    queries = head_rows[:, 0]
    key_rows = head_rows[:, 1]
    value_rows = head_rows[:, 2]

    def one_block(block_index):
        first_row = block_index * block_rows
        block_q = lax.dynamic_slice_in_dim(queries, first_row, block_rows)
        scores = block_scores(block_q, key_rows, doc_row, first_row, score_scale)
        row_max = jnp.max(scores, axis=-1, keepdims=True)
        weights = jnp.exp(scores - row_max)
        row_total = jnp.sum(weights, axis=-1, keepdims=True)
        probs_low = (weights / row_total).astype(jnp.bfloat16)
        mixed_rows = jnp.einsum(
            "hqk,khd->qhd", probs_low, value_rows, preferred_element_type=jnp.float32
        )
        return (mixed_rows.astype(jnp.bfloat16), (row_max + jnp.log(row_total))[..., 0])

    mixed_rows, log_total = lax.map(one_block, jnp.arange(length // block_rows, dtype=jnp.int32))
    return (mixed_rows.reshape(length, local_heads, head_size), log_total)


def attention_backward(head_rows, doc_row, log_total, grad_mixed):
    length, _, local_heads, head_size = head_rows.shape
    score_scale = head_size ** (-0.5)
    block_rows = min(512, length)
    queries = head_rows[:, 0]
    key_rows = head_rows[:, 1]
    value_rows = head_rows[:, 2]

    def one_block(running, block_index):
        grad_keys, grad_values = running
        first_row = block_index * block_rows
        block_q = lax.dynamic_slice_in_dim(queries, first_row, block_rows)
        block_grad = lax.dynamic_slice_in_dim(grad_mixed, first_row, block_rows)
        scores = block_scores(block_q, key_rows, doc_row, first_row, score_scale)
        attn_probs = jnp.exp(scores - log_total[block_index][..., None])
        grad_probs = jnp.einsum(
            "qhd,khd->hqk", block_grad, value_rows, preferred_element_type=jnp.float32
        )
        row_inner = jnp.sum(attn_probs * grad_probs, axis=-1, keepdims=True)
        grad_scores = (attn_probs * (grad_probs - row_inner)).astype(jnp.bfloat16)
        grad_query = (
            jnp.einsum("hqk,khd->qhd", grad_scores, key_rows, preferred_element_type=jnp.float32)
            * score_scale
        )
        grad_keys = (
            grad_keys
            + jnp.einsum("hqk,qhd->khd", grad_scores, block_q, preferred_element_type=jnp.float32)
            * score_scale
        )
        grad_values = grad_values + jnp.einsum(
            "hqk,qhd->khd",
            attn_probs.astype(jnp.bfloat16),
            block_grad,
            preferred_element_type=jnp.float32,
        )
        return ((grad_keys, grad_values), grad_query.astype(jnp.bfloat16))

    zero_rows = jnp.zeros((length, local_heads, head_size), jnp.float32)
    (grad_keys, grad_values), grad_query = lax.scan(
        one_block, (zero_rows, zero_rows), jnp.arange(length // block_rows, dtype=jnp.int32)
    )
    grad_query = grad_query.reshape(length, local_heads, head_size)
    return jnp.stack(
        [grad_query, grad_keys.astype(jnp.bfloat16), grad_values.astype(jnp.bfloat16)], axis=1
    )


def layer_forward(stream, params, doc_row):
    w_qkv, w_o, w_fc, w_proj, norm_gain, norm_bias, qv_bias, out_bias, fc_bias = params
    tokens, model_width = stream.shape
    norm_scale = norm_gain.astype(jnp.float32)
    norm_shift = norm_bias.astype(jnp.float32)
    query_value = qv_bias.astype(jnp.float32)
    qkv_bias = jnp.concatenate([query_value[0], jnp.zeros_like(query_value[0]), query_value[1]])
    ln_a = layer_norm(stream, norm_scale[0], norm_shift[0]).astype(jnp.bfloat16)
    qkv_rows = (matmul(ln_a, w_qkv) + qkv_bias).astype(jnp.bfloat16).reshape(tokens, 3, H, HD)
    head_rows = lax.all_to_all(qkv_rows, "seq", split_axis=2, concat_axis=0, tiled=True)
    mixed_rows, log_total = attention_forward(head_rows, doc_row)
    attended = lax.all_to_all(mixed_rows, "seq", split_axis=0, concat_axis=1, tiled=True).reshape(
        tokens, model_width
    )
    out_shift = out_bias.astype(jnp.float32)
    mid_stream = stream + branch_scale * (matmul(attended, w_o) + out_shift[0])
    ln_c = layer_norm(mid_stream, norm_scale[1], norm_shift[1]).astype(jnp.bfloat16)
    pre_act = matmul(ln_c, w_fc) + fc_bias.astype(jnp.float32)
    act_low = gelu_tanh(pre_act).astype(jnp.bfloat16)
    result = mid_stream + branch_scale * (matmul(act_low, w_proj) + out_shift[1])
    return (result, (ln_a, head_rows, log_total, attended, mid_stream, ln_c, pre_act, act_low))


def layer_backward(stream, params, doc_row, gradient):
    w_qkv, w_o, w_fc, w_proj, norm_gain, norm_bias, qv_bias, out_bias, fc_bias = params
    tokens, model_width = stream.shape
    norm_scale = norm_gain.astype(jnp.float32)
    norm_shift = norm_bias.astype(jnp.float32)
    _, saved = layer_forward(stream, params, doc_row)
    ln_a, head_rows, log_total, attended, mid_stream, ln_c, pre_act, act_low = saved
    grad_mlp = (branch_scale * gradient).astype(jnp.bfloat16)
    grad_w_proj = matmul_tn(act_low, grad_mlp)
    grad_outb_mlp = jnp.sum(grad_mlp, axis=0, dtype=jnp.float32)
    grad_act = matmul_nt(grad_mlp, w_proj)
    grad_pre = jax.vjp(gelu_tanh, pre_act)[1](grad_act)[0].astype(jnp.bfloat16)
    grad_fcb = jnp.sum(grad_pre, axis=0, dtype=jnp.float32)
    grad_w_fc = matmul_tn(ln_c, grad_pre)
    grad_lnc = matmul_nt(grad_pre, w_fc)
    _, norm_back_c = jax.vjp(layer_norm, mid_stream, norm_scale[1], norm_shift[1])
    part_mid, grad_gain_mlp, grad_shift_mlp = norm_back_c(grad_lnc)
    grad_mid = gradient + part_mid
    grad_attn = (branch_scale * grad_mid).astype(jnp.bfloat16)
    grad_w_o = matmul_tn(attended, grad_attn)
    grad_outb_attn = jnp.sum(grad_attn, axis=0, dtype=jnp.float32)
    grad_att = matmul_nt(grad_attn, w_o).astype(jnp.bfloat16).reshape(tokens, H, HD)
    grad_mixed = lax.all_to_all(grad_att, "seq", split_axis=1, concat_axis=0, tiled=True)
    grad_head_rows = attention_backward(head_rows, doc_row, log_total, grad_mixed)
    grad_qkv = lax.all_to_all(
        grad_head_rows, "seq", split_axis=0, concat_axis=2, tiled=True
    ).reshape(tokens, 3 * model_width)
    grad_w_qkv = matmul_tn(ln_a, grad_qkv)
    column_sums = jnp.sum(grad_qkv, axis=0, dtype=jnp.float32).reshape(3, model_width)
    grad_lna = matmul_nt(grad_qkv, w_qkv)
    _, norm_back_a = jax.vjp(layer_norm, stream, norm_scale[0], norm_shift[0])
    part_input, grad_gain_attn, grad_shift_attn = norm_back_a(grad_lna)
    grad_input = grad_mid + part_input
    all_parts = (
        lax.psum_scatter(
            grad_w_qkv.astype(jnp.bfloat16), "seq", scatter_dimension=0, tiled=True
        ).astype(jnp.float32),
        lax.psum_scatter(
            grad_w_o.astype(jnp.bfloat16), "seq", scatter_dimension=0, tiled=True
        ).astype(jnp.float32),
        lax.psum_scatter(
            grad_w_fc.astype(jnp.bfloat16), "seq", scatter_dimension=0, tiled=True
        ).astype(jnp.float32),
        lax.psum_scatter(
            grad_w_proj.astype(jnp.bfloat16), "seq", scatter_dimension=0, tiled=True
        ).astype(jnp.float32),
        lax.psum_scatter(
            jnp.stack([grad_gain_attn, grad_gain_mlp]).astype(jnp.bfloat16),
            "seq",
            scatter_dimension=1,
            tiled=True,
        ).astype(jnp.float32),
        lax.psum_scatter(
            jnp.stack([grad_shift_attn, grad_shift_mlp]).astype(jnp.bfloat16),
            "seq",
            scatter_dimension=1,
            tiled=True,
        ).astype(jnp.float32),
        lax.psum_scatter(
            jnp.stack([column_sums[0], column_sums[2]]).astype(jnp.bfloat16),
            "seq",
            scatter_dimension=1,
            tiled=True,
        ).astype(jnp.float32),
        lax.psum_scatter(
            jnp.stack([grad_outb_attn, grad_outb_mlp]).astype(jnp.bfloat16),
            "seq",
            scatter_dimension=1,
            tiled=True,
        ).astype(jnp.float32),
        lax.psum_scatter(
            grad_fcb.astype(jnp.bfloat16), "seq", scatter_dimension=0, tiled=True
        ).astype(jnp.float32),
    )
    (
        qkv_share,
        wo_share,
        fc_share,
        proj_share,
        gain_share,
        shift_share,
        qv_share,
        outb_share,
        fcb_share,
    ) = all_parts
    layer_grads = lax.psum(
        (
            qkv_share,
            wo_share,
            fc_share,
            proj_share,
            gain_share,
            shift_share,
            qv_share,
            outb_share,
            fcb_share,
        ),
        "rows",
    )
    return (grad_input, layer_grads)


def on_device(
    block_input,
    output_cotangent,
    doc_ids,
    w_qkv,
    w_o,
    w_fc,
    w_proj,
    norm_gain,
    norm_bias,
    qv_bias,
    out_bias,
    fc_bias,
):
    sharded = (w_qkv, w_o, w_fc, w_proj, norm_gain, norm_bias, qv_bias, out_bias, fc_bias)
    doc_row = doc_ids[0]
    layer_count = w_qkv.shape[0]
    current = block_input[0].astype(jnp.float32)
    inputs = []
    fetched = []
    for layer_index in range(layer_count):
        params = fetch_params(sharded, layer_index)
        inputs.append(current)
        fetched.append(params)
        current, _ = layer_forward(current, params, doc_row)
    gradient = output_cotangent[0].astype(jnp.float32)
    shares = [None] * layer_count
    for layer_index in reversed(range(layer_count)):
        params = fetch_again(sharded, layer_index)
        gradient, shares[layer_index] = layer_backward(
            inputs[layer_index], params, doc_row, gradient
        )
    stacked = [
        jnp.stack([shares[layer_index][member] for layer_index in range(layer_count)])
        for member in range(9)
    ]
    return (
        current[None],
        gradient[None],
        stacked[0],
        stacked[1],
        stacked[2],
        stacked[3],
        stacked[4],
        stacked[5],
        stacked[6],
        stacked[7],
        stacked[8],
    )


def solution(mesh):
    in_specs = (
        P("rows", "seq", None),
        P("rows", "seq", None),
        P("rows", None),
        P(None, "seq", None),
        P(None, "seq", None),
        P(None, "seq", None),
        P(None, "seq", None),
        P(None, None, "seq"),
        P(None, None, "seq"),
        P(None, None, "seq"),
        P(None, None, "seq"),
        P(None, "seq"),
    )
    out_specs = (
        P("rows", "seq", None),
        P("rows", "seq", None),
        P(None, "seq", None),
        P(None, "seq", None),
        P(None, "seq", None),
        P(None, "seq", None),
        P(None, None, "seq"),
        P(None, None, "seq"),
        P(None, None, "seq"),
        P(None, None, "seq"),
        P(None, "seq"),
    )
    return jax.shard_map(
        on_device, mesh=mesh, in_specs=in_specs, out_specs=out_specs, check_vma=False
    )
```

profile of v0, /device:TPU:0, one launch (start us, length us, event | category | flops | bytes accessed | tf_op | source)
XLA Modules:
  0.0 1460.1 jit_solution(13311984270841761625)
XLA Ops:
  18.1 10.0 all-gather.12
  28.7 9.1 all-gather.3
  38.4 9.1 all-gather.1
  48.6 7.1 all-gather
  85.9 32.9 %all-gather.5 = bf16[1,2,768]{1,0,2:T(2,128)(2,1)S(1)} all-gather(bf16[1,2,192]{1,0,2:T(2,128)(2,1)S(1)} %copy.234), channel_id=7, replica_groups=mesh['rows'=8,'seq'=4] {'seq'}, dimensions={2}, use_global_device_ids=true | all-gather | bytes 3840 | tf_op jit(solution)/shard_map/all_gather | solution.py:51
  150.4 24.0 %while.74 = (s32[]{:T(128)}, bf16[2,512,3,64]{1,3,2,0:T(8,128)(2,1)S(1)}, s32[2]{0:T(128)S(1)}, s32[1,1024]{1,0:T(1,128)S(1)}, s32[1024]{0:T(1024)S(1)}, /*index...) while((s32[]{:T(128)}, ...), condition=%wide.region_5.6_spmd, body=%wide.region_2.5_spmd.sunk | while | flops 413763072 | bytes 14840007 | solution.py:106
  184.6 8.4 all-gather.7
  193.2 7.7 all-gather.9
  209.4 6.9 fusion.360
  227.9 19.7 %while.77 = (s32[]{:T(128)}, bf16[2,512,3,64]{1,3,2,0:T(8,128)(2,1)S(1)}, f32[2,3,512]{2,1,0:T(4,128)}, s32[2]{0:T(128)S(1)}, s32[1,1024]{1,0:T(1,128)S(1)}, /*i...) while((s32[]{:T(128)}, ...), condition=%wide.region_32.33_spmd, body=%wide.region_29.32_spmd.sunk | while | flops 423197696 | bytes 22221012 | solution.py:106
  264.8 19.5 %while.76 = (s32[]{:T(128)}, bf16[2,512,3,64]{1,3,2,0:T(8,128)(2,1)S(1)}, f32[2,3,512]{2,1,0:T(4,128)}, s32[2]{0:T(128)S(1)}, s32[1,1024]{1,0:T(1,128)S(1)}, /*i...) while((s32[]{:T(128)}, ...), condition=%wide.region_19.20_spmd, body=%wide.region_16.19_spmd.sunk | while | flops 423197696 | bytes 22221012 | solution.py:106
  291.7 13.0 all-gather.16
  320.3 7.5 fusion.366
  347.2 52.3 %while.78 = (s32[]{:T(128)}, f32[1024,3,64]{0,2,1:T(8,128)}, f32[1024,3,64]{0,2,1:T(8,128)}, bf16[2,512,3,64]{1,3,2,0:T(8,128)(2,1)}, s32[2]{0:T(128)S(1)}, /*in...) while((s32[]{:T(128)}, f32[1024,3,64]{0,2,1:T(8,128)}, ...), condition=%wide.region_26.27_spmd.clone, body=%wide.region_24.26_spmd.clone.sunk | while | flops 1032977408 | bytes 87155208 | solution.py:148
  423.5 8.3 all-to-all-done.6
  472.9 53.1 %while.79 = (s32[]{:T(128)}, f32[1024,3,64]{0,2,1:T(8,128)}, f32[1024,3,64]{0,2,1:T(8,128)}, bf16[2,512,3,64]{1,3,2,0:T(8,128)(2,1)}, s32[2]{0:T(128)S(1)}, /*in...) while((s32[]{:T(128)}, f32[1024,3,64]{0,2,1:T(8,128)}, ...), condition=%wide.region_39.40_spmd.clone, body=%wide.region_37.39_spmd.clone.sunk | while | flops 1032977408 | bytes 87155328 | solution.py:148
  537.9 20.2 %all_to_all.172 = bf16[4,2,73728]{2,1,0:T(2,128)(2,1)} all-to-all(bf16[4,2,73728]{2,1,0:T(2,128)(2,1)} %reshape.727), channel_id=1, replica_groups=mesh['rows'=8,'seq'=4] {'seq'}, dimensions={0} | all-to-all | bytes 2359296 | tf_op jit(solution)/shard_map/all_to_all | solution.py:204
  645.1 16.2 %reduce-scatter.43.cloned.1.call-done = bf16[192,3072]{1,0:T(8,128)(2,1)} async-done(((bf16[768,3072]{1,0:T(8,128)(2,1)}), bf16[192,3072]{1,0:T(8,128)(2,1)}) %reduce-scatter.43.cloned.1.call-update) | async-done | bytes 1179664 | tf_op jit(solution)/shard_map/reduce_scatter | solution.py:220
  664.2 47.5 %reduce-scatter.47.cloned.1.call-done = bf16[768,768]{1,0:T(8,128)(2,1)} async-done(((bf16[3072,768]{1,0:T(8,128)(2,1)}), bf16[768,768]{1,0:T(8,128)(2,1)}) %reduce-scatter.47.cloned.1.call-update) | async-done | bytes 1179664 | tf_op jit(solution)/shard_map/reduce_scatter | solution.py:223
  714.6 48.0 %reduce-scatter.41.cloned.1.call-done = bf16[192,3072]{1,0:T(8,128)(2,1)} async-done(((bf16[768,3072]{1,0:T(8,128)(2,1)}), bf16[192,3072]{1,0:T(8,128)(2,1)}) %reduce-scatter.41.cloned.1.call-update) | async-done | bytes 1179664 | tf_op jit(solution)/shard_map/reduce_scatter | solution.py:220
  765.4 47.5 %reduce-scatter.45.cloned.1.call-done = bf16[768,768]{1,0:T(8,128)(2,1)} async-done(((bf16[3072,768]{1,0:T(8,128)(2,1)}), bf16[768,768]{1,0:T(8,128)(2,1)}) %reduce-scatter.45.cloned.1.call-update) | async-done | bytes 1179664 | tf_op jit(solution)/shard_map/reduce_scatter | solution.py:223
  816.8 23.4 %while.75 = (s32[]{:T(128)}, bf16[2,512,3,64]{1,3,2,0:T(8,128)(2,1)S(1)}, s32[2]{0:T(128)S(1)}, s32[1,1024]{1,0:T(1,128)S(1)}, s32[1024]{0:T(1024)S(1)}, /*index...) while((s32[]{:T(128)}, ...), condition=%wide.region_13.14_spmd, body=%wide.region_10.13_spmd.sunk | while | flops 413763072 | bytes 14840007 | solution.py:106
  849.7 7.3 all-to-all-done.3
  861.7 7.8 fusion.246
  870.4 10.1 all-reduce.4
  882.5 19.5 %reduce-scatter.59.cloned.1.call-done = bf16[192,2]{1,0:T(8,128)(2,1)} async-done(((bf16[768,2]{1,0:T(8,128)(2,1)}), bf16[192,2]{1,0:T(8,128)(2,1)}) %reduce-scatter.59.cloned.1.call-update) | async-done | bytes 784
  902.9 21.3 %reduce-scatter.61.cloned.1.call-done = bf16[192,2]{1,0:T(8,128)(2,1)} async-done(((bf16[768,2]{1,0:T(8,128)(2,1)}), bf16[192,2]{1,0:T(8,128)(2,1)}) %reduce-scatter.61.cloned.1.call-update) | async-done | bytes 784
  927.5 18.8 %reduce-scatter.49.cloned.1.call-done = bf16[192,2]{1,0:T(8,128)(2,1)} async-done(((bf16[768,2]{1,0:T(8,128)(2,1)}), bf16[192,2]{1,0:T(8,128)(2,1)}) %reduce-scatter.49.cloned.1.call-update) | async-done | bytes 784
  947.2 21.3 %reduce-scatter.53.cloned.1.call-done = bf16[192,2]{1,0:T(8,128)(2,1)} async-done(((bf16[768,2]{1,0:T(8,128)(2,1)}), bf16[192,2]{1,0:T(8,128)(2,1)}) %reduce-scatter.53.cloned.1.call-update) | async-done | bytes 784
  969.4 21.2 %reduce-scatter.57.cloned.1.call-done = bf16[192,2]{1,0:T(8,128)(2,1)} async-done(((bf16[768,2]{1,0:T(8,128)(2,1)}), bf16[192,2]{1,0:T(8,128)(2,1)}) %reduce-scatter.57.cloned.1.call-update) | async-done | bytes 784
  991.5 38.5 %all-reduce.2 = (f32[1,2,192]{2,1,0:T(2,128)S(1)}, f32[1,2,192]{2,1,0:T(2,128)S(1)}, f32[1,2,192]{2,1,0:T(2,128)S(1)}, f32[1,2,192]{2,1,0:T(2,128)S(1)}, f32[1,2...) all-reduce(f32[1,2,192]{2,1,0:T(2,128)S(1)} %bitcast_convert_fusion, ...), channel_id=1, replica_groups=mesh['rows'=8,'seq'=4] {'rows'}, use_global_device_ids=true, to_apply=%region_65.66 | all-reduce | flops 4608 | bytes 36864 | tf_op jit(solution)/shard_map/psum | solution.py:265
  1033.0 408.4 %all-reduce.7.cloned.1.call-done = (f32[1,192,2304]{2,1,0:T(8,128)}, f32[1,192,2304]{2,1,0:T(8,128)}, f32[1,192,768]{2,1,0:T(8,128)}, f32[1,192,768]{2,1,0:T(8,1...) async-done(((f32[1,192,2304]{2,1,0:T(8,128)}, f32[1,192,2304]{2,1,0:T(8,128)}, ...) | async-done | bytes 14155792 | tf_op jit(solution)/shard_map/psum | solution.py:265
  (774 shorter events, 552.8 us)
Async XLA Ops:
  7.2 68.6 %all-gather.27.cloned.1.call-start = ((), (), s32[]{:S(2)}) async-start(), calls=%async_computation.34 | async-start | bytes 4423680 | tf_op jit(solution)/shard_map/all_gather | solution.py:44
  10.2 196.9 %all-gather.29.cloned.1.call-start = ((), (), s32[]{:S(2)}) async-start(), calls=%async_computation.35 | async-start | bytes 1474560 | tf_op jit(solution)/shard_map/all_gather | solution.py:45
  11.1 198.2 %all-gather.33.cloned.1.call-start = ((), (), s32[]{:S(2)}) async-start(), calls=%async_computation.37 | async-start | bytes 5898240 | tf_op jit(solution)/shard_map/all_gather | solution.py:47
  12.8 196.6 %all-gather.31.cloned.1.call-start = ((), (), s32[]{:S(2)}) async-start(), calls=%async_computation.36 | async-start | bytes 5898240 | tf_op jit(solution)/shard_map/all_gather | solution.py:46
  16.0 200.6 %all-gather.35.cloned.1.call-start = ((), (), s32[]{:S(2)}) async-start(), calls=%async_computation.38 | async-start | bytes 4423680 | tf_op jit(solution)/shard_map/all_gather | solution.py:44
  16.6 295.3 %all-gather.37.cloned.1.call-start = ((), (), s32[]{:S(2)}) async-start(), calls=%async_computation.39 | async-start | bytes 1474560 | tf_op jit(solution)/shard_map/all_gather | solution.py:45
  17.2 297.0 %all-gather.39.cloned.1.call-start = ((), (), s32[]{:S(2)}) async-start(), calls=%async_computation.40 | async-start | bytes 5898240 | tf_op jit(solution)/shard_map/all_gather | solution.py:46
  81.4 63.2 %all-to-all-start = ((bf16[256,3,12,64]{0,3,1,2:T(8,128)(2,1)}), bf16[256,3,12,64]{0,3,1,2:T(8,128)(2,1)S(1)}, u32[]{:S(2)}, u32[]{:S(2)}) async-start(bf16[256,3,12,64]{0,3,1,2:T(8,128)(2,1)} %copy.143), calls=%async_computation | async-start | bytes 2359296 | tf_op jit(solution)/shard_map/all_to_all | solution.py:166
  85.0 235.3 %all-gather.41.cloned.1.call-start = ((), (), s32[]{:S(2)}) async-start(), calls=%async_computation.41 | async-start | bytes 5898240 | tf_op jit(solution)/shard_map/all_gather | solution.py:47
  176.5 29.4 %all-to-all-start.1 = ((bf16[4,2,24576]{2,1,0:T(2,128)(2,1)}), bf16[4,2,24576]{2,1,0:T(2,128)(2,1)S(1)}, u32[]{:S(2)}, u32[]{:S(2)}) async-start(bf16[4,2,24576]{2,1,0:T(2,128)(2,1)} %reshape.717), calls=%async_computation.1 | async-start | bytes 786432 | tf_op jit(solution)/shard_map/all_to_all | solution.py:168
  223.5 31.5 %all-to-all-start.2 = ((bf16[256,3,12,64]{0,3,1,2:T(8,128)(2,1)}), bf16[256,3,12,64]{0,3,1,2:T(8,128)(2,1)S(1)}, u32[]{:S(2)}, u32[]{:S(2)}) async-start(bf16[256,3,12,64]{0,3,1,2:T(8,128)(2,1)} %copy.155), calls=%async_computation.2 | async-start | bytes 2359296 | tf_op jit(solution)/shard_map/all_to_all | solution.py:166
  255.1 33.1 %all-to-all-start.7 = ((bf16[4,2,24576]{2,1,0:T(2,128)(2,1)}), bf16[4,2,24576]{2,1,0:T(2,128)(2,1)S(1)}, u32[]{:S(2)}, u32[]{:S(2)}) async-start(bf16[4,2,24576]{2,1,0:T(2,128)(2,1)} %reshape.725), calls=%async_computation.7 | async-start | bytes 786432 | tf_op jit(solution)/shard_map/all_to_all | solution.py:168
  288.2 20.8 %all-to-all-start.4 = ((bf16[4,2,24576]{2,1,0:T(2,128)(2,1)}), bf16[4,2,24576]{2,1,0:T(2,128)(2,1)S(1)}, u32[]{:S(2)}, u32[]{:S(2)}) async-start(bf16[4,2,24576]{2,1,0:T(2,128)(2,1)} %reshape.721), calls=%async_computation.4 | async-start | bytes 786432 | tf_op jit(solution)/shard_map/all_to_all | solution.py:168
  411.6 20.2 %all-to-all-start.6 = ((bf16[4,2,73728]{2,1,0:T(2,128)(2,1)}), bf16[4,2,73728]{2,1,0:T(2,128)(2,1)}, u32[]{:S(2)}, u32[]{:S(2)}) async-start(bf16[4,2,73728]{2,1,0:T(2,128)(2,1)} %reshape.723), calls=%async_computation.6 | async-start | bytes 2359296 | tf_op jit(solution)/shard_map/all_to_all | solution.py:204
  415.9 220.4 %reduce-scatter.39.cloned.1.call-start = ((), (), s32[]{:S(2)}) async-start(), calls=%async_computation.29 | async-start | bytes 1474560 | tf_op jit(solution)/shard_map/reduce_scatter | solution.py:217
  423.3 214.8 %reduce-scatter.37.cloned.1.call-start = ((), (), s32[]{:S(2)}) async-start(), calls=%async_computation.28 | async-start | bytes 1474560 | tf_op jit(solution)/shard_map/reduce_scatter | solution.py:217
  463.9 176.1 %reduce-scatter.35.cloned.1.call-start = ((), (), s32[]{:S(2)}) async-start(), calls=%async_computation.27 | async-start | bytes 4423680 | tf_op jit(solution)/shard_map/reduce_scatter | solution.py:214
  467.1 175.5 %reduce-scatter.33.cloned.1.call-start = ((), (), s32[]{:S(2)}) async-start(), calls=%async_computation.26 | async-start | bytes 4423680 | tf_op jit(solution)/shard_map/reduce_scatter | solution.py:214
  570.0 91.3 %reduce-scatter.43.cloned.1.call-start = ((), (), s32[]{:S(2)}) async-start(), calls=%async_computation.31 | async-start | bytes 5898240 | tf_op jit(solution)/shard_map/reduce_scatter | solution.py:220
  575.3 136.3 %reduce-scatter.47.cloned.1.call-start = ((), (), s32[]{:S(2)}) async-start(), calls=%async_computation.33 | async-start | bytes 5898240 | tf_op jit(solution)/shard_map/reduce_scatter | solution.py:223
  583.3 179.2 %reduce-scatter.41.cloned.1.call-start = ((), (), s32[]{:S(2)}) async-start(), calls=%async_computation.30 | async-start | bytes 5898240 | tf_op jit(solution)/shard_map/reduce_scatter | solution.py:220
  588.7 224.3 %reduce-scatter.45.cloned.1.call-start = ((), (), s32[]{:S(2)}) async-start(), calls=%async_computation.32 | async-start | bytes 5898240 | tf_op jit(solution)/shard_map/reduce_scatter | solution.py:223
  596.1 273.4 %reduce-scatter.63.cloned.1.call-start = ((), (), s32[]{:S(2)}) async-start(), calls=%async_computation.49 | async-start | bytes 245760
  600.3 280.4 %reduce-scatter.51.cloned.1.call-start = ((), (), s32[]{:S(2)}) async-start(), calls=%async_computation.43 | async-start | bytes 245760
  609.7 271.9 %reduce-scatter.55.cloned.1.call-start = ((), (), s32[]{:S(2)}) async-start(), calls=%async_computation.45 | async-start | bytes 245760
  611.8 290.2 %reduce-scatter.59.cloned.1.call-start = ((), (), s32[]{:S(2)}) async-start(), calls=%async_computation.47 | async-start | bytes 245760
  614.1 310.1 %reduce-scatter.61.cloned.1.call-start = ((), (), s32[]{:S(2)}) async-start(), calls=%async_computation.48 | async-start | bytes 245760
  617.4 328.9 %reduce-scatter.49.cloned.1.call-start = ((), (), s32[]{:S(2)}) async-start(), calls=%async_computation.42 | async-start | bytes 245760
  633.3 335.3 %reduce-scatter.53.cloned.1.call-start = ((), (), s32[]{:S(2)}) async-start(), calls=%async_computation.44 | async-start | bytes 245760
  635.3 355.3 %reduce-scatter.57.cloned.1.call-start = ((), (), s32[]{:S(2)}) async-start(), calls=%async_computation.46 | async-start | bytes 245760
  636.3 805.2 %all-reduce.7.cloned.1.call-start = ((), (), s32[]{:S(2)}) async-start(), calls=%async_computation.50 | async-start | bytes 28311552 | tf_op jit(solution)/shard_map/psum | solution.py:265
  844.1 12.9 all-to-all-start.3
  (175 other events, 2011.9 us)
Sparse Core Ops, SparseCore 0:
  10.3 39.6 all-gather.26
  52.1 17.5 all-gather.28
  71.9 52.1 all-gather.32
  125.5 37.4 all-gather.30
  164.4 35.8 all-gather.34
  201.7 17.2 all-gather.36
  221.1 53.0 all-gather.38
  276.3 41.8 all-gather.40
  423.4 26.9 reduce-scatter.38
  457.8 25.6 reduce-scatter.36
  486.6 40.4 reduce-scatter.34
  570.1 40.1 reduce-scatter.32
  613.4 47.8 reduce-scatter.42
  663.8 47.7 reduce-scatter.46
  714.6 47.8 reduce-scatter.40
  765.1 47.8 reduce-scatter.44
  815.3 19.7 reduce-scatter.62
  837.3 20.2 reduce-scatter.50
  860.1 19.7 reduce-scatter.54
  882.2 19.7 reduce-scatter.58
  904.4 19.7 reduce-scatter.60
  926.6 19.7 reduce-scatter.48
  948.8 19.7 reduce-scatter.52
  970.9 19.7 reduce-scatter.56
  996.8 444.6 all-reduce.6
where the time goes:
time: 1470 us; the launch traced here: 1460 us
  waiting for transfers between devices  702 us (48%)
  matrix products  242 us (16%)
  local copies, waits for them, and re-layouts  184 us (13%)
  blocking collectives  179 us (12%)
  other arithmetic  83.4 us (6%)
  starting transfers between devices  35.6 us (2%)
  between operations  17.1 us (1%)
  loops' own time  16.5 us (1%)
    psum x1, waiting for transfers between devices, layer_backward(): lax.psum((qkv_share, wo_share, fc_share, proj_share, gain_share, shift_sh...  408 us
    unnamed x33, waiting for transfers between devices  105 us
    reduce_scatter x2, waiting for transfers between devices, layer_backward(): lax.psum_scatter(grad_w_proj.astype(jnp.bfloat16), 'seq', scatter_dimensi...  95 us
    reduce_scatter x2, waiting for transfers between devices, layer_backward(): lax.psum_scatter(grad_w_fc.astype(jnp.bfloat16), 'seq', scatter_dimension...  64.1 us
    unnamed x311, local copies, waits for them, and re-layouts  51.9 us
    dot_general x10, matrix products, matmul(): return jnp.dot(left, right, preferred_element_type=jnp.float32)  41.7 us
    all_gather x2, blocking collectives, fetch_params(): lax.all_gather(out_bias[layer_index], 'seq', axis=1, tiled=True)  39.5 us
    psum x1, blocking collectives, layer_backward(): lax.psum((qkv_share, wo_share, fc_share, proj_share, gain_share, shift_sh...  38.5 us
  transfers between devices with their start and end apart: 34, of which 15 were waited for; matrix products, arithmetic and copies ran while one was open for 28% of the time, Pallas kernels for 0%

commit v1 on v0

v1 whole, which is shorter than its diff:
```python
import functools
import math

import jax
import jax.numpy as jnp
from jax import lax
from jax.experimental import pallas as pl
from jax.experimental.pallas import tpu as pltpu
from jax.sharding import PartitionSpec as P

HD = 64
branch_scale = 48.0 ** (-0.5)
norm_eps = 1e-05
masked_score = -1e30
log2_e = math.log2(math.e)
MIB = 1 << 20
BLK = 256

f32 = jnp.float32
bf16 = jnp.bfloat16

SWAP_CORE = [(s, s ^ 1) for s in range(4)]
SWAP_X = [(s, s ^ 2) for s in range(4)]
SWAP_BOTH = [(s, s ^ 3) for s in range(4)]


def dot_nn(a, b):
    return lax.dot_general(a, b, (((1,), (0,)), ((), ())), preferred_element_type=f32)


def dot_nt(a, b):
    return lax.dot_general(a, b, (((1,), (1,)), ((), ())), preferred_element_type=f32)


def dot_tn(a, b):
    return lax.dot_general(a, b, (((0,), (0,)), ((), ())), preferred_element_type=f32)


def call(body, name, sidx, grid, ins, outs, scratch, flops, vmem, exps=0):
    arrays = [a for a, _, _ in ins]
    in_specs = [
        pl.BlockSpec(memory_space=pl.ANY) if b is None else pl.BlockSpec(b, m) for _, b, m in ins
    ]
    out_specs = [pl.BlockSpec(b, m) for _, b, m in outs]
    out_shape = [s for s, _, _ in outs]
    nbytes = sum(a.size * a.dtype.itemsize for a in arrays)
    nbytes += sum(math.prod(s.shape) * s.dtype.itemsize for s in out_shape)
    return pl.pallas_call(
        body,
        name=name,
        grid_spec=pltpu.PrefetchScalarGridSpec(
            num_scalar_prefetch=1,
            grid=grid,
            in_specs=in_specs,
            out_specs=out_specs,
            scratch_shapes=scratch,
        ),
        out_shape=out_shape,
        compiler_params=pltpu.CompilerParams(
            dimension_semantics=("arbitrary",) * len(grid), vmem_limit_bytes=vmem * MIB
        ),
        cost_estimate=pl.CostEstimate(
            flops=int(flops), bytes_accessed=int(nbytes), transcendentals=int(exps)
        ),
    )(sidx, *arrays)


def sds(shape, dtype):
    return jax.ShapeDtypeStruct(shape, dtype)


def whole(block):
    zeros = (0,) * len(block)
    return lambda i, m: zeros


def row_tile(i, m):
    return (i, 0)


def stack_tile(i, m):
    return (i ^ m[0], 0, 0)


def piece_copies(refs, dst, sems, first, rows):
    out = []
    for j, ref in enumerate(refs):
        where = pl.multiple_of((first ^ j) * rows, 16)
        out.append(pltpu.make_async_copy(ref, dst.at[pl.ds(where, rows)], sems.at[j]))
    return out


def normed(x):
    centre = x - jnp.mean(x, axis=-1, keepdims=True)
    spread = jnp.mean(centre * centre, axis=-1, keepdims=True)
    rstd = lax.rsqrt(spread + norm_eps)
    return centre * rstd, rstd


def norm_back(x, grad, gain):
    unit, rstd = normed(x)
    inner = grad * gain
    mean_inner = jnp.mean(inner, axis=-1, keepdims=True)
    mean_prod = jnp.mean(inner * unit, axis=-1, keepdims=True)
    return rstd * (inner - mean_inner - unit * mean_prod), unit


GAIN_A, GAIN_C, SHIFT_A, SHIFT_C, OUT_A, OUT_M = range(6)


def row_of(ref, k):
    return ref[k : k + 1, :]


def qkv_body(first, m, *refs):
    if first:
        x_ref, vec, bias, w0, w1, w2, w3, ln_ref, qkv_ref, w, sems = refs
    else:
        mid_ref, p_ref, r_ref, prev, vec, bias, w0, w1, w2, w3, x_out, ln_ref, qkv_ref, w, sems = refs
    rows = w0.shape[0]
    copies = piece_copies((w0, w1, w2, w3), w, sems, m[0], rows)

    @pl.when(pl.program_id(0) == 0)
    def _():
        for cp in copies:
            cp.start()

    if first:
        x = x_ref[0].astype(f32)
    else:
        part = p_ref[...].astype(f32) + r_ref[...].astype(f32) + row_of(prev, OUT_M)
        x = mid_ref[...] + branch_scale * part
        x_out[...] = x
    unit, _ = normed(x)
    ln = (unit * row_of(vec, GAIN_A) + row_of(vec, SHIFT_A)).astype(bf16)
    ln_ref[...] = ln

    @pl.when(pl.program_id(0) == 0)
    def _():
        for cp in copies:
            cp.wait()

    qkv_ref[...] = (dot_nn(ln, w[...]) + bias[...]).astype(bf16)


def qkv_forward(sidx, source, vec, prev_vec, bias, pieces):
    rows, cols = pieces[0].shape
    depth = 4 * rows
    first = len(source) == 1
    tokens = source[0].shape[0] * source[0].shape[1] if first else source[0].shape[0]
    ins = []
    outs = []
    if first:
        ins.append((source[0], (1, BLK, depth), stack_tile))
    else:
        for a in source:
            ins.append((a, (BLK, depth), row_tile))
        ins.append((prev_vec, prev_vec.shape, whole(prev_vec.shape)))
        outs.append((sds((tokens, depth), f32), (BLK, depth), row_tile))
    ins.append((vec, vec.shape, whole(vec.shape)))
    ins.append((bias, bias.shape, whole(bias.shape)))
    ins += [(p, None, None) for p in pieces]
    outs.append((sds((tokens, depth), bf16), (BLK, depth), row_tile))
    outs.append((sds((tokens, cols), bf16), (BLK, cols), row_tile))
    return call(
        functools.partial(qkv_body, first),
        "norm_qkv",
        sidx,
        (tokens // BLK,),
        ins,
        outs,
        [pltpu.VMEM((depth, cols), bf16), pltpu.SemaphoreType.DMA((4,))],
        2 * tokens * depth * cols,
        24,
    )


def lane_half(shape):
    return lax.broadcasted_iota(jnp.int32, shape, 1) // HD


def block_start(i):
    return BLK * (i * (i + 1) // 2)


def attn_body(m, q_ref, k_ref, v_ref, drow, dcol, wo0, wo1, att_ref, lse_ref, part_ref, bias, wo, held, sems):
    pair = pl.program_id(0)
    tokens = q_ref.shape[0]
    blocks = tokens // BLK
    rows = wo0.shape[0]
    copies = piece_copies((wo0, wo1), wo, sems, m[1], rows)

    @pl.when(pair == 0)
    def _():
        for cp in copies:
            cp.start()
        for i in range(blocks):
            width = BLK * (i + 1)
            first = i * BLK
            qpos = first + lax.broadcasted_iota(jnp.int32, (BLK, width), 0)
            kpos = lax.broadcasted_iota(jnp.int32, (BLK, width), 1)
            same = dcol[first : first + BLK, :] == drow[:, :width]
            allowed = (kpos <= qpos) & same
            bias[:, block_start(i) : block_start(i) + width] = jnp.where(allowed, 0.0, masked_score)

    half = lane_half((BLK, 2 * HD))
    scale = HD ** (-0.5) * log2_e
    for i in range(blocks):
        width = BLK * (i + 1)
        span = slice(i * BLK, (i + 1) * BLK)
        qb = q_ref[span, :]
        kk = k_ref[:width, :]
        vv = v_ref[:width, :]
        mixed = []
        logs = []
        for h in range(2):
            qh = jnp.where(half == h, qb, jnp.zeros_like(qb))
            t = dot_nt(qh, kk) * scale + bias[:, block_start(i) : block_start(i) + width]
            top = jnp.max(t, axis=-1, keepdims=True)
            p = jnp.exp2(t - top)
            total = jnp.sum(p, axis=-1, keepdims=True)
            o = dot_nn(p.astype(bf16), vv)
            mixed.append(o / total)
            logs.append(jnp.broadcast_to(top + jnp.log2(total), (BLK, 2 * HD)))
        att = jnp.where(half == 0, mixed[0], mixed[1]).astype(bf16)
        att_ref[span, :] = att
        held[pair, span, :] = att
        turned = jnp.transpose(jnp.where(half == 0, logs[0], logs[1]))
        lse_ref[0, 0:1, span] = turned[0:1, :]
        lse_ref[0, 1:2, span] = turned[HD : HD + 1, :]

    @pl.when(pair == pl.num_programs(0) - 1)
    def _():
        for cp in copies:
            cp.wait()
        for i in range(blocks):
            span = slice(i * BLK, (i + 1) * BLK)
            row = jnp.concatenate([held[p, span, :] for p in range(held.shape[0])], axis=1)
            part_ref[span, :] = dot_nn(row, wo[...]).astype(bf16)


def attention_forward(sidx, qkv, drow, dcol, wo_pieces):
    tokens = qkv.shape[0]
    width = qkv.shape[1] // 3
    pairs = width // (2 * HD)
    depth = wo_pieces[0].shape[1]
    col = lambda k: (lambda i, m: (0, k * pairs + i))
    pair_block = (tokens, 2 * HD)
    ins = [(qkv, pair_block, col(0)), (qkv, pair_block, col(1)), (qkv, pair_block, col(2))]
    ins += [(drow, drow.shape, whole(drow.shape)), (dcol, dcol.shape, whole(dcol.shape))]
    ins += [(p, None, None) for p in wo_pieces]
    outs = [
        (sds((tokens, width), bf16), pair_block, lambda i, m: (0, i)),
        (sds((pairs, 8, tokens), f32), (1, 8, tokens), lambda i, m: (i, 0, 0)),
        (sds((tokens, depth), bf16), (tokens, depth), whole((0, 0))),
    ]
    blocks = tokens // BLK
    scratch = [
        pltpu.VMEM((BLK, block_start(blocks)), f32),
        pltpu.VMEM((width, depth), bf16),
        pltpu.VMEM((pairs, tokens, 2 * HD), bf16),
        pltpu.SemaphoreType.DMA((2,)),
    ]
    return call(
        attn_body,
        "attention_forward",
        sidx,
        (pairs,),
        ins,
        outs,
        scratch,
        4 * tokens * tokens * width,
        40,
        exps=tokens * tokens * pairs,
    )


def mlp_body(first, m, x_ref, p_ref, r_ref, vec, fcb, f0, f1, f2, f3, j0, j1, mid_ref, ln_ref, act_ref, slope_ref, part_ref, wf, wp, sems):
    copies = piece_copies((f0, f1, f2, f3), wf, sems, m[0], f0.shape[0])
    copies2 = piece_copies((j0, j1), wp, sems.at[pl.ds(4, 2)], m[1], j0.shape[0])

    @pl.when(pl.program_id(0) == 0)
    def _():
        for cp in copies + copies2:
            cp.start()

    x = x_ref[0].astype(f32) if first else x_ref[...]
    part = p_ref[...].astype(f32) + r_ref[...].astype(f32) + row_of(vec, OUT_A)
    mid = x + branch_scale * part
    mid_ref[...] = mid
    unit, _ = normed(mid)
    ln = (unit * row_of(vec, GAIN_C) + row_of(vec, SHIFT_C)).astype(bf16)
    ln_ref[...] = ln

    @pl.when(pl.program_id(0) == 0)
    def _():
        for cp in copies:
            cp.wait()

    pre = dot_nn(ln, wf[...]) + fcb[...]
    root = math.sqrt(2.0 / math.pi)
    sq = pre * pre
    th = jnp.tanh(root * pre * (1.0 + 0.044715 * sq))
    gate = 0.5 * (1.0 + th)
    act = (pre * gate).astype(bf16)
    act_ref[...] = act
    inner = root * (1.0 + 3.0 * 0.044715 * sq)
    slope_ref[...] = (gate + 0.5 * pre * (1.0 - th * th) * inner).astype(bf16)

    @pl.when(pl.program_id(0) == 0)
    def _():
        for cp in copies2:
            cp.wait()

    part_ref[...] = dot_nn(act, wp[...]).astype(bf16)


def mlp_forward(sidx, x, part, recv, vec, fcb, fc_pieces, proj_pieces):
    first = x.ndim == 3
    tokens, depth = part.shape
    hidden = fc_pieces[0].shape[1]
    ins = [(x, (1, BLK, depth), stack_tile) if first else (x, (BLK, depth), row_tile)]
    ins += [(part, (BLK, depth), row_tile), (recv, (BLK, depth), row_tile)]
    ins += [(vec, vec.shape, whole(vec.shape)), (fcb, fcb.shape, whole(fcb.shape))]
    ins += [(p, None, None) for p in fc_pieces + proj_pieces]
    outs = [
        (sds((tokens, depth), f32), (BLK, depth), row_tile),
        (sds((tokens, depth), bf16), (BLK, depth), row_tile),
        (sds((tokens, hidden), bf16), (BLK, hidden), row_tile),
        (sds((tokens, hidden), bf16), (BLK, hidden), row_tile),
        (sds((tokens, depth), bf16), (BLK, depth), row_tile),
    ]
    scratch = [
        pltpu.VMEM((depth, hidden), bf16),
        pltpu.VMEM((hidden, depth), bf16),
        pltpu.SemaphoreType.DMA((6,)),
    ]
    return call(
        functools.partial(mlp_body, first),
        "mlp_forward",
        sidx,
        (tokens // BLK,),
        ins,
        outs,
        scratch,
        4 * tokens * depth * hidden,
        32,
        exps=tokens * hidden,
    )


def add_rows(ref, value, start):
    @pl.when(start)
    def _():
        ref[...] = jnp.zeros_like(ref)

    ref[...] += jnp.sum(value, axis=0, keepdims=True)


def mlp_back_body(last, m, *refs):
    if last:
        g_ref, slope_ref, f0, f1, f2, f3, j0, j1 = refs[:8]
        dmlp_ref, dpre_ref, part_ref, sum_mlp, sum_pre, wf, wp, sems = refs[8:]
    else:
        gm_ref, x_ref, p_ref, r_ref, nvec, slope_ref, f0, f1, f2, f3, j0, j1 = refs[:12]
        g_out, dmlp_ref, dpre_ref, part_ref, sum_mlp, sum_pre, sum_gain, sum_shift, wf, wp, sems = refs[12:]
    start = pl.program_id(0) == 0
    copies = piece_copies((f0, f1, f2, f3), wf, sems, m[0], f0.shape[0])
    copies2 = piece_copies((j0, j1), wp, sems.at[pl.ds(4, 2)], m[1], j0.shape[0])

    @pl.when(start)
    def _():
        for cp in copies2 + copies:
            cp.start()

    if last:
        g = g_ref[0].astype(f32)
    else:
        grad = p_ref[...].astype(f32) + r_ref[...].astype(f32)
        part, unit = norm_back(x_ref[...], grad, row_of(nvec, GAIN_A))
        add_rows(sum_gain, grad * unit, start)
        add_rows(sum_shift, grad, start)
        g = gm_ref[...] + part
        g_out[...] = g
    dmlp = (branch_scale * g).astype(bf16)
    dmlp_ref[...] = dmlp
    add_rows(sum_mlp, dmlp.astype(f32), start)

    @pl.when(start)
    def _():
        for cp in copies2:
            cp.wait()

    dact = dot_nt(dmlp, wp[...])
    dpre = (dact * slope_ref[...].astype(f32)).astype(bf16)
    dpre_ref[...] = dpre
    add_rows(sum_pre, dpre.astype(f32), start)

    @pl.when(start)
    def _():
        for cp in copies:
            cp.wait()

    part_ref[...] = dot_nt(dpre, wf[...]).astype(bf16)


def mlp_backward(sidx, source, slope, fc_pieces, proj_pieces):
    last = len(source) == 1
    tokens, hidden = slope.shape
    depth = proj_pieces[0].shape[1]
    tile = (BLK, depth)
    ins = []
    outs = []
    if last:
        ins.append((source[0], (1, BLK, depth), stack_tile))
    else:
        gm, x, part, recv, vec = source
        ins += [(a, tile, row_tile) for a in (gm, x, part, recv)]
        ins.append((vec, vec.shape, whole(vec.shape)))
        outs.append((sds((tokens, depth), f32), tile, row_tile))
    ins.append((slope, (BLK, hidden), row_tile))
    ins += [(p, None, None) for p in fc_pieces + proj_pieces]
    outs += [
        (sds((tokens, depth), bf16), tile, row_tile),
        (sds((tokens, hidden), bf16), (BLK, hidden), row_tile),
        (sds((tokens, depth), bf16), tile, row_tile),
        (sds((1, depth), f32), (1, depth), whole((0, 0))),
        (sds((1, hidden), f32), (1, hidden), whole((0, 0))),
    ]
    if not last:
        outs += [(sds((1, depth), f32), (1, depth), whole((0, 0)))] * 2
    scratch = [
        pltpu.VMEM((depth, hidden), bf16),
        pltpu.VMEM((hidden, depth), bf16),
        pltpu.SemaphoreType.DMA((6,)),
    ]
    return call(
        functools.partial(mlp_back_body, last),
        "mlp_backward",
        sidx,
        (tokens // BLK,),
        ins,
        outs,
        scratch,
        4 * tokens * depth * hidden,
        32,
    )


def out_back_body(last, m, g_ref, mid_ref, p_ref, r_ref, vec, wo0, wo1, gm_ref, dattn_ref, datt_ref, sum_attn, sum_gain, sum_shift, wo, sems):
    start = pl.program_id(0) == 0
    copies = piece_copies((wo0, wo1), wo, sems, m[1], wo0.shape[0])

    @pl.when(start)
    def _():
        for cp in copies:
            cp.start()

    g = g_ref[0].astype(f32) if last else g_ref[...]
    grad = p_ref[...].astype(f32) + r_ref[...].astype(f32)
    part, unit = norm_back(mid_ref[...], grad, row_of(vec, GAIN_C))
    add_rows(sum_gain, grad * unit, start)
    add_rows(sum_shift, grad, start)
    gm = g + part
    gm_ref[...] = gm
    dattn = (branch_scale * gm).astype(bf16)
    dattn_ref[...] = dattn
    add_rows(sum_attn, dattn.astype(f32), start)

    @pl.when(start)
    def _():
        for cp in copies:
            cp.wait()

    datt_ref[...] = dot_nt(dattn, wo[...]).astype(bf16)


def out_backward(sidx, g, mid, part, recv, vec, wo_pieces):
    last = g.ndim == 3
    tokens, depth = part.shape
    width = 2 * wo_pieces[0].shape[0]
    tile = (BLK, depth)
    ins = [(g, (1, BLK, depth), stack_tile) if last else (g, tile, row_tile)]
    ins += [(a, tile, row_tile) for a in (mid, part, recv)]
    ins.append((vec, vec.shape, whole(vec.shape)))
    ins += [(p, None, None) for p in wo_pieces]
    outs = [
        (sds((tokens, depth), f32), tile, row_tile),
        (sds((tokens, depth), bf16), tile, row_tile),
        (sds((tokens, width), bf16), (BLK, width), row_tile),
    ]
    outs += [(sds((1, depth), f32), (1, depth), whole((0, 0)))] * 3
    return call(
        functools.partial(out_back_body, last),
        "out_backward",
        sidx,
        (tokens // BLK,),
        ins,
        outs,
        [pltpu.VMEM((width, depth), bf16), pltpu.SemaphoreType.DMA((2,))],
        2 * tokens * depth * width,
        24,
    )


def attn_back_body(m, q_ref, k_ref, v_ref, do_ref, att_ref, lse_ref, drow, dcol, w0, w1, w2, w3, dqkv_ref, part_ref, sum_ref, bias, w, held, dq_acc, sems):
    pair = pl.program_id(0)
    pairs = pl.num_programs(0)
    tokens = q_ref.shape[0]
    blocks = tokens // BLK
    copies = piece_copies((w0, w1, w2, w3), w, sems, m[0], w0.shape[0])
    starts = [sum(tokens - BLK * a for a in range(j)) for j in range(blocks)]

    @pl.when(pair == 0)
    def _():
        for cp in copies:
            cp.start()
        for j in range(blocks):
            width = tokens - j * BLK
            first = j * BLK
            kpos = lax.broadcasted_iota(jnp.int32, (BLK, width), 0)
            qpos = lax.broadcasted_iota(jnp.int32, (BLK, width), 1)
            same = dcol[first : first + BLK, :] == drow[:, first:]
            allowed = (kpos <= qpos) & same
            bias[:, starts[j] : starts[j] + width] = jnp.where(allowed, 0.0, masked_score)

    half = lane_half((BLK, 2 * HD))
    score_scale = HD ** (-0.5)
    scale = score_scale * log2_e
    pick_row = lax.broadcasted_iota(jnp.int32, (8, 2 * HD), 0)
    pick = jnp.where(lane_half((8, 2 * HD)) == pick_row, 1.0, 0.0)
    prod = do_ref[...].astype(f32) * att_ref[...].astype(f32)
    delta = lax.dot_general(
        pick, prod, (((1,), (1,)), ((), ())), precision=lax.Precision.HIGHEST, preferred_element_type=f32
    )
    for j in range(blocks):
        first = j * BLK
        span = slice(first, first + BLK)
        kj = k_ref[span, :]
        vj = v_ref[span, :]
        qq = q_ref[first:, :]
        dd = do_ref[first:, :]
        width = tokens - first
        zero = jnp.zeros_like(kj)
        dks = []
        dvs = []
        dss = []
        khs = []
        for h in range(2):
            kh = jnp.where(half == h, kj, zero)
            vh = jnp.where(half == h, vj, zero)
            t = dot_nt(kh, qq) * scale + bias[:, starts[j] : starts[j] + width]
            p = jnp.exp2(t - lse_ref[0, h : h + 1, first:])
            dp = dot_nt(vh, dd)
            ds = (p * (dp - delta[h : h + 1, first:])).astype(bf16)
            dvs.append(dot_nn(p.astype(bf16), dd))
            dks.append(dot_nn(ds, qq))
            dss.append(ds)
            khs.append(kh)
        dk = jnp.where(half == 0, dks[0], dks[1]) * score_scale
        dv = jnp.where(half == 0, dvs[0], dvs[1])
        held[pair + pairs, span, :] = dk.astype(bf16)
        held[pair + 2 * pairs, span, :] = dv.astype(bf16)
        dq = dot_tn(jnp.concatenate(dss, axis=0), jnp.concatenate(khs, axis=0))
        if j == 0:
            dq_acc[...] = dq
        else:
            dq_acc[first:, :] += dq
    held[pair] = (dq_acc[...] * score_scale).astype(bf16)

    @pl.when(pair == pairs - 1)
    def _():
        for cp in copies:
            cp.wait()
        total = None
        for i in range(blocks):
            span = slice(i * BLK, (i + 1) * BLK)
            row = jnp.concatenate([held[p, span, :] for p in range(held.shape[0])], axis=1)
            dqkv_ref[span, :] = row
            part_ref[span, :] = dot_nt(row, w[...]).astype(bf16)
            here = jnp.sum(row.astype(f32), axis=0, keepdims=True)
            total = here if total is None else total + here
        sum_ref[...] = total


def attention_backward(sidx, qkv, datt, att, lse, drow, dcol, pieces):
    tokens, cols = qkv.shape
    width = cols // 3
    pairs = width // (2 * HD)
    rows = pieces[0].shape[0]
    depth = 4 * rows
    col = lambda k: (lambda i, m: (0, k * pairs + i))
    pair_block = (tokens, 2 * HD)
    ins = [(qkv, pair_block, col(0)), (qkv, pair_block, col(1)), (qkv, pair_block, col(2))]
    ins += [(datt, pair_block, col(0)), (att, pair_block, col(0))]
    ins += [(lse, (1, 8, tokens), lambda i, m: (i, 0, 0))]
    ins += [(drow, drow.shape, whole(drow.shape)), (dcol, dcol.shape, whole(dcol.shape))]
    ins += [(p, None, None) for p in pieces]
    outs = [
        (sds((tokens, cols), bf16), (tokens, cols), whole((0, 0))),
        (sds((tokens, depth), bf16), (tokens, depth), whole((0, 0))),
        (sds((1, cols), f32), (1, cols), whole((0, 0))),
    ]
    blocks = tokens // BLK
    scratch = [
        pltpu.VMEM((BLK, block_start(blocks)), f32),
        pltpu.VMEM((depth, cols), bf16),
        pltpu.VMEM((3 * pairs, tokens, 2 * HD), bf16),
        pltpu.VMEM((tokens, 2 * HD), f32),
        pltpu.SemaphoreType.DMA((4,)),
    ]
    return call(
        attn_back_body,
        "attention_backward",
        sidx,
        (pairs,),
        ins,
        outs,
        scratch,
        10 * tokens * tokens * width,
        48,
        exps=tokens * tokens * pairs,
    )


def weight_grad_body(parts, m, a_ref, b_ref, *refs):
    outs, turned = refs[:-1], refs[-1]

    @pl.when(pl.program_id(0) == 0)
    def _():
        turned[...] = jnp.transpose(a_ref[...])

    for out, (pick, rows) in zip(outs, parts):
        if rows == turned.shape[0]:
            left = turned[...]
        else:
            left = turned[pl.ds(pl.multiple_of(pick(m) * rows, 16), rows), :]
        out[...] = dot_nn(left, b_ref[...]).astype(bf16)


def weight_grad(name, sidx, a, a_width, a_pick, b, parts, tile):
    tokens, cols = b.shape
    ins = [(a, (tokens, a_width), lambda i, m: (0, a_pick(m))), (b, (tokens, tile), lambda i, m: (0, i))]
    outs = [(sds((rows, cols), bf16), (rows, tile), lambda i, m: (0, i)) for _, rows in parts]
    return call(
        functools.partial(weight_grad_body, parts),
        name,
        sidx,
        (cols // tile,),
        ins,
        outs,
        [pltpu.VMEM((a_width, tokens), bf16)],
        2 * tokens * cols * sum(rows for _, rows in parts),
        24,
    )


def input_back_body(m, gm_ref, x_ref, p_ref, r_ref, vec, out_ref, sum_gain, sum_shift):
    tile = pl.program_id(0)
    grad = p_ref[...].astype(f32) + r_ref[...].astype(f32)
    part, unit = norm_back(x_ref[0].astype(f32), grad, row_of(vec, GAIN_A))
    add_rows(sum_gain, grad * unit, tile == 0)
    add_rows(sum_shift, grad, tile == 0)

    @pl.when(tile == m[0])
    def _():
        out_ref[...] = gm_ref[...] + part


def input_backward(sidx, gm, x, part, recv, vec):
    tokens, depth = gm.shape
    tile = (BLK, depth)
    ins = [(gm, tile, row_tile), (x, (1, BLK, depth), stack_tile)]
    ins += [(a, tile, row_tile) for a in (part, recv)]
    ins.append((vec, vec.shape, whole(vec.shape)))
    outs = [(sds((BLK, depth), f32), tile, whole((0, 0)))]
    outs += [(sds((1, depth), f32), (1, depth), whole((0, 0)))] * 2
    return call(input_back_body, "input_backward", sidx, (tokens // BLK,), ins, outs, [], tokens * depth, 16)


def swap(a, perm):
    return lax.ppermute(a, "seq", perm)


def core_columns(w, parts, core):
    rows, cols = w.shape
    cut = w.reshape(rows, parts, 2, 2, cols // (4 * parts))
    one = cut[:, :, :, 0].reshape(rows, cols // 2)
    two = cut[:, :, :, 1].reshape(rows, cols // 2)
    return jnp.where(core == 0, one, two), jnp.where(core == 0, two, one)


def column_pieces(w, parts, core):
    keep, send = core_columns(w, parts, core)
    return [keep, swap(send, SWAP_CORE), swap(keep, SWAP_X), swap(send, SWAP_BOTH)]


def row_pieces(w):
    return [w, swap(w, SWAP_X)]


def gather_rows(a):
    near = swap(a, SWAP_CORE)
    far = swap(a, SWAP_X)
    return jnp.stack([a, near, far, swap(far, SWAP_CORE)])


def interleave(keep, recv, core):
    rows, cols = keep.shape
    q = cols // 2
    keep = keep.reshape(rows, 2, 1, q)
    recv = recv.reshape(rows, 2, 1, q)
    both = jnp.where(
        core == 0, jnp.concatenate([keep, recv], axis=2), jnp.concatenate([recv, keep], axis=2)
    )
    return both.reshape(rows, 2 * cols)


def interleave3(keep, recv, core):
    rows, cols = keep.shape
    q = cols // 6
    keep = keep.reshape(rows, 3, 2, 1, q)
    recv = recv.reshape(rows, 3, 2, 1, q)
    both = jnp.where(
        core == 0, jnp.concatenate([keep, recv], axis=3), jnp.concatenate([recv, keep], axis=3)
    )
    return both.reshape(rows, 2 * cols)


def vectors(norm_gain, norm_bias, qv_bias, out_bias, fc_bias, s, core):
    layers, _, q = norm_gain.shape
    mine = jnp.concatenate(
        [norm_gain, norm_bias, qv_bias, out_bias, fc_bias.reshape(layers, -1, q)], axis=1
    )
    got = jnp.stack([mine, swap(mine, SWAP_CORE), swap(mine, SWAP_X), swap(mine, SWAP_BOTH)])
    full = jnp.stack([lax.dynamic_index_in_dim(got, j ^ s, 0, keepdims=False) for j in range(4)])
    full = full.astype(f32)
    wide = jnp.concatenate([full[:, :, 0:4], full[:, :, 6:8]], axis=2)
    wide = wide.transpose(1, 2, 0, 3).reshape(layers, 6, 4 * q)
    wide = jnp.pad(wide, ((0, 0), (0, 2), (0, 0)))
    here = lax.dynamic_index_in_dim(full.reshape(2, 2, layers, -1, q), core, 1, keepdims=False)
    qv = here[:, :, 4:6].transpose(1, 2, 0, 3).reshape(layers, 2, 2 * q)
    qkv_bias = jnp.concatenate([qv[:, 0], jnp.zeros_like(qv[:, 0]), qv[:, 1]], axis=1)
    fcb = here[:, :, 8:].transpose(1, 0, 2, 3).reshape(layers, -1)
    return wide, qkv_bias, fcb


def on_device(
    block_input,
    output_cotangent,
    doc_ids,
    w_qkv,
    w_o,
    w_fc,
    w_proj,
    norm_gain,
    norm_bias,
    qv_bias,
    out_bias,
    fc_bias,
):
    s = lax.axis_index("seq").astype(jnp.int32)
    xi, core = s // 2, s % 2
    sidx = jnp.stack([s, xi, core])
    layers = w_qkv.shape[0]
    quarter = w_qkv.shape[1]
    tokens = doc_ids.shape[1]
    drow = doc_ids
    dcol = doc_ids.reshape(tokens, 1)
    xs = gather_rows(block_input[0])
    wide, qkv_bias, fcb = vectors(norm_gain, norm_bias, qv_bias, out_bias, fc_bias, s, core)
    wq, wo, wf, wp = [], [], [], []
    for l in range(layers):
        wq.append(column_pieces(w_qkv[l], 3, core))
        wo.append(row_pieces(w_o[l]))
        wf.append(column_pieces(w_fc[l], 1, core))
        wp.append(row_pieces(w_proj[l]))
    cot = gather_rows(output_cotangent[0])

    saved = []
    source = (xs,)
    for l in range(layers):
        vec = wide[l]
        outs = qkv_forward(
            sidx, source, vec, wide[l - 1] if l else None, qkv_bias[l : l + 1], wq[l]
        )
        x = xs if l == 0 else outs[0]
        ln_a, qkv = outs[-2:]
        att, lse, part = attention_forward(sidx, qkv, drow, dcol, wo[l])
        recv = swap(part, SWAP_CORE)
        mid, ln_c, act, slope, part = mlp_forward(
            sidx, x, part, recv, vec, fcb[l : l + 1], wf[l], wp[l]
        )
        recv = swap(part, SWAP_CORE)
        source = (mid, part, recv)
        saved.append((x, ln_a, qkv, att, lse, mid, ln_c, act, slope))
    mid, part, recv = source
    first = s * block_input.shape[1]
    own = lambda a: lax.dynamic_slice_in_dim(a, first, block_input.shape[1])
    result = own(mid) + branch_scale * (
        own(part).astype(f32) + own(recv).astype(f32) + wide[layers - 1][OUT_M]
    )

    quarter_of = lambda a: lax.dynamic_slice_in_dim(a[0], s * quarter, quarter)
    x_pick = lambda m: m[1]
    zero_pick = lambda m: 0
    core_pick = lambda m: m[2]
    other_pick = lambda m: 1 - m[2]
    grads = [None] * layers
    norm_a = [None] * layers
    back = (cot,)
    g = cot
    for l in reversed(range(layers)):
        x, ln_a, qkv, att, lse, mid, ln_c, act, slope = saved[l]
        outs = mlp_backward(sidx, back, slope, wf[l], wp[l])
        if len(back) > 1:
            g, dmlp, dpre, part, sum_mlp, sum_pre, gain_a, shift_a = outs
            norm_a[l + 1] = (gain_a, shift_a)
        else:
            dmlp, dpre, part, sum_mlp, sum_pre = outs
        recv = swap(part, SWAP_CORE)
        (g_proj,) = weight_grad(
            "grad_proj", sidx, act, act.shape[1] // 2, x_pick, dmlp, [(zero_pick, act.shape[1] // 2)], 256
        )
        fc_keep, fc_send = weight_grad(
            "grad_fc", sidx, ln_c, 2 * quarter, x_pick, dpre, [(core_pick, quarter), (other_pick, quarter)], 512
        )
        fc_recv = swap(fc_send, SWAP_CORE)
        gm, dattn, datt, sum_attn, gain_c, shift_c = out_backward(
            sidx, g, mid, part, recv, wide[l], wo[l]
        )
        dqkv, part, sum_qkv = attention_backward(sidx, qkv, datt, att, lse, drow, dcol, wq[l])
        recv = swap(part, SWAP_CORE)
        (g_o,) = weight_grad("grad_o", sidx, att, att.shape[1], zero_pick, dattn, [(x_pick, quarter)], 256)
        q_keep, q_send = weight_grad(
            "grad_qkv", sidx, ln_a, 2 * quarter, x_pick, dqkv, [(core_pick, quarter), (other_pick, quarter)], 384
        )
        q_recv = swap(q_send, SWAP_CORE)
        back = (gm, x, part, recv, wide[l])
        own_q = lambda a, at: lax.dynamic_slice_in_dim(a[0], at + xi * quarter, quarter)
        hidden_q = sum_pre.shape[1] // 2
        grads[l] = [
            [g_proj, fc_keep, fc_recv, g_o, q_keep, q_recv],
            [
                own_q(sum_qkv, 0),
                own_q(sum_qkv, 4 * quarter),
                quarter_of(sum_attn),
                quarter_of(sum_mlp),
                lax.dynamic_slice_in_dim(sum_pre[0], xi * hidden_q, hidden_q),
                quarter_of(gain_c),
                quarter_of(shift_c),
            ],
        ]
    gm, x, part, recv, vec = back
    grad_input, gain_a, shift_a = input_backward(sidx, gm, x, part, recv, vec)
    norm_a[0] = (gain_a, shift_a)

    big = []
    small = []
    for l in reversed(range(layers)):
        summed = lax.psum(tuple(grads[l][0]), "rows")
        big.append(summed)
    big = big[::-1]
    for l in range(layers):
        qb, vb, ob, mb, fb, gain_c, shift_c = grads[l][1]
        small.append(
            jnp.concatenate(
                [quarter_of(norm_a[l][0]), gain_c, quarter_of(norm_a[l][1]), shift_c, qb, vb, ob, mb, fb]
            )
        )
    small = lax.psum(jnp.stack(small), "rows")
    out_proj = jnp.stack([big[l][0] for l in range(layers)]).astype(f32)
    out_fc = jnp.stack([interleave(big[l][1], big[l][2], core) for l in range(layers)]).astype(f32)
    out_o = jnp.stack([big[l][3] for l in range(layers)]).astype(f32)
    out_qkv = jnp.stack([interleave3(big[l][4], big[l][5], core) for l in range(layers)]).astype(f32)
    pair = lambda k: small[:, k * quarter : (k + 2) * quarter].reshape(layers, 2, quarter)
    return (
        result[None],
        grad_input[None],
        out_qkv,
        out_o,
        out_fc,
        out_proj,
        pair(0),
        pair(2),
        pair(4),
        pair(6),
        small[:, 8 * quarter :],
    )


def solution(mesh):
    in_specs = (
        P("rows", "seq", None),
        P("rows", "seq", None),
        P("rows", None),
        P(None, "seq", None),
        P(None, "seq", None),
        P(None, "seq", None),
        P(None, "seq", None),
        P(None, None, "seq"),
        P(None, None, "seq"),
        P(None, None, "seq"),
        P(None, None, "seq"),
        P(None, "seq"),
    )
    out_specs = (
        P("rows", "seq", None),
        P("rows", "seq", None),
        P(None, "seq", None),
        P(None, "seq", None),
        P(None, "seq", None),
        P(None, "seq", None),
        P(None, None, "seq"),
        P(None, None, "seq"),
        P(None, None, "seq"),
        P(None, None, "seq"),
        P(None, "seq"),
    )
    return jax.shard_map(
        on_device, mesh=mesh, in_specs=in_specs, out_specs=out_specs, check_vma=False
    )
```

time: 1470 us -> 735 us (0.50)
  waiting for transfers between devices: 702 us -> 312 us
  matrix products: 242 us -> 0 us
  Pallas kernels: 0 us -> 185 us
  blocking collectives: 179 us -> 39.9 us
  local copies, waits for them, and re-layouts: 184 us -> 120 us
  other arithmetic: 83.4 us -> 34.4 us
  loops' own time: 16.5 us -> 0 us
    dot_general x58 -> x0, matrix products: 218 us -> none  [the longest x10 41.7 us: matmul(): return jnp.dot(left, right, preferred_element_type=jnp.float32)]
    psum x1, waiting for transfers between devices: 408 us -> 202 us  [on_device(): summed = lax.psum(tuple(grads[l][0]), 'rows')]
    pallas_call x0 -> x21, Pallas kernels: none -> 185 us  [call(): pl.pallas_call(body, name=name, grid_spec=pltpu.PrefetchScalarGridSpec(nu...]
    reduce_scatter x8 -> x0, waiting for transfers between devices: 159 us -> none  [the longest x2 95 us: layer_backward(): lax.psum_scatter(grad_w_proj.astype(jnp.bfloat16), 'seq', scatter_dimensi...]
    all_gather x10 -> x0, blocking collectives: 111 us -> none  [the longest x2 39.5 us: fetch_params(): lax.all_gather(out_bias[layer_index], 'seq', axis=1, tiled=True)]
    ppermute x0 -> x37, waiting for transfers between devices: none -> 110 us  [swap(): return lax.ppermute(a, 'seq', perm)]
    unnamed x33 -> x1, waiting for transfers between devices: 105 us -> 0.02 us
    another operation x38 -> x5, other arithmetic: 41.9 us -> 3.87 us  [the longest x2 2.99 us: gather_rows(): return jnp.stack([a, near, far, swap(far, SWAP_CORE)])]
  transfers between devices with their start and end apart: 34 -> 38, of which waited for: 15 -> 13; matrix products, arithmetic and copies ran while one was open for 28% -> 10% of each run, Pallas kernels for 0% -> 12%
where the time goes in v1:
time: 735 us; the launch traced here: 728 us
  waiting for transfers between devices  312 us (42%)
  Pallas kernels  185 us (25%)
  local copies, waits for them, and re-layouts  120 us (16%)
  blocking collectives  39.9 us (5%)
  other arithmetic  34.4 us (5%)
  starting transfers between devices  21.1 us (3%)
  between operations  15.3 us (2%)
    psum x1, waiting for transfers between devices, on_device(): summed = lax.psum(tuple(grads[l][0]), 'rows')  202 us
    pallas_call x21, Pallas kernels, call(): pl.pallas_call(body, name=name, grid_spec=pltpu.PrefetchScalarGridSpec(nu...  185 us
    ppermute x37, waiting for transfers between devices, swap(): return lax.ppermute(a, 'seq', perm)  110 us
    unnamed x188, local copies, waits for them, and re-layouts  45.5 us
    psum x1, blocking collectives, on_device(): small = lax.psum(jnp.stack(small), 'rows')  39.9 us
    ppermute x37, starting transfers between devices, swap(): return lax.ppermute(a, 'seq', perm)  21.1 us
  transfers between devices with their start and end apart: 38, of which 13 were waited for; matrix products, arithmetic and copies ran while one was open for 10% of the time, Pallas kernels for 12%

profile of v1, /device:TPU:0, one launch (start us, length us, event | category | flops | bytes accessed | tf_op | source)
XLA Modules:
  0.0 728.0 jit_solution(13598684891630920626)
XLA Ops:
  35.0 15.4 %collective-permute-done.7.refs_5_.w2 = bf16[192,1152]{1,0:T(8,128)(2,1)S(1)} collective-permute-done((bf16[192,1152]{1,0:T(8,128)(2,1)S(1)}, bf16[192,1152]{1,0:T(8,128)(2,1)S(1)}, u32[]{:S(2)}, u32[]{:S(2)}) %collective-permute-start.7) | collective-permute-done | bytes 442400 | tf_op jit(solution)/shard_map/ppermute | solution.py:682
  50.5 6.0 norm_qkv.2
  57.8 14.1 %attention_forward.2 = (bf16[1024,384]{1,0:T(8,128)(2,1)S(1)}, f32[3,8,1024]{2,1,0:T(8,128)S(1)}, bf16[1024,768]{1,0:T(8,128)(2,1)}) custom-call(s32[3]{0:T(128)S(1)} %pad_add_fusion.m, bf16[1024,1152]{1,0:T(8,128)(2,1)S(1)} %get-tuple-element.74.q_ref.k_ref.v_ref, bf16[1024,1152]{1,0:T(8,128)(2,1)S(1)} %get-tuple-element.74.q_ref.k_ref.v_ref, ...), custom_call_target="tpu_custom_call" | custom-call | flops 1610612736 | bytes 10133504 | tf_op jit(solution)/shard_map/attention_forward/pallas_call | solution.py:48
  84.9 13.7 %collective-permute-done.12.f2.refs_8_ = bf16[192,1536]{1,0:T(8,128)(2,1)} collective-permute-done((bf16[192,1536]{1,0:T(8,128)(2,1)}, bf16[192,1536]{1,0:T(8,128)(2,1)}, u32[]{:S(2)}, u32[]{:S(2)}) %collective-permute-start.12) | collective-permute-done | bytes 589856 | tf_op jit(solution)/shard_map/ppermute | solution.py:682
  98.5 10.8 %collective-permute-done.13.f3.refs_9_ = bf16[192,1536]{1,0:T(8,128)(2,1)} collective-permute-done((bf16[192,1536]{1,0:T(8,128)(2,1)}, bf16[192,1536]{1,0:T(8,128)(2,1)}, u32[]{:S(2)}, u32[]{:S(2)}) %collective-permute-start.13) | collective-permute-done | bytes 589856 | tf_op jit(solution)/shard_map/ppermute | solution.py:682
  109.4 16.1 %mlp_forward.2 = (f32[1024,768]{1,0:T(8,128)S(1)}, bf16[1024,768]{1,0:T(8,128)(2,1)S(1)}, bf16[1024,1536]{1,0:T(8,128)(2,1)S(1)}, bf16[1024,1536]{1,0:T(8,128)(2,1)S(1)}, bf16[1024,768]{1,0:T(8,128)(2,1)}) custom-call(s32[3]{0:T(128)S(1)} %pad_add_fusion.m, bf16[4,256,768]{2,1,0:T(8,128)(2,1)S(1)} %copy-done.6, bf16[1024,768]{1,0:T(8,128)(2,1)} %get-tuple-element.75.p_ref, ...), custom_call_target="tpu_custom_call" | custom-call | flops 4831838208 | bytes 22050816 | tf_op jit(solution)/shard_map/mlp_forward/pallas_call | solution.py:48
  132.4 3.7 reshape_squeeze.10
  144.1 10.8 %collective-permute-done.17.refs_8_.w2 = bf16[192,1152]{1,0:T(8,128)(2,1)S(1)} collective-permute-done((bf16[192,1152]{1,0:T(8,128)(2,1)S(1)}, bf16[192,1152]{1,0:T(8,128)(2,1)S(1)}, u32[]{:S(2)}, u32[]{:S(2)}) %collective-permute-start.17) | collective-permute-done | bytes 442400 | tf_op jit(solution)/shard_map/ppermute | solution.py:682
  154.9 8.7 %collective-permute-done.18.refs_9_.w3 = bf16[192,1152]{1,0:T(8,128)(2,1)S(1)} collective-permute-done((bf16[192,1152]{1,0:T(8,128)(2,1)S(1)}, bf16[192,1152]{1,0:T(8,128)(2,1)S(1)}, u32[]{:S(2)}, u32[]{:S(2)}) %collective-permute-start.18) | collective-permute-done | bytes 442400 | tf_op jit(solution)/shard_map/ppermute | solution.py:682
  165.6 7.2 norm_qkv.3
  175.8 14.3 %attention_forward.3 = (bf16[1024,384]{1,0:T(8,128)(2,1)S(1)}, f32[3,8,1024]{2,1,0:T(8,128)S(1)}, bf16[1024,768]{1,0:T(8,128)(2,1)}) custom-call(s32[3]{0:T(128)S(1)} %pad_add_fusion.m, bf16[1024,1152]{1,0:T(8,128)(2,1)S(1)} %get-tuple-element.79.q_ref.k_ref.v_ref, bf16[1024,1152]{1,0:T(8,128)(2,1)S(1)} %get-tuple-element.79.q_ref.k_ref.v_ref, ...), custom_call_target="tpu_custom_call" | custom-call | flops 1610612736 | bytes 10133504 | tf_op jit(solution)/shard_map/attention_forward/pallas_call | solution.py:48
  192.8 4.0 reshape_squeeze.11
  196.8 3.7 fusion.6
  210.1 30.9 %collective-permute-done.22.f2.refs_4_ = bf16[192,1536]{1,0:T(8,128)(2,1)} collective-permute-done((bf16[192,1536]{1,0:T(8,128)(2,1)S(1)}, bf16[192,1536]{1,0:T(8,128)(2,1)}, u32[]{:S(2)}, u32[]{:S(2)}) %collective-permute-start.22) | collective-permute-done | bytes 589856 | tf_op jit(solution)/shard_map/ppermute | solution.py:682
  241.0 10.9 %collective-permute-done.23.f3.refs_5_ = bf16[192,1536]{1,0:T(8,128)(2,1)} collective-permute-done((bf16[192,1536]{1,0:T(8,128)(2,1)}, bf16[192,1536]{1,0:T(8,128)(2,1)}, u32[]{:S(2)}, u32[]{:S(2)}) %collective-permute-start.23) | collective-permute-done | bytes 589856 | tf_op jit(solution)/shard_map/ppermute | solution.py:682
  251.9 15.9 %mlp_forward.3 = (f32[1024,768]{1,0:T(8,128)S(1)}, bf16[1024,768]{1,0:T(8,128)(2,1)S(1)}, bf16[1024,1536]{1,0:T(8,128)(2,1)S(1)}, bf16[1024,1536]{1,0:T(8,128)(2,1)S(1)}, bf16[1024,768]{1,0:T(8,128)(2,1)}) custom-call(s32[3]{0:T(128)S(1)} %pad_add_fusion.m, f32[1024,768]{1,0:T(8,128)} %copy-done.60, bf16[1024,768]{1,0:T(8,128)(2,1)} %get-tuple-element.80.p_ref, ...), custom_call_target="tpu_custom_call" | custom-call | flops 4831838208 | bytes 23623680 | tf_op jit(solution)/shard_map/mlp_forward/pallas_call | solution.py:48
  270.7 11.8 %mlp_backward.2 = (bf16[1024,768]{1,0:T(8,128)(2,1)S(1)}, bf16[1024,1536]{1,0:T(8,128)(2,1)S(1)}, bf16[1024,768]{1,0:T(8,128)(2,1)S(1)}, f32[1,768]{1,0:T(1,128)S(1)}, f32[1,1536]{1,0:T(1,128)S(1)}) custom-call(s32[3]{0:T(128)S(1)} %pad_add_fusion.m, bf16[4,256,768]{2,1,0:T(8,128)(2,1)S(1)} %pad_maximum_fusion.1.refs_0_.g_ref, ...), custom_call_target="tpu_custom_call" | custom-call | flops 4831838208 | bytes 15737856 | tf_op jit(solution)/shard_map/mlp_backward/pallas_call | solution.py:48
  287.4 5.7 out_backward.2
  298.9 19.8 %attention_backward.2 = (bf16[1024,1152]{1,0:T(8,128)(2,1)}, bf16[1024,768]{1,0:T(8,128)(2,1)S(1)}, f32[1,1152]{1,0:T(1,128)S(1)}) custom-call(s32[3]{0:T(128)S(1)} %pad_add_fusion.m, bf16[1024,1152]{1,0:T(8,128)(2,1)} %copy-done.1, bf16[1024,1152]{1,0:T(8,128)(2,1)} %copy-done.1, bf16[1024,1152]{1,0:T(8,128)(2,1)} %copy-done.1, ...), custom_call_target="tpu_custom_call" | custom-call | flops 4026531840 | bytes 14463488 | tf_op jit(solution)/shard_map/attention_backward/pallas_call | solution.py:48
  325.5 15.1 %mlp_backward.3 = (f32[1024,768]{1,0:T(8,128)S(1)}, bf16[1024,768]{1,0:T(8,128)(2,1)S(1)}, bf16[1024,1536]{1,0:T(8,128)(2,1)S(1)}, bf16[1024,768]{1,0:T(8,128)(2...) custom-call(s32[3]{0:T(128)S(1)} %pad_add_fusion.m, ...), custom_call_target="tpu_custom_call" | custom-call | flops 4831838208 | bytes 26778624 | tf_op jit(solution)/shard_map/mlp_backward/pallas_call | solution.py:48
  341.1 3.6 grad_fc.3
  344.8 3.6 grad_qkv.3
  348.8 3.6 grad_fc.2
  352.7 5.8 out_backward.3
  361.4 19.8 %attention_backward.3 = (bf16[1024,1152]{1,0:T(8,128)(2,1)}, bf16[1024,768]{1,0:T(8,128)(2,1)S(1)}, f32[1,1152]{1,0:T(1,128)S(1)}) custom-call(s32[3]{0:T(128)S(1)} %pad_add_fusion.m, bf16[1024,1152]{1,0:T(8,128)(2,1)} %copy-done, bf16[1024,1152]{1,0:T(8,128)(2,1)} %copy-done, bf16[1024,1152]{1,0:T(8,128)(2,1)} %copy-done, ...), custom_call_target="tpu_custom_call" | custom-call | flops 4026531840 | bytes 14463488 | tf_op jit(solution)/shard_map/attention_backward/pallas_call | solution.py:48
  383.5 3.6 grad_qkv.2
  392.3 3.9 grad_proj.3
  412.4 3.9 grad_proj.2
  436.3 5.5 input_backward.1
  442.0 39.9 %psum.103 = f32[2,2304]{1,0:T(2,128)S(1)} all-reduce(f32[2,2304]{1,0:T(2,128)S(1)} %pad_maximum_fusion.3), channel_id=1, replica_groups=mesh['rows'=8,'seq'=4] {'rows'}, use_global_device_ids=true, to_apply=%region_12.13 | all-reduce | flops 4608 | bytes 36864 | tf_op jit(solution)/shard_map/psum | solution.py:871
  485.2 201.6 %all-reduce.4.cloned.1.call-done = (bf16[192,3,2,1,192]{4,2,1,0,3:T(2,128)(2,1)}, bf16[192,3,2,1,192]{4,2,1,0,3:T(2,128)(2,1)}, bf16[192,3,2,1,192]{4,2,1,0,3:T(...) async-done(((bf16[192,3,2,1,192]{4,2,1,0,3:T(2,128)(2,1)}, ...) | async-done | bytes 7077904 | tf_op jit(solution)/shard_map/psum | solution.py:861
  686.8 8.2 %broadcast_select_fusion.2 = (bf16[192,3,2,2,192]{4,2,1,0,3:T(2,128)(2,1)S(1)}, bf16[192,3,2,2,192]{4,2,1,0,3:T(2,128)(2,1)S(1)}) fusion(pred[]{:T(512)S(6)} %eq.4, bf16[192,3,2,1,192]{4,2,1,0,3:T(2,128)(2,1)} %get-tuple-element.137, bf16[192,3,2,1,192]{4,2,1,0,3:T(2,128)(2,1)} %get-tuple-element.138, bf16[192,3,2,1,192]{4,2,1,0,3:T(2,128)(2,1)} %get-tuple-element.140, ...), kind=kLoop, calls=%fused_computation.4 | loop fusion | flops 2654208 | bytes 3538945 | tf_op jit(solution)/shard_map/jit(_where)/select_n | solution.py:724
  (351 shorter events, 171.2 us)
Async XLA Ops:
  7.2 679.6 %all-reduce.4.cloned.1.call-start = ((), (), s32[]{:S(2)}) async-start(), calls=%async_computation | async-start | bytes 15335424 | tf_op jit(solution)/shard_map/psum | solution.py:861
  7.2 23.8 %collective-permute-start.1 = (bf16[256,768]{1,0:T(8,128)(2,1)}, bf16[256,768]{1,0:T(8,128)(2,1)}, u32[]{:S(2)}, u32[]{:S(2)}) collective-permute-start(bf16[256,768]{1,0:T(8,128)(2,1)} %bitcast.101), channel_id=1, source_target_pairs={{0,2},{1,3},{2,0},{3,1},{4,6},{5,7},{6,4},{7,5},{8,10},{9,11},{10,... | collective-permute-start | bytes 1179656 | tf_op jit(solution)/shard_map/ppermute | solution.py:682
  10.2 21.1 %collective-permute-start = (bf16[256,768]{1,0:T(8,128)(2,1)}, bf16[256,768]{1,0:T(8,128)(2,1)}, u32[]{:S(2)}, u32[]{:S(2)}) collective-permute-start(bf16[256,768]{1,0:T(8,128)(2,1)} %bitcast.102), channel_id=1, source_target_pairs={{0,1},{1,0},{2,3},{3,2},{4,5},{5,4},{6,7},{7,6},{8,9},{9,8},{10,11... | collective-permute-start | bytes 1179656 | tf_op jit(solution)/shard_map/ppermute | solution.py:682
  13.0 14.5 %collective-permute-start.5 = (bf16[2,12,192]{2,1,0:T(8,128)(2,1)}, bf16[2,12,192]{2,1,0:T(8,128)(2,1)}, u32[]{:S(2)}, u32[]{:S(2)}) collective-permute-start(bf16[2,12,192]{2,1,0:T(8,128)(2,1)} %concatenate.39), channel_id=1, source_target_pairs={{0,3},{1,2},{2,1},{3,0},{4,7},{5,6},{6,5},{7,4},{8,11},{9,10},{10,... | collective-permute-start | bytes 27656 | tf_op jit(solution)/shard_map/ppermute | solution.py:682
  13.2 14.9 %collective-permute-start.4 = (bf16[2,12,192]{2,1,0:T(8,128)(2,1)}, bf16[2,12,192]{2,1,0:T(8,128)(2,1)}, u32[]{:S(2)}, u32[]{:S(2)}) collective-permute-start(bf16[2,12,192]{2,1,0:T(8,128)(2,1)} %concatenate.39), channel_id=1, source_target_pairs={{0,2},{1,3},{2,0},{3,1},{4,6},{5,7},{6,4},{7,5},{8,10},{9,11},{10,... | collective-permute-start | bytes 27656 | tf_op jit(solution)/shard_map/ppermute | solution.py:682
  15.1 13.0 %collective-permute-start.3 = (bf16[2,12,192]{2,1,0:T(8,128)(2,1)}, bf16[2,12,192]{2,1,0:T(8,128)(2,1)}, u32[]{:S(2)}, u32[]{:S(2)}) collective-permute-start(bf16[2,12,192]{2,1,0:T(8,128)(2,1)} %concatenate.39), channel_id=1, source_target_pairs={{0,1},{1,0},{2,3},{3,2},{4,5},{5,4},{6,7},{7,6},{8,9},{9,8},{10,11... | collective-permute-start | bytes 27656 | tf_op jit(solution)/shard_map/ppermute | solution.py:682
  27.5 7.5 %collective-permute-start.6 = (bf16[192,1152]{1,0:T(8,128)(2,1)}, bf16[192,1152]{1,0:T(8,128)(2,1)S(1)}, u32[]{:S(2)}, u32[]{:S(2)}) collective-permute-start(bf16[192,1152]{1,0:T(8,128)(2,1)} %select_n.194), channel_id=1, source_target_pairs={{0,1},{1,0},{2,3},{3,2},{4,5},{5,4},{6,7},{7,6},{8,9},{9,8},{10,11... | collective-permute-start | bytes 1327112 | tf_op jit(solution)/shard_map/ppermute | solution.py:682
  28.1 22.4 %collective-permute-start.8 = (bf16[192,1152]{1,0:T(8,128)(2,1)}, bf16[192,1152]{1,0:T(8,128)(2,1)S(1)}, u32[]{:S(2)}, u32[]{:S(2)}) collective-permute-start(bf16[192,1152]{1,0:T(8,128)(2,1)} %select_n.194), channel_id=1, source_target_pairs={{0,3},{1,2},{2,1},{3,0},{4,7},{5,6},{6,5},{7,4},{8,11},{9,10},{10,... | collective-permute-start | bytes 1327112 | tf_op jit(solution)/shard_map/ppermute | solution.py:682
  28.1 22.4 %collective-permute-start.7 = (bf16[192,1152]{1,0:T(8,128)(2,1)S(1)}, bf16[192,1152]{1,0:T(8,128)(2,1)S(1)}, u32[]{:S(2)}, u32[]{:S(2)}) collective-permute-start(bf16[192,1152]{1,0:T(8,128)(2,1)S(1)} %select_n.192.refs_3_.w0), channel_id=1, source_target_pairs={{0,2},{1,3},{2,0},{3,1},{4,6},{5,7},{6,4},{7,5},{8,10},{9,11},{10,... | collective-permute-start | bytes 1327112 | tf_op jit(solution)/shard_map/ppermute | solution.py:682
  31.5 26.2 %collective-permute-start.9 = (bf16[192,768]{1,0:T(8,128)(2,1)S(1)}, bf16[192,768]{1,0:T(8,128)(2,1)S(1)}, u32[]{:S(2)}, u32[]{:S(2)}) collective-permute-start(bf16[192,768]{1,0:T(8,128)(2,1)S(1)} %get-tuple-element.172.wo0), channel_id=1, source_target_pairs={{0,2},{1,3},{2,0},{3,1},{4,6},{5,7},{6,4},{7,5},{8,10},{9,11},{10,... | collective-permute-start | bytes 884744 | tf_op jit(solution)/shard_map/ppermute | solution.py:682
  33.1 76.3 %collective-permute-start.14 = (bf16[768,768]{1,0:T(8,128)(2,1)}, bf16[768,768]{1,0:T(8,128)(2,1)}, u32[]{:S(2)}, u32[]{:S(2)}) collective-permute-start(bf16[768,768]{1,0:T(8,128)(2,1)} %get-tuple-element.150.j0.refs_10_), channel_id=1, source_target_pairs={{0,2},{1,3},{2,0},{3,1},{4,6},{5,7},{6,4},{7,5},{8,10},{9,11},{10,... | collective-permute-start | bytes 3538952 | tf_op jit(solution)/shard_map/ppermute | solution.py:682
  71.9 37.4 %collective-permute-start.10 = (bf16[1024,768]{1,0:T(8,128)(2,1)}, bf16[1024,768]{1,0:T(8,128)(2,1)}, u32[]{:S(2)}, u32[]{:S(2)}) collective-permute-start(bf16[1024,768]{1,0:T(8,128)(2,1)} %get-tuple-element.75.p_ref), channel_id=1, source_target_pairs={{0,1},{1,0},{2,3},{3,2},{4,5},{5,4},{6,7},{7,6},{8,9},{9,8},{10,11... | collective-permute-start | bytes 4718600 | tf_op jit(solution)/shard_map/ppermute | solution.py:682
  80.7 4.2 collective-permute-start.11
  82.0 16.5 %collective-permute-start.12 = (bf16[192,1536]{1,0:T(8,128)(2,1)}, bf16[192,1536]{1,0:T(8,128)(2,1)}, u32[]{:S(2)}, u32[]{:S(2)}) collective-permute-start(bf16[192,1536]{1,0:T(8,128)(2,1)} %bitcast.58.f0.refs_6_), channel_id=1, source_target_pairs={{0,2},{1,3},{2,0},{3,1},{4,6},{5,7},{6,4},{7,5},{8,10},{9,11},{10,... | collective-permute-start | bytes 1769480 | tf_op jit(solution)/shard_map/ppermute | solution.py:682
  82.3 27.1 %collective-permute-start.13 = (bf16[192,1536]{1,0:T(8,128)(2,1)}, bf16[192,1536]{1,0:T(8,128)(2,1)}, u32[]{:S(2)}, u32[]{:S(2)}) collective-permute-start(bf16[192,1536]{1,0:T(8,128)(2,1)} %bitcast.62), channel_id=1, source_target_pairs={{0,3},{1,2},{2,1},{3,0},{4,7},{5,6},{6,5},{7,4},{8,11},{9,10},{10,... | collective-permute-start | bytes 1769480 | tf_op jit(solution)/shard_map/ppermute | solution.py:682
  131.7 31.9 %collective-permute-start.15 = (bf16[1024,768]{1,0:T(8,128)(2,1)}, bf16[1024,768]{1,0:T(8,128)(2,1)}, u32[]{:S(2)}, u32[]{:S(2)}) collective-permute-start(bf16[1024,768]{1,0:T(8,128)(2,1)} %get-tuple-element.77.refs_1_), channel_id=1, source_target_pairs={{0,1},{1,0},{2,3},{3,2},{4,5},{5,4},{6,7},{7,6},{8,9},{9,8},{10,11... | collective-permute-start | bytes 4718600 | tf_op jit(solution)/shard_map/ppermute | solution.py:682
  141.9 13.0 %collective-permute-start.17 = (bf16[192,1152]{1,0:T(8,128)(2,1)S(1)}, bf16[192,1152]{1,0:T(8,128)(2,1)S(1)}, u32[]{:S(2)}, u32[]{:S(2)}) collective-permute-start(bf16[192,1152]{1,0:T(8,128)(2,1)S(1)} %select_n.201.refs_6_.w0), channel_id=1, source_target_pairs={{0,2},{1,3},{2,0},{3,1},{4,6},{5,7},{6,4},{7,5},{8,10},{9,11},{10,... | collective-permute-start | bytes 1327112 | tf_op jit(solution)/shard_map/ppermute | solution.py:682
  142.2 21.4 %collective-permute-start.18 = (bf16[192,1152]{1,0:T(8,128)(2,1)S(1)}, bf16[192,1152]{1,0:T(8,128)(2,1)S(1)}, u32[]{:S(2)}, u32[]{:S(2)}) collective-permute-start(bf16[192,1152]{1,0:T(8,128)(2,1)S(1)} %select_n.203), channel_id=1, source_target_pairs={{0,3},{1,2},{2,1},{3,0},{4,7},{5,6},{6,5},{7,4},{8,11},{9,10},{10,... | collective-permute-start | bytes 1327112 | tf_op jit(solution)/shard_map/ppermute | solution.py:682
  143.8 32.0 %collective-permute-start.19 = (bf16[192,768]{1,0:T(8,128)(2,1)S(1)}, bf16[192,768]{1,0:T(8,128)(2,1)S(1)}, u32[]{:S(2)}, u32[]{:S(2)}) collective-permute-start(bf16[192,768]{1,0:T(8,128)(2,1)S(1)} %get-tuple-element.171.wo0), channel_id=1, source_target_pairs={{0,2},{1,3},{2,0},{3,1},{4,6},{5,7},{6,4},{7,5},{8,10},{9,11},{10,... | collective-permute-start | bytes 884744 | tf_op jit(solution)/shard_map/ppermute | solution.py:682
  190.1 61.8 %collective-permute-start.20 = (bf16[1024,768]{1,0:T(8,128)(2,1)}, bf16[1024,768]{1,0:T(8,128)(2,1)}, u32[]{:S(2)}, u32[]{:S(2)}) collective-permute-start(bf16[1024,768]{1,0:T(8,128)(2,1)} %get-tuple-element.80.p_ref), channel_id=1, source_target_pairs={{0,1},{1,0},{2,3},{3,2},{4,5},{5,4},{6,7},{7,6},{8,9},{9,8},{10,11... | collective-permute-start | bytes 4718600 | tf_op jit(solution)/shard_map/ppermute | solution.py:682
  190.8 12.3 %collective-permute-start.27 = (bf16[256,768]{1,0:T(8,128)(2,1)}, bf16[256,768]{1,0:T(8,128)(2,1)}, u32[]{:S(2)}, u32[]{:S(2)}) collective-permute-start(bf16[256,768]{1,0:T(8,128)(2,1)} %bitcast.26), channel_id=1, source_target_pairs={{0,2},{1,3},{2,0},{3,1},{4,6},{5,7},{6,4},{7,5},{8,10},{9,11},{10,... | collective-permute-start | bytes 1179656 | tf_op jit(solution)/shard_map/ppermute | solution.py:682
  191.1 14.7 %collective-permute-start.26 = (bf16[256,768]{1,0:T(8,128)(2,1)}, bf16[256,768]{1,0:T(8,128)(2,1)}, u32[]{:S(2)}, u32[]{:S(2)}) collective-permute-start(bf16[256,768]{1,0:T(8,128)(2,1)} %bitcast.26), channel_id=1, source_target_pairs={{0,1},{1,0},{2,3},{3,2},{4,5},{5,4},{6,7},{7,6},{8,9},{9,8},{10,11... | collective-permute-start | bytes 1179656 | tf_op jit(solution)/shard_map/ppermute | solution.py:682
  191.1 60.8 %collective-permute-start.24 = (bf16[768,768]{1,0:T(8,128)(2,1)}, bf16[768,768]{1,0:T(8,128)(2,1)}, u32[]{:S(2)}, u32[]{:S(2)}) collective-permute-start(bf16[768,768]{1,0:T(8,128)(2,1)} %get-tuple-element.149.j0.refs_6_), channel_id=1, source_target_pairs={{0,2},{1,3},{2,0},{3,1},{4,6},{5,7},{6,4},{7,5},{8,10},{9,11},{10,... | collective-permute-start | bytes 3538952 | tf_op jit(solution)/shard_map/ppermute | solution.py:682
  205.2 5.0 collective-permute-start.21
  205.8 35.2 %collective-permute-start.22 = (bf16[192,1536]{1,0:T(8,128)(2,1)S(1)}, bf16[192,1536]{1,0:T(8,128)(2,1)}, u32[]{:S(2)}, u32[]{:S(2)}) collective-permute-start(bf16[192,1536]{1,0:T(8,128)(2,1)S(1)} %bitcast.92), channel_id=1, source_target_pairs={{0,2},{1,3},{2,0},{3,1},{4,6},{5,7},{6,4},{7,5},{8,10},{9,11},{10,... | collective-permute-start | bytes 1769480 | tf_op jit(solution)/shard_map/ppermute | solution.py:682
  206.1 45.8 %collective-permute-start.23 = (bf16[192,1536]{1,0:T(8,128)(2,1)}, bf16[192,1536]{1,0:T(8,128)(2,1)}, u32[]{:S(2)}, u32[]{:S(2)}) collective-permute-start(bf16[192,1536]{1,0:T(8,128)(2,1)} %bitcast.72), channel_id=1, source_target_pairs={{0,3},{1,2},{2,1},{3,0},{4,7},{5,6},{6,5},{7,4},{8,11},{9,10},{10,... | collective-permute-start | bytes 1769480 | tf_op jit(solution)/shard_map/ppermute | solution.py:682
  340.6 12.0 %collective-permute-start.31 = (bf16[1024,768]{1,0:T(8,128)(2,1)S(1)}, bf16[1024,768]{1,0:T(8,128)(2,1)S(1)}, u32[]{:S(2)}, u32[]{:S(2)}) collective-permute-start(bf16[1024,768]{1,0:T(8,128)(2,1)S(1)} %get-tuple-element.92.p_ref), channel_id=1, source_target_pairs={{0,1},{1,0},{2,3},{3,2},{4,5},{5,4},{6,7},{7,6},{8,9},{9,8},{10,11... | collective-permute-start | bytes 4718600 | tf_op jit(solution)/shard_map/ppermute | solution.py:682
  344.7 51.5 %collective-permute-start.36 = (bf16[192,1536]{1,0:T(8,128)(2,1)}, bf16[192,1536]{1,0:T(8,128)(2,1)}, u32[]{:S(2)}, u32[]{:S(2)}) collective-permute-start(bf16[192,1536]{1,0:T(8,128)(2,1)} %get-tuple-element.116), channel_id=1, source_target_pairs={{0,1},{1,0},{2,3},{3,2},{4,5},{5,4},{6,7},{7,6},{8,9},{9,8},{10,11... | collective-permute-start | bytes 1769480 | tf_op jit(solution)/shard_map/ppermute | solution.py:682
  348.5 57.1 %collective-permute-start.34 = (bf16[192,1152]{1,0:T(8,128)(2,1)}, bf16[192,1152]{1,0:T(8,128)(2,1)}, u32[]{:S(2)}, u32[]{:S(2)}) collective-permute-start(bf16[192,1152]{1,0:T(8,128)(2,1)} %get-tuple-element.106), channel_id=1, source_target_pairs={{0,1},{1,0},{2,3},{3,2},{4,5},{5,4},{6,7},{7,6},{8,9},{9,8},{10,11... | collective-permute-start | bytes 1327112 | tf_op jit(solution)/shard_map/ppermute | solution.py:682
  352.5 63.8 %collective-permute-start.35 = (bf16[192,1536]{1,0:T(8,128)(2,1)}, bf16[192,1536]{1,0:T(8,128)(2,1)}, u32[]{:S(2)}, u32[]{:S(2)}) collective-permute-start(bf16[192,1536]{1,0:T(8,128)(2,1)} %get-tuple-element.112), channel_id=1, source_target_pairs={{0,1},{1,0},{2,3},{3,2},{4,5},{5,4},{6,7},{7,6},{8,9},{9,8},{10,11... | collective-permute-start | bytes 1769480 | tf_op jit(solution)/shard_map/ppermute | solution.py:682
  387.9 37.4 %collective-permute-start.33 = (bf16[192,1152]{1,0:T(8,128)(2,1)}, bf16[192,1152]{1,0:T(8,128)(2,1)}, u32[]{:S(2)}, u32[]{:S(2)}) collective-permute-start(bf16[192,1152]{1,0:T(8,128)(2,1)} %get-tuple-element.102), channel_id=1, source_target_pairs={{0,1},{1,0},{2,3},{3,2},{4,5},{5,4},{6,7},{7,6},{8,9},{9,8},{10,11... | collective-permute-start | bytes 1327112 | tf_op jit(solution)/shard_map/ppermute | solution.py:682
  429.0 5.3 collective-permute-start.32
  (98 other events, 859.9 us)
Sparse Core Ops, SparseCore 0:
  427.7 258.9 all-reduce.3

commit v2 on v1

--- a/solution.py
+++ b/solution.py
@@ -65,6 +65,22 @@
     )(sidx, *arrays)
 
 
+RING = [0, 2, 4, 6, 7, 5, 3, 1]
+RING_NEXT = [(RING[i], RING[(i + 1) % 8]) for i in range(8)]
+RING_PREV = [(b, a) for a, b in RING_NEXT]
+RING_AT = [RING.index(r) for r in range(8)]
+RING_STEPS = [0, -1, 1, -2, 2, -3, 3, -4]
+
+
+def ring_place():
+    return jnp.asarray(RING_AT, jnp.int32)[lax.axis_index("rows")]
+
+
+def ring_index(s, xi, core):
+    place = ring_place() if lax.axis_size("rows") == 8 else jnp.int32(0)
+    return jnp.stack([s, xi, core, place])
+
+
 def sds(shape, dtype):
     return jax.ShapeDtypeStruct(shape, dtype)
 
@@ -88,6 +104,34 @@
         where = pl.multiple_of((first ^ j) * rows, 16)
         out.append(pltpu.make_async_copy(ref, dst.at[pl.ds(where, rows)], sems.at[j]))
     return out
+
+
+def mlp_copies(refs, wf, wp, sems, m):
+    if len(refs) == 6:
+        return (
+            piece_copies(refs[:4], wf, sems, m[0], refs[0].shape[0]),
+            piece_copies(refs[4:], wp, sems.at[pl.ds(4, 2)], m[1], refs[4].shape[0]),
+        )
+    keep, near, own = refs[:3]
+    far = refs[3:]
+    rows = keep.shape[0]
+    deep, wide = own.shape
+    first = piece_copies((keep, near), wf, sems, m[0], rows)
+    second = piece_copies((own,), wp, sems.at[pl.ds(2, 1)], m[1], deep)
+    n = len(far)
+    part = far[0].shape[0] // 2
+    k = 3
+    for ref, t in zip(far, RING_STEPS):
+        chunk = (m[3] + t + n) % n
+        at = pl.multiple_of((1 - m[1]) * 2 * rows + chunk * part, 16)
+        first.append(pltpu.make_async_copy(ref.at[pl.ds(0, part)], wf.at[pl.ds(at, part)], sems.at[k]))
+        k += 1
+        for side in range(2):
+            at = pl.multiple_of((1 - m[1]) * deep + side * (deep // 2) + chunk * part, 16)
+            src = ref.at[pl.ds(part, part), pl.ds(side * wide, wide)]
+            second.append(pltpu.make_async_copy(src, wp.at[pl.ds(at, part)], sems.at[k]))
+            k += 1
+    return first, second
 
 
 def normed(x):
@@ -275,9 +319,9 @@
     )
 
 
-def mlp_body(first, m, x_ref, p_ref, r_ref, vec, fcb, f0, f1, f2, f3, j0, j1, mid_ref, ln_ref, act_ref, slope_ref, part_ref, wf, wp, sems):
-    copies = piece_copies((f0, f1, f2, f3), wf, sems, m[0], f0.shape[0])
-    copies2 = piece_copies((j0, j1), wp, sems.at[pl.ds(4, 2)], m[1], j0.shape[0])
+def mlp_body(first, m, x_ref, p_ref, r_ref, vec, fcb, *refs):
+    mid_ref, ln_ref, act_ref, slope_ref, part_ref, wf, wp, sems = refs[-8:]
+    copies, copies2 = mlp_copies(refs[:-8], wf, wp, sems, m)
 
     @pl.when(pl.program_id(0) == 0)
     def _():
@@ -315,14 +359,14 @@
     part_ref[...] = dot_nn(act, wp[...]).astype(bf16)
 
 
-def mlp_forward(sidx, x, part, recv, vec, fcb, fc_pieces, proj_pieces):
+def mlp_forward(sidx, x, part, recv, vec, fcb, pieces):
     first = x.ndim == 3
     tokens, depth = part.shape
-    hidden = fc_pieces[0].shape[1]
+    hidden = fcb.shape[1]
     ins = [(x, (1, BLK, depth), stack_tile) if first else (x, (BLK, depth), row_tile)]
     ins += [(part, (BLK, depth), row_tile), (recv, (BLK, depth), row_tile)]
     ins += [(vec, vec.shape, whole(vec.shape)), (fcb, fcb.shape, whole(fcb.shape))]
-    ins += [(p, None, None) for p in fc_pieces + proj_pieces]
+    ins += [(p, None, None) for p in pieces]
     outs = [
         (sds((tokens, depth), f32), (BLK, depth), row_tile),
         (sds((tokens, depth), bf16), (BLK, depth), row_tile),
@@ -333,7 +377,7 @@
     scratch = [
         pltpu.VMEM((depth, hidden), bf16),
         pltpu.VMEM((hidden, depth), bf16),
-        pltpu.SemaphoreType.DMA((6,)),
+        pltpu.SemaphoreType.DMA((32,)),
     ]
     return call(
         functools.partial(mlp_body, first),
@@ -359,14 +403,15 @@
 
 def mlp_back_body(last, m, *refs):
     if last:
-        g_ref, slope_ref, f0, f1, f2, f3, j0, j1 = refs[:8]
-        dmlp_ref, dpre_ref, part_ref, sum_mlp, sum_pre, wf, wp, sems = refs[8:]
+        g_ref, slope_ref = refs[:2]
+        dmlp_ref, dpre_ref, part_ref, sum_mlp, sum_pre, wf, wp, sems = refs[-8:]
+        weights = refs[2:-8]
     else:
-        gm_ref, x_ref, p_ref, r_ref, nvec, slope_ref, f0, f1, f2, f3, j0, j1 = refs[:12]
-        g_out, dmlp_ref, dpre_ref, part_ref, sum_mlp, sum_pre, sum_gain, sum_shift, wf, wp, sems = refs[12:]
+        gm_ref, x_ref, p_ref, r_ref, nvec, slope_ref = refs[:6]
+        g_out, dmlp_ref, dpre_ref, part_ref, sum_mlp, sum_pre, sum_gain, sum_shift, wf, wp, sems = refs[-11:]
+        weights = refs[6:-11]
     start = pl.program_id(0) == 0
-    copies = piece_copies((f0, f1, f2, f3), wf, sems, m[0], f0.shape[0])
-    copies2 = piece_copies((j0, j1), wp, sems.at[pl.ds(4, 2)], m[1], j0.shape[0])
+    copies, copies2 = mlp_copies(weights, wf, wp, sems, m)
 
     @pl.when(start)
     def _():
@@ -404,10 +449,10 @@
     part_ref[...] = dot_nt(dpre, wf[...]).astype(bf16)
 
 
-def mlp_backward(sidx, source, slope, fc_pieces, proj_pieces):
+def mlp_backward(sidx, source, slope, pieces):
     last = len(source) == 1
     tokens, hidden = slope.shape
-    depth = proj_pieces[0].shape[1]
+    depth = source[0].shape[-1]
     tile = (BLK, depth)
     ins = []
     outs = []
@@ -419,7 +464,7 @@
         ins.append((vec, vec.shape, whole(vec.shape)))
         outs.append((sds((tokens, depth), f32), tile, row_tile))
     ins.append((slope, (BLK, hidden), row_tile))
-    ins += [(p, None, None) for p in fc_pieces + proj_pieces]
+    ins += [(p, None, None) for p in pieces]
     outs += [
         (sds((tokens, depth), bf16), tile, row_tile),
         (sds((tokens, hidden), bf16), (BLK, hidden), row_tile),
@@ -432,7 +477,7 @@
     scratch = [
         pltpu.VMEM((depth, hidden), bf16),
         pltpu.VMEM((hidden, depth), bf16),
-        pltpu.SemaphoreType.DMA((6,)),
+        pltpu.SemaphoreType.DMA((32,)),
     ]
     return call(
         functools.partial(mlp_back_body, last),
@@ -682,21 +727,73 @@
     return lax.ppermute(a, "seq", perm)
 
 
-def core_columns(w, parts, core):
-    rows, cols = w.shape
-    cut = w.reshape(rows, parts, 2, 2, cols // (4 * parts))
-    one = cut[:, :, :, 0].reshape(rows, cols // 2)
-    two = cut[:, :, :, 1].reshape(rows, cols // 2)
-    return jnp.where(core == 0, one, two), jnp.where(core == 0, two, one)
-
-
-def column_pieces(w, parts, core):
-    keep, send = core_columns(w, parts, core)
+def split_body(m, qkv_ref, fc_ref, qkv_keep, qkv_send, fc_keep, fc_send):
+    core = m[2]
+    q = qkv_ref.shape[1]
+    pair = 2 * q
+    for p in range(3):
+        own, other = [], []
+        for xside in range(2):
+            col = (2 * p + xside) * pair
+            both = qkv_ref[0, :, col : col + pair]
+            own.append(jnp.where(core == 0, both[:, :q], both[:, q:]))
+            other.append(jnp.where(core == 0, both[:, q:], both[:, :q]))
+        qkv_keep[:, p * pair : (p + 1) * pair] = jnp.concatenate(own, axis=1)
+        qkv_send[:, p * pair : (p + 1) * pair] = jnp.concatenate(other, axis=1)
+    d = fc_ref.shape[2] // 4
+    for xside in range(2):
+        one = fc_ref[0, :, 2 * xside * d : (2 * xside + 1) * d]
+        two = fc_ref[0, :, (2 * xside + 1) * d : (2 * xside + 2) * d]
+        fc_keep[:, xside * d : (xside + 1) * d] = jnp.where(core == 0, one, two)
+        fc_send[:, xside * d : (xside + 1) * d] = jnp.where(core == 0, two, one)
+
+
+def split_columns(sidx, w_qkv, w_fc, l):
+    _, rows, cols = w_qkv.shape
+    hidden = w_fc.shape[2]
+    at = lambda i, m: (l, 0, 0)
+    ins = [(w_qkv, (1, rows, cols), at), (w_fc, (1, rows, hidden), at)]
+    outs = []
+    for width in (cols // 2, cols // 2, hidden // 2, hidden // 2):
+        outs.append((sds((rows, width), bf16), (rows, width), whole((0, 0))))
+    return call(split_body, "split_columns", sidx, (1,), ins, outs, [], rows * cols, 16)
+
+
+def column_pieces(keep, send):
     return [keep, swap(send, SWAP_CORE), swap(keep, SWAP_X), swap(send, SWAP_BOTH)]
 
 
 def row_pieces(w):
     return [w, swap(w, SWAP_X)]
+
+
+def mlp_pieces(keep, send, w_proj, core):
+    if lax.axis_size("rows") != 8:
+        return column_pieces(keep, send) + row_pieces(w_proj), None
+    n = 8
+    near = swap(send, SWAP_CORE)
+    place = ring_place()
+    rows = keep.shape[0]
+    part = 2 * rows // n
+    deep = w_proj.shape[0] // 2
+    at = (place % 4) * part
+    cut = lambda a, first: lax.dynamic_slice_in_dim(a, first, part)
+    top = jnp.where(place // 4 == core, cut(keep, at), cut(near, at))
+    low = jnp.concatenate([cut(w_proj, place * part), cut(w_proj, deep + place * part)], axis=1)
+    mine = swap(jnp.concatenate([top, low]), SWAP_X)
+    return [keep, near, w_proj], [mine]
+
+
+def ring_pass(held, t):
+    if held is None:
+        return []
+    on = lax.ppermute(held[max(0, len(held) - 2)], "rows", RING_NEXT)
+    if t == 4:
+        new = [on]
+    else:
+        new = [on, lax.ppermute(held[-1], "rows", RING_PREV)]
+    held += new
+    return new
 
 
 def gather_rows(a):
@@ -705,26 +802,169 @@
     return jnp.stack([a, near, far, swap(far, SWAP_CORE)])
 
 
-def interleave(keep, recv, core):
-    rows, cols = keep.shape
-    q = cols // 2
-    keep = keep.reshape(rows, 2, 1, q)
-    recv = recv.reshape(rows, 2, 1, q)
-    both = jnp.where(
-        core == 0, jnp.concatenate([keep, recv], axis=2), jnp.concatenate([recv, keep], axis=2)
-    )
-    return both.reshape(rows, 2 * cols)
-
-
-def interleave3(keep, recv, core):
-    rows, cols = keep.shape
-    q = cols // 6
-    keep = keep.reshape(rows, 3, 2, 1, q)
-    recv = recv.reshape(rows, 3, 2, 1, q)
-    both = jnp.where(
-        core == 0, jnp.concatenate([keep, recv], axis=3), jnp.concatenate([recv, keep], axis=3)
-    )
-    return both.reshape(rows, 2 * cols)
+def pack_mlp(g_proj, fc_keep, fc_recv):
+    d = g_proj.shape[1]
+    return jnp.concatenate(
+        [g_proj, fc_keep[:, :d], fc_keep[:, d:], fc_recv[:, :d], fc_recv[:, d:]], axis=0
+    )
+
+
+def pack_attn(g_o, q_keep, q_recv):
+    d = g_o.shape[1]
+    h = d // 2
+    both = jnp.concatenate([q_keep[:, d : d + h], q_recv[:, d : d + h]], axis=1)
+    return jnp.concatenate([g_o, q_keep[:, :d], q_recv[:, :d], both], axis=0)
+
+
+def ring_sum(packed):
+    n = lax.axis_size("rows")
+    if n != 8:
+        return [lax.psum(packed, "rows")]
+    place = ring_place()
+    rows, cols = packed.shape
+    step = rows // n
+    part = step // 2
+    half = cols // 2
+
+    def chunk(k, way, side):
+        first = jnp.mod(k, n) * step + way * part
+        return lax.dynamic_slice(packed, (first, side * half), (part, half))
+
+    rings = [(way, side) for side in range(2) for way in range(2)]
+    perms = (RING_NEXT, RING_PREV)
+    sign = (-1, 1)
+    held = [chunk(place, way, side) for way, side in rings]
+    for t in range(1, n):
+        for i, (way, side) in enumerate(rings):
+            got = lax.ppermute(held[i], "rows", perms[way])
+            mine = chunk(place + sign[way] * t, way, side)
+            held[i] = (got.astype(f32) + mine.astype(f32)).astype(bf16)
+    pieces = [[h] for h in held]
+    for t in range(1, n):
+        for i, (way, side) in enumerate(rings):
+            pieces[i].append(lax.ppermute(pieces[i][-1], "rows", perms[way]))
+    return [p for ring in pieces for p in ring]
+
+
+def double_sum(a):
+    n = lax.axis_size("rows")
+    if n & (n - 1):
+        return lax.psum(a, "rows")
+    step = 1
+    while step < n:
+        a = a + lax.ppermute(a, "rows", [(r, r ^ step) for r in range(n)])
+        step *= 2
+    return a
+
+
+def write_mlp(full, first, core, q, out_fc, out_proj):
+    d = 4 * q
+    out_proj[0] = full[first : first + d, :].astype(f32)
+    block = lambda i: full[first + d + i * q : first + d + (i + 1) * q, :].astype(f32)
+    for xside in range(2):
+        for c in range(2):
+            col = (2 * xside + c) * d
+            out_fc[0, :, col : col + d] = jnp.where(core == c, block(xside), block(2 + xside))
+
+
+def write_attn(full, first, core, q, out_qkv, out_o, at):
+    d = 4 * q
+    h = d // 2
+    block = lambda i: full[first + i * q : first + (i + 1) * q, :].astype(f32)
+    out_o[at] = block(0)
+    keep_qk, recv_qk, both_v = block(1), block(2), block(3)
+    parts = [
+        (keep_qk[:, :h], recv_qk[:, :h]),
+        (keep_qk[:, h:], recv_qk[:, h:]),
+        (both_v[:, :h], both_v[:, h:]),
+    ]
+    for p, (keep, recv) in enumerate(parts):
+        for xside in range(2):
+            a = keep[:, xside * q : (xside + 1) * q]
+            b = recv[:, xside * q : (xside + 1) * q]
+            col = p * d + xside * h
+            out_qkv[at, :, col : col + h] = jnp.concatenate(
+                [jnp.where(core == 0, a, b), jnp.where(core == 0, b, a)], axis=1
+            )
+
+
+def finish_mlp_body(q, m, proj, keep, recv, out_fc, out_proj):
+    out_proj[0] = proj[...].astype(f32)
+    d = 4 * q
+    for xside in range(2):
+        a = keep[:, xside * d : (xside + 1) * d].astype(f32)
+        b = recv[:, xside * d : (xside + 1) * d].astype(f32)
+        for c in range(2):
+            col = (2 * xside + c) * d
+            out_fc[0, :, col : col + d] = jnp.where(m[2] == c, a, b)
+
+
+def finish_mlp(sidx, l, layers, sums, q):
+    d = 4 * q
+    size = sum(a.size for a in sums)
+    shapes = [(q, 4 * d), (d, d)]
+    return pl.pallas_call(
+        functools.partial(finish_mlp_body, q),
+        name="unpack_mlp",
+        grid_spec=pltpu.PrefetchScalarGridSpec(
+            num_scalar_prefetch=1,
+            grid=(1,),
+            in_specs=[pl.BlockSpec(a.shape, lambda i, m: (0, 0)) for a in sums],
+            out_specs=[pl.BlockSpec((1,) + sh, lambda i, m: (l, 0, 0)) for sh in shapes],
+        ),
+        out_shape=[sds((layers,) + sh, f32) for sh in shapes],
+        compiler_params=pltpu.CompilerParams(vmem_limit_bytes=48 * MIB),
+        cost_estimate=pl.CostEstimate(flops=size, bytes_accessed=6 * size, transcendentals=0),
+    )(sidx, *sums)
+
+
+def finish_body(count, layers, q, m, *refs):
+    pieces = refs[:count]
+    out_fc, out_proj, out_qkv, out_o, full = refs[-5:]
+    rows, d = full.shape
+    if count == 1:
+        full[...] = pieces[0][...].astype(f32)
+    else:
+        n = 8
+        step = rows // n
+        part = step // 2
+        half = d // 2
+        k = 0
+        for side in range(2):
+            for way in range(2):
+                for t in range(n):
+                    chunk = (m[3] + (1 - t if way == 0 else t - 1) + 2 * n) % n
+                    first = pl.multiple_of(chunk * step + way * part, 8)
+                    full[pl.ds(first, part), side * half : (side + 1) * half] = pieces[k][...].astype(f32)
+                    k += 1
+    write_mlp(full, 0, m[2], q, out_fc, out_proj)
+    for l in range(layers):
+        write_attn(full, 2 * d + l * d, m[2], q, out_qkv, out_o, l)
+
+
+def finish(sidx, layers, pieces, before, q):
+    count = len(pieces)
+    d = 4 * q
+    rows = 2 * d + layers * d
+    shapes = [(1, q, 4 * d), (1, d, d), (layers, q, 3 * d), (layers, q, d)]
+    in_specs = [pl.BlockSpec(p.shape, lambda i, m: (0, 0)) for p in pieces]
+    in_specs += [pl.BlockSpec(memory_space=pl.ANY)] * len(before)
+    aliases = {1 + count + k: k for k in range(len(before))}
+    return pl.pallas_call(
+        functools.partial(finish_body, count, layers, q),
+        name="unpack_grads",
+        grid_spec=pltpu.PrefetchScalarGridSpec(
+            num_scalar_prefetch=1,
+            grid=(1,),
+            in_specs=in_specs,
+            out_specs=[pl.BlockSpec(sh, lambda i, m: (0, 0, 0)) for sh in shapes],
+            scratch_shapes=[pltpu.VMEM((rows, d), f32)],
+        ),
+        out_shape=[sds((layers,) + sh[1:], f32) for sh in shapes],
+        input_output_aliases=aliases,
+        compiler_params=pltpu.CompilerParams(vmem_limit_bytes=56 * MIB),
+        cost_estimate=pl.CostEstimate(flops=rows * d, bytes_accessed=6 * rows * d, transcendentals=0),
+    )(sidx, *pieces, *before)
 
 
 def vectors(norm_gain, norm_bias, qv_bias, out_bias, fc_bias, s, core):
@@ -761,7 +1001,7 @@
 ):
     s = lax.axis_index("seq").astype(jnp.int32)
     xi, core = s // 2, s % 2
-    sidx = jnp.stack([s, xi, core])
+    sidx = ring_index(s, xi, core)
     layers = w_qkv.shape[0]
     quarter = w_qkv.shape[1]
     tokens = doc_ids.shape[1]
@@ -769,31 +1009,59 @@
     dcol = doc_ids.reshape(tokens, 1)
     xs = gather_rows(block_input[0])
     wide, qkv_bias, fcb = vectors(norm_gain, norm_bias, qv_bias, out_bias, fc_bias, s, core)
-    wq, wo, wf, wp = [], [], [], []
+    wq, wo, near, far = [], [], [], []
     for l in range(layers):
-        wq.append(column_pieces(w_qkv[l], 3, core))
+        keep, send, fc_keep, fc_send = split_columns(sidx, w_qkv, w_fc, l)
+        fixed, moved = mlp_pieces(fc_keep, fc_send, w_proj[l], core)
+        near.append(fixed)
+        far.append(moved)
+        wq.append(column_pieces(keep, send))
         wo.append(row_pieces(w_o[l]))
-        wf.append(column_pieces(w_fc[l], 1, core))
-        wp.append(row_pieces(w_proj[l]))
     cot = gather_rows(output_cotangent[0])
 
+    def pin(outs, *groups):
+        flat, tree = jax.tree.flatten((outs, groups))
+        outs, groups = jax.tree.unflatten(tree, lax.optimization_barrier(flat))
+        return (outs,) + tuple(groups)
+
+    ring_pass(far[0], 1)
+    ring_pass(far[0], 2)
+    xs, far[0] = pin(xs, far[0])
     saved = []
     source = (xs,)
     for l in range(layers):
         vec = wide[l]
+        more = l + 1 < layers
         outs = qkv_forward(
             sidx, source, vec, wide[l - 1] if l else None, qkv_bias[l : l + 1], wq[l]
         )
+        ring_pass(far[l], 3)
+        outs, far[l] = pin(outs, far[l])
+        if more:
+            outs, far[l + 1] = pin(outs, far[l + 1])
+        else:
+            outs, cot = pin(outs, cot)
         x = xs if l == 0 else outs[0]
         ln_a, qkv = outs[-2:]
         att, lse, part = attention_forward(sidx, qkv, drow, dcol, wo[l])
+        ring_pass(far[l], 4)
+        part, far[l] = pin(part, far[l])
+        if more:
+            ring_pass(far[l + 1], 1)
+            part, far[l + 1], wq[l + 1][2] = pin(part, far[l + 1], wq[l + 1][2])
         recv = swap(part, SWAP_CORE)
         mid, ln_c, act, slope, part = mlp_forward(
-            sidx, x, part, recv, vec, fcb[l : l + 1], wf[l], wp[l]
+            sidx, x, part, recv, vec, fcb[l : l + 1], near[l] + (far[l] or [])
         )
+        if more:
+            ring_pass(far[l + 1], 2)
+            part, far[l + 1], wq[l + 1][3], wo[l + 1][1] = pin(
+                part, far[l + 1], wq[l + 1][3], wo[l + 1][1]
+            )
         recv = swap(part, SWAP_CORE)
         source = (mid, part, recv)
         saved.append((x, ln_a, qkv, att, lse, mid, ln_c, act, slope))
+    wm = [a + (b or []) for a, b in zip(near, far)]
     mid, part, recv = source
     first = s * block_input.shape[1]
     own = lambda a: lax.dynamic_slice_in_dim(a, first, block_input.shape[1])
@@ -812,7 +1080,7 @@
     g = cot
     for l in reversed(range(layers)):
         x, ln_a, qkv, att, lse, mid, ln_c, act, slope = saved[l]
-        outs = mlp_backward(sidx, back, slope, wf[l], wp[l])
+        outs = mlp_backward(sidx, back, slope, wm[l])
         if len(back) > 1:
             g, dmlp, dpre, part, sum_mlp, sum_pre, gain_a, shift_a = outs
             norm_a[l + 1] = (gain_a, shift_a)
@@ -826,6 +1094,7 @@
             "grad_fc", sidx, ln_c, 2 * quarter, x_pick, dpre, [(core_pick, quarter), (other_pick, quarter)], 512
         )
         fc_recv = swap(fc_send, SWAP_CORE)
+        recv, g_proj, fc_keep, fc_recv = lax.optimization_barrier((recv, g_proj, fc_keep, fc_recv))
         gm, dattn, datt, sum_attn, gain_c, shift_c = out_backward(
             sidx, g, mid, part, recv, wide[l], wo[l]
         )
@@ -840,7 +1109,7 @@
         own_q = lambda a, at: lax.dynamic_slice_in_dim(a[0], at + xi * quarter, quarter)
         hidden_q = sum_pre.shape[1] // 2
         grads[l] = [
-            [g_proj, fc_keep, fc_recv, g_o, q_keep, q_recv],
+            ((g_proj, fc_keep, fc_recv), pack_attn(g_o, q_keep, q_recv)),
             [
                 own_q(sum_qkv, 0),
                 own_q(sum_qkv, 4 * quarter),
@@ -855,12 +1124,7 @@
     grad_input, gain_a, shift_a = input_backward(sidx, gm, x, part, recv, vec)
     norm_a[0] = (gain_a, shift_a)
 
-    big = []
     small = []
-    for l in reversed(range(layers)):
-        summed = lax.psum(tuple(grads[l][0]), "rows")
-        big.append(summed)
-    big = big[::-1]
     for l in range(layers):
         qb, vb, ob, mb, fb, gain_c, shift_c = grads[l][1]
         small.append(
@@ -868,11 +1132,10 @@
                 [quarter_of(norm_a[l][0]), gain_c, quarter_of(norm_a[l][1]), shift_c, qb, vb, ob, mb, fb]
             )
         )
-    small = lax.psum(jnp.stack(small), "rows")
-    out_proj = jnp.stack([big[l][0] for l in range(layers)]).astype(f32)
-    out_fc = jnp.stack([interleave(big[l][1], big[l][2], core) for l in range(layers)]).astype(f32)
-    out_o = jnp.stack([big[l][3] for l in range(layers)]).astype(f32)
-    out_qkv = jnp.stack([interleave3(big[l][4], big[l][5], core) for l in range(layers)]).astype(f32)
+    small = double_sum(jnp.stack(small))
+    before = finish_mlp(sidx, 1, layers, lax.psum(grads[1][0][0], "rows"), quarter)
+    packed = jnp.concatenate([pack_mlp(*grads[0][0][0])] + [grads[l][0][1] for l in range(layers)])
+    out_fc, out_proj, out_qkv, out_o = finish(sidx, layers, ring_sum(packed), before, quarter)
     pair = lambda k: small[:, k * quarter : (k + 2) * quarter].reshape(layers, 2, quarter)
     return (
         result[None],

time: 735 us -> 587 us (0.80)
  waiting for transfers between devices: 312 us -> 118 us
  starting transfers between devices: 21.1 us -> 95.8 us
  blocking collectives: 39.9 us -> 0 us
  Pallas kernels: 185 us -> 204 us
  local copies, waits for them, and re-layouts: 120 us -> 106 us
  between operations: 15.3 us -> 28.6 us
  other arithmetic: 34.4 us -> 24.4 us
    psum x1, waiting for transfers between devices: 202 us -> 0.01 us  [on_device(): lax.psum(grads[1][0][0], 'rows')]
    ppermute x0 -> x73, waiting for transfers between devices: none -> 87.3 us  [the longest x28 47.1 us: ring_sum(): got = lax.ppermute(held[i], 'rows', perms[way])]
    ppermute x37 -> x33, waiting for transfers between devices: 110 us -> 30.2 us  [swap(): return lax.ppermute(a, 'seq', perm)]
    ppermute x0 -> x73, starting transfers between devices: none -> 79.2 us  [the longest x28 31.9 us: ring_sum(): pieces[i].append(lax.ppermute(pieces[i][-1], 'rows', perms[way]))]
    psum x1 -> x0, blocking collectives: 39.9 us -> none  [on_device(): small = lax.psum(jnp.stack(small), 'rows')]
    unnamed x188 -> x301, local copies, waits for them, and re-layouts: 45.5 us -> 81.4 us
    reshape x8 -> x0, local copies, waits for them, and re-layouts: 19.5 us -> none  [the longest x2 5.77 us: interleave(): keep = keep.reshape(rows, 2, 1, q)]
    select_n x12 -> x0, local copies, waits for them, and re-layouts: 17.3 us -> none  [the longest x4 7.06 us: interleave3(): jnp.where(core == 0, jnp.concatenate([keep, recv], axis=3), jnp.concatena...]
  transfers between devices with their start and end apart: 38 -> 107, of which waited for: 13 -> 38; matrix products, arithmetic and copies ran while one was open for 10% -> 9% of each run, Pallas kernels for 12% -> 15%
where the time goes in v2:
time: 587 us; the launch traced here: 576 us
  Pallas kernels  204 us (35%)
  waiting for transfers between devices  118 us (20%)
  local copies, waits for them, and re-layouts  106 us (18%)
  starting transfers between devices  95.8 us (16%)
  between operations  28.6 us (5%)
  other arithmetic  24.4 us (4%)
    pallas_call x23, Pallas kernels, call(): pl.pallas_call(body, name=name, grid_spec=pltpu.PrefetchScalarGridSpec(nu...  193 us
    unnamed x301, local copies, waits for them, and re-layouts  81.4 us
    ppermute x28, waiting for transfers between devices, ring_sum(): got = lax.ppermute(held[i], 'rows', perms[way])  47.1 us
    ppermute x28, waiting for transfers between devices, ring_sum(): pieces[i].append(lax.ppermute(pieces[i][-1], 'rows', perms[way]))  35.1 us
    ppermute x28, starting transfers between devices, ring_sum(): pieces[i].append(lax.ppermute(pieces[i][-1], 'rows', perms[way]))  31.9 us
    ppermute x33, waiting for transfers between devices, swap(): return lax.ppermute(a, 'seq', perm)  30.2 us
    ppermute x28, starting transfers between devices, ring_sum(): got = lax.ppermute(held[i], 'rows', perms[way])  28.6 us
    ppermute x33, starting transfers between devices, swap(): return lax.ppermute(a, 'seq', perm)  16.6 us
  transfers between devices with their start and end apart: 107, of which 38 were waited for; matrix products, arithmetic and copies ran while one was open for 9% of the time, Pallas kernels for 15%

profile of v2, /device:TPU:0, one launch (start us, length us, event | category | flops | bytes accessed | tf_op | source)
XLA Modules:
  0.0 576.3 jit_solution(9902429899668193344)
XLA Ops:
  14.0 4.1 slice_bitcast_fusion.6
  41.0 8.8 %collective-permute-done.4.refs_3_.refs_9_ = bf16[96,1536]{1,0:T(8,128)(2,1)S(1)} collective-permute-done((bf16[96,1536]{1,0:T(8,128)(2,1)S(1)}, bf16[96,1536]{1,0:T(8,128)(2,1)S(1)}, u32[]{:S(2)}, u32[]{:S(2)}) %collective-permute-start.4) | collective-permute-done | bytes 294944 | tf_op jit(solution)/shard_map/ppermute | solution.py:727
  55.2 3.1 collective-permute-done.5.refs_4_.refs_10_
  71.0 4.9 collective-permute-done.13.refs_5_.w2
  83.2 5.9 %norm_qkv.2 = (bf16[1024,768]{1,0:T(8,128)(2,1)S(1)}, bf16[1024,1152]{1,0:T(8,128)(2,1)S(1)}) custom-call(s32[4]{0:T(128)S(1)} %pad_add_fusion.m, bf16[4,256,768]{2,1,0:T(8,128)(2,1)S(1)} %copy-done.7, f32[8,768]{1,0:T(8,128)S(1)} %get-tuple-element.357.refs_1_.vec.refs_3_, f32[1,1152]{1,0:T(1,128)S(1)} %get-tuple-element.365.refs_2_, ...), custom_call_target="tpu_custom_call" | custom-call | flops 1811939328 | bytes 7303680 | tf_op jit(solution)/shard_map/norm_qkv/pallas_call | solution.py:48
  94.1 14.1 %attention_forward.2 = (bf16[1024,384]{1,0:T(8,128)(2,1)S(1)}, f32[3,8,1024]{2,1,0:T(8,128)S(1)}, bf16[1024,768]{1,0:T(8,128)(2,1)}) custom-call(s32[4]{0:T(128)S(1)} %pad_add_fusion.m, bf16[1024,1152]{1,0:T(8,128)(2,1)S(1)} %get-tuple-element.175.q_ref.k_ref.v_ref, bf16[1024,1152]{1,0:T(8,128)(2,1)S(1)} %get-tuple-element.175.q_ref.k_ref.v_ref, ...), custom_call_target="tpu_custom_call" | custom-call | flops 1610612736 | bytes 10133504 | tf_op jit(solution)/shard_map/attention_forward/pallas_call | solution.py:48
  122.8 15.3 %mlp_forward.2 = (f32[1024,768]{1,0:T(8,128)S(1)}, bf16[1024,768]{1,0:T(8,128)(2,1)S(1)}, bf16[1024,1536]{1,0:T(8,128)(2,1)S(1)}, bf16[1024,1536]{1,0:T(8,128)(2,1)S(1)}, bf16[1024,768]{1,0:T(8,128)(2,1)S(1)}) custom-call(s32[4]{0:T(128)S(1)} %pad_add_fusion.m, bf16[4,256,768]{2,1,0:T(8,128)(2,1)S(1)} %copy-done.8, ...), custom_call_target="tpu_custom_call" | custom-call | flops 4831838208 | bytes 22050816 | tf_op jit(solution)/shard_map/mlp_forward/pallas_call | solution.py:48
  141.8 10.4 %collective-permute-done.34 = bf16[256,768]{1,0:T(8,128)(2,1)S(1)} collective-permute-done((bf16[256,768]{1,0:T(8,128)(2,1)S(1)}, bf16[256,768]{1,0:T(8,128)(2,1)S(1)}, u32[]{:S(2)}, u32[]{:S(2)}) %collective-permute-start.34) | collective-permute-done | bytes 393248 | tf_op jit(solution)/shard_map/ppermute | solution.py:727
  155.7 5.9 %norm_qkv.3 = (f32[1024,768]{1,0:T(8,128)S(1)}, bf16[1024,768]{1,0:T(8,128)(2,1)S(1)}, bf16[1024,1152]{1,0:T(8,128)(2,1)S(1)}) custom-call(s32[4]{0:T(128)S(1)} %pad_add_fusion.m, f32[1024,768]{1,0:T(8,128)S(1)} %get-tuple-element.196.refs_0_.mid_ref, bf16[1024,768]{1,0:T(8,128)(2,1)S(1)} %get-tuple-element.202.refs_1_, ...), custom_call_target="tpu_custom_call" | custom-call | flops 1811939328 | bytes 15192576 | tf_op jit(solution)/shard_map/norm_qkv/pallas_call | solution.py:48
  168.9 13.0 %attention_forward.3 = (bf16[1024,384]{1,0:T(8,128)(2,1)S(1)}, f32[3,8,1024]{2,1,0:T(8,128)S(1)}, bf16[1024,768]{1,0:T(8,128)(2,1)S(1)}) custom-call(s32[4]{0:T(128)S(1)} %pad_add_fusion.m, bf16[1024,1152]{1,0:T(8,128)(2,1)S(1)} %get-tuple-element.217.q_ref.k_ref.v_ref, bf16[1024,1152]{1,0:T(8,128)(2,1)S(1)} %get-tuple-element.217.q_ref.k_ref.v_ref, ...), custom_call_target="tpu_custom_call" | custom-call | flops 1610612736 | bytes 10133504 | tf_op jit(solution)/shard_map/attention_forward/pallas_call | solution.py:48
  196.4 16.0 %mlp_forward.3 = (f32[1024,768]{1,0:T(8,128)S(1)}, bf16[1024,768]{1,0:T(8,128)(2,1)S(1)}, bf16[1024,1536]{1,0:T(8,128)(2,1)S(1)}, bf16[1024,1536]{1,0:T(8,128)(2,1)S(1)}, bf16[1024,768]{1,0:T(8,128)(2,1)S(1)}) custom-call(s32[4]{0:T(128)S(1)} %pad_add_fusion.m, f32[1024,768]{1,0:T(8,128)} %copy-done.71, bf16[1024,768]{1,0:T(8,128)(2,1)S(1)} %copy-done.77, ...), custom_call_target="tpu_custom_call" | custom-call | flops 4831838208 | bytes 23623680 | tf_op jit(solution)/shard_map/mlp_forward/pallas_call | solution.py:48
  215.2 12.1 %mlp_backward.2 = (bf16[1024,768]{1,0:T(8,128)(2,1)S(1)}, bf16[1024,1536]{1,0:T(8,128)(2,1)S(1)}, bf16[1024,768]{1,0:T(8,128)(2,1)S(1)}, f32[1,768]{1,0:T(1,128)S(1)}, f32[1,1536]{1,0:T(1,128)S(1)}) custom-call(s32[4]{0:T(128)S(1)} %pad_add_fusion.m, bf16[4,256,768]{2,1,0:T(8,128)(2,1)S(1)} %copy-done.6, bf16[1024,1536]{1,0:T(8,128)(2,1)S(1)} %get-tuple-element.239.refs_1_, ...), custom_call_target="tpu_custom_call" | custom-call | flops 4831838208 | bytes 15737856 | tf_op jit(solution)/shard_map/mlp_backward/pallas_call | solution.py:48
  227.6 3.5 grad_fc.2
  231.5 3.9 grad_proj.2
  242.1 14.0 %out_backward.2 = (f32[1024,768]{1,0:T(8,128)S(1)}, bf16[1024,768]{1,0:T(8,128)(2,1)S(1)}, bf16[1024,384]{1,0:T(8,128)(2,1)S(1)}, f32[1,768]{1,0:T(1,128)S(1)}, ...) custom-call(s32[4]{0:T(128)S(1)} %pad_add_fusion.m, bf16[4,256,768]{2,1,0:T(8,128)(2,1)S(1)} %copy-done.6, ...), custom_call_target="tpu_custom_call" | custom-call | flops 603979776 | bytes 13992960 | tf_op jit(solution)/shard_map/out_backward/pallas_call | solution.py:48
  262.9 19.5 %attention_backward.2 = (bf16[1024,1152]{1,0:T(8,128)(2,1)}, bf16[1024,768]{1,0:T(8,128)(2,1)S(1)}, f32[1,1152]{1,0:T(1,128)S(1)}) custom-call(s32[4]{0:T(128)S(1)} %pad_add_fusion.m, bf16[1024,1152]{1,0:T(8,128)(2,1)} %copy-done.1, bf16[1024,1152]{1,0:T(8,128)(2,1)} %copy-done.1, bf16[1024,1152]{1,0:T(8,128)(2,1)} %copy-done.1, ...), custom_call_target="tpu_custom_call" | custom-call | flops 4026531840 | bytes 14463488 | tf_op jit(solution)/shard_map/attention_backward/pallas_call | solution.py:48
  287.4 16.5 %mlp_backward.3 = (f32[1024,768]{1,0:T(8,128)S(1)}, bf16[1024,768]{1,0:T(8,128)(2,1)S(1)}, bf16[1024,1536]{1,0:T(8,128)(2,1)S(1)}, bf16[1024,768]{1,0:T(8,128)(2...) custom-call(s32[4]{0:T(128)S(1)} %pad_add_fusion.m, ...), custom_call_target="tpu_custom_call" | custom-call | flops 4831838208 | bytes 26778624 | tf_op jit(solution)/shard_map/mlp_backward/pallas_call | solution.py:48
  304.2 3.7 grad_fc.3
  309.1 3.8 grad_qkv.3
  324.8 7.1 %out_backward.3 = (f32[1024,768]{1,0:T(8,128)S(1)}, bf16[1024,768]{1,0:T(8,128)(2,1)S(1)}, bf16[1024,384]{1,0:T(8,128)(2,1)S(1)}, f32[1,768]{1,0:T(1,128)S(1)}, ...) custom-call(s32[4]{0:T(128)S(1)} %pad_add_fusion.m, f32[1024,768]{1,0:T(8,128)S(1)} %copy-done.17, f32[1024,768]{1,0:T(8,128)S(1)} %copy-done.3, ...), custom_call_target="tpu_custom_call" | custom-call | flops 603979776 | bytes 15565824 | tf_op jit(solution)/shard_map/out_backward/pallas_call | solution.py:48
  333.7 20.0 %attention_backward.3 = (bf16[1024,1152]{1,0:T(8,128)(2,1)}, bf16[1024,768]{1,0:T(8,128)(2,1)}, f32[1,1152]{1,0:T(1,128)S(1)}) custom-call(s32[4]{0:T(128)S(1)} %pad_add_fusion.m, bf16[1024,1152]{1,0:T(8,128)(2,1)} %copy-done, bf16[1024,1152]{1,0:T(8,128)(2,1)} %copy-done, bf16[1024,1152]{1,0:T(8,128)(2,1)} %copy-done, ...), custom_call_target="tpu_custom_call" | custom-call | flops 4026531840 | bytes 14463488 | tf_op jit(solution)/shard_map/attention_backward/pallas_call | solution.py:48
  401.6 9.1 %collective-permute-done.91 = bf16[192,384]{1,0:T(8,128)(2,1)S(1)} collective-permute-done((bf16[192,384]{1,0:T(8,128)(2,1)S(1)}, bf16[192,384]{1,0:T(8,128)(2,1)S(1)}, u32[]{:S(2)}, u32[]{:S(2)}) %collective-permute-start.91) | collective-permute-done | bytes 147488 | tf_op jit(solution)/shard_map/ppermute | solution.py:839
  410.7 8.2 %collective-permute-done.63 = bf16[192,384]{1,0:T(8,128)(2,1)S(1)} collective-permute-done((bf16[192,384]{1,0:T(8,128)(2,1)S(1)}, bf16[192,384]{1,0:T(8,128)(2,1)S(1)}, u32[]{:S(2)}, u32[]{:S(2)}) %collective-permute-start.63) | collective-permute-done | bytes 147488 | tf_op jit(solution)/shard_map/ppermute | solution.py:839
  426.0 7.2 %collective-permute-done.92 = bf16[192,384]{1,0:T(8,128)(2,1)S(1)} collective-permute-done((bf16[192,384]{1,0:T(8,128)(2,1)}, bf16[192,384]{1,0:T(8,128)(2,1)S(1)}, u32[]{:S(2)}, u32[]{:S(2)}) %collective-permute-start.92) | collective-permute-done | bytes 147488 | tf_op jit(solution)/shard_map/ppermute | solution.py:839
  456.5 5.6 input_backward.1
  473.6 3.7 collective-permute-done.67
  493.1 3.1 collective-permute-done.55.refs_2_
  498.7 4.4 collective-permute-done.69.refs_10_
  506.2 6.9 %collective-permute-done.97.refs_26_ = bf16[192,384]{1,0:T(8,128)(2,1)S(1)} collective-permute-done((bf16[192,384]{1,0:T(8,128)(2,1)S(1)}, bf16[192,384]{1,0:T(8,128)(2,1)S(1)}, u32[]{:S(2)}, u32[]{:S(2)}) %collective-permute-start.97) | collective-permute-done | bytes 147488 | tf_op jit(solution)/shard_map/ppermute | solution.py:845
  515.2 7.4 %collective-permute-done.70.refs_11_ = bf16[192,384]{1,0:T(8,128)(2,1)S(1)} collective-permute-done((bf16[192,384]{1,0:T(8,128)(2,1)S(1)}, bf16[192,384]{1,0:T(8,128)(2,1)S(1)}, u32[]{:S(2)}, u32[]{:S(2)}) %collective-permute-start.70) | collective-permute-done | bytes 147488 | tf_op jit(solution)/shard_map/ppermute | solution.py:845
  524.6 5.3 collective-permute-done.98.refs_27_
  560.8 8.2 %unpack_grads.1 = (f32[2,192,3072]{2,1,0:T(8,128)}, f32[2,768,768]{2,1,0:T(8,128)}, f32[2,192,2304]{2,1,0:T(8,128)}, f32[2,192,768]{2,1,0:T(8,128)}) custom-call(s32[4]{0:T(128)} %copy-done.55, bf16[192,384]{1,0:T(8,128)(2,1)} %copy-done.120, bf16[192,384]{1,0:T(8,128)(2,1)} %copy-done.123, ...), custom_call_target="tpu_custom_call", output_to_operand_aliasing={{0}: (33, {}), {1}: (34, {})} | custom-call | flops 2359296 | bytes 14155776 | tf_op jit(solution)/shard_map/unpack_grads/pallas_call | solution.py:953
  (589 shorter events, 272.8 us)
Async XLA Ops:
  7.2 538.1 %all-reduce.4.cloned.1.call-start = ((), (), s32[]{:S(2)}) async-start(), calls=%async_computation | async-start | bytes 4718592 | tf_op jit(solution)/shard_map/psum | solution.py:1136
  7.2 33.5 %collective-permute-start.1 = (bf16[256,768]{1,0:T(8,128)(2,1)}, bf16[256,768]{1,0:T(8,128)(2,1)}, u32[]{:S(2)}, u32[]{:S(2)}) collective-permute-start(bf16[256,768]{1,0:T(8,128)(2,1)} %bitcast.75), channel_id=1, source_target_pairs={{0,2},{1,3},{2,0},{3,1},{4,6},{5,7},{6,4},{7,5},{8,10},{9,11},{10,... | collective-permute-start | bytes 1179656 | tf_op jit(solution)/shard_map/ppermute | solution.py:727
  10.2 42.9 %collective-permute-start = (bf16[256,768]{1,0:T(8,128)(2,1)}, bf16[256,768]{1,0:T(8,128)(2,1)}, u32[]{:S(2)}, u32[]{:S(2)}) collective-permute-start(bf16[256,768]{1,0:T(8,128)(2,1)} %bitcast.76), channel_id=1, source_target_pairs={{0,1},{1,0},{2,3},{3,2},{4,5},{5,4},{6,7},{7,6},{8,9},{9,8},{10,11... | collective-permute-start | bytes 1179656 | tf_op jit(solution)/shard_map/ppermute | solution.py:727
  11.8 24.3 %collective-permute-start.11 = (bf16[2,12,192]{2,1,0:T(8,128)(2,1)S(1)}, bf16[2,12,192]{2,1,0:T(8,128)(2,1)S(1)}, u32[]{:S(2)}, u32[]{:S(2)}) collective-permute-start(bf16[2,12,192]{2,1,0:T(8,128)(2,1)S(1)} %concatenate.38), channel_id=1, source_target_pairs={{0,3},{1,2},{2,1},{3,0},{4,7},{5,6},{6,5},{7,4},{8,11},{9,10},{10,... | collective-permute-start | bytes 27656 | tf_op jit(solution)/shard_map/ppermute | solution.py:727
  12.0 24.6 %collective-permute-start.10 = (bf16[2,12,192]{2,1,0:T(8,128)(2,1)S(1)}, bf16[2,12,192]{2,1,0:T(8,128)(2,1)S(1)}, u32[]{:S(2)}, u32[]{:S(2)}) collective-permute-start(bf16[2,12,192]{2,1,0:T(8,128)(2,1)S(1)} %concatenate.38), channel_id=1, source_target_pairs={{0,2},{1,3},{2,0},{3,1},{4,6},{5,7},{6,4},{7,5},{8,10},{9,11},{10,... | collective-permute-start | bytes 27656 | tf_op jit(solution)/shard_map/ppermute | solution.py:727
  14.0 22.7 %collective-permute-start.9 = (bf16[2,12,192]{2,1,0:T(8,128)(2,1)S(1)}, bf16[2,12,192]{2,1,0:T(8,128)(2,1)S(1)}, u32[]{:S(2)}, u32[]{:S(2)}) collective-permute-start(bf16[2,12,192]{2,1,0:T(8,128)(2,1)S(1)} %concatenate.38), channel_id=1, source_target_pairs={{0,1},{1,0},{2,3},{3,2},{4,5},{5,4},{6,7},{7,6},{8,9},{9,8},{10,11... | collective-permute-start | bytes 27656 | tf_op jit(solution)/shard_map/ppermute | solution.py:727
  51.9 16.9 %collective-permute-start.12 = (bf16[192,1152]{1,0:T(8,128)(2,1)}, bf16[192,1152]{1,0:T(8,128)(2,1)S(1)}, u32[]{:S(2)}, u32[]{:S(2)}) collective-permute-start(bf16[192,1152]{1,0:T(8,128)(2,1)} %copy-done.91), channel_id=1, source_target_pairs={{0,1},{1,0},{2,3},{3,2},{4,5},{5,4},{6,7},{7,6},{8,9},{9,8},{10,11... | collective-permute-start | bytes 1327112 | tf_op jit(solution)/shard_map/ppermute | solution.py:727
  53.1 23.1 %collective-permute-start.14 = (bf16[192,1152]{1,0:T(8,128)(2,1)}, bf16[192,1152]{1,0:T(8,128)(2,1)S(1)}, u32[]{:S(2)}, u32[]{:S(2)}) collective-permute-start(bf16[192,1152]{1,0:T(8,128)(2,1)} %copy-done.91), channel_id=1, source_target_pairs={{0,3},{1,2},{2,1},{3,0},{4,7},{5,6},{6,5},{7,4},{8,11},{9,10},{10,... | collective-permute-start | bytes 1327112 | tf_op jit(solution)/shard_map/ppermute | solution.py:727
  53.4 22.5 %collective-permute-start.13 = (bf16[192,1152]{1,0:T(8,128)(2,1)S(1)}, bf16[192,1152]{1,0:T(8,128)(2,1)}, u32[]{:S(2)}, u32[]{:S(2)}) collective-permute-start(bf16[192,1152]{1,0:T(8,128)(2,1)S(1)} %get-tuple-element.162.refs_3_.w0), channel_id=1, source_target_pairs={{0,2},{1,3},{2,0},{3,1},{4,6},{5,7},{6,4},{7,5},{8,10},{9,11},{10,... | collective-permute-start | bytes 1327112 | tf_op jit(solution)/shard_map/ppermute | solution.py:727
  66.0 25.9 %collective-permute-start.18 = (bf16[96,1536]{1,0:T(8,128)(2,1)}, bf16[96,1536]{1,0:T(8,128)(2,1)}, u32[]{:S(2)}, u32[]{:S(2)}) collective-permute-start(bf16[96,1536]{1,0:T(8,128)(2,1)} %maximum_maximum_fusion.1), channel_id=1, source_target_pairs={{0,2},{1,3},{2,0},{3,1},{4,6},{5,7},{6,4},{7,5},{8,10},{9,11},{10,... | collective-permute-start | bytes 884744 | tf_op jit(solution)/shard_map/ppermute | solution.py:727
  67.3 22.9 %collective-permute-start.15 = (bf16[96,1536]{1,0:T(8,128)(2,1)}, bf16[96,1536]{1,0:T(8,128)(2,1)}, u32[]{:S(2)}, u32[]{:S(2)}) collective-permute-start(bf16[96,1536]{1,0:T(8,128)(2,1)} %collective-permute-done.7.refs_6_.refs_12_), channel_id=1, source_target_pairs={{0,8},{8,16},{16,24},{24,28},{28,20},{20,12},{12,4},{4,0},{1,9},{9... | collective-permute-start | bytes 884744 | tf_op jit(solution)/shard_map/ppermute | solution.py:790
  68.9 21.3 %collective-permute-start.16 = (bf16[96,1536]{1,0:T(8,128)(2,1)}, bf16[96,1536]{1,0:T(8,128)(2,1)}, u32[]{:S(2)}, u32[]{:S(2)}) collective-permute-start(bf16[96,1536]{1,0:T(8,128)(2,1)} %collective-permute-done.8.refs_7_.refs_13_), channel_id=1, source_target_pairs={{8,0},{16,8},{24,16},{28,24},{20,28},{12,20},{4,12},{0,4},{9,1},{1... | collective-permute-start | bytes 884744 | tf_op jit(solution)/shard_map/ppermute | solution.py:794
  75.9 18.2 %collective-permute-start.19 = (bf16[192,768]{1,0:T(8,128)(2,1)S(1)}, bf16[192,768]{1,0:T(8,128)(2,1)}, u32[]{:S(2)}, u32[]{:S(2)}) collective-permute-start(bf16[192,768]{1,0:T(8,128)(2,1)S(1)} %get-tuple-element.351.wo0), channel_id=1, source_target_pairs={{0,2},{1,3},{2,0},{3,1},{4,6},{5,7},{6,4},{7,5},{8,10},{9,11},{10,... | collective-permute-start | bytes 884744 | tf_op jit(solution)/shard_map/ppermute | solution.py:727
  76.9 32.8 %collective-permute-start.23 = (bf16[192,1152]{1,0:T(8,128)(2,1)}, bf16[192,1152]{1,0:T(8,128)(2,1)}, u32[]{:S(2)}, u32[]{:S(2)}) collective-permute-start(bf16[192,1152]{1,0:T(8,128)(2,1)} %get-tuple-element.186.refs_6_.w0), channel_id=1, source_target_pairs={{0,2},{1,3},{2,0},{3,1},{4,6},{5,7},{6,4},{7,5},{8,10},{9,11},{10,... | collective-permute-start | bytes 1327112 | tf_op jit(solution)/shard_map/ppermute | solution.py:727
  90.2 19.5 %collective-permute-start.20 = (bf16[96,1536]{1,0:T(8,128)(2,1)}, bf16[96,1536]{1,0:T(8,128)(2,1)}, u32[]{:S(2)}, u32[]{:S(2)}) collective-permute-start(bf16[96,1536]{1,0:T(8,128)(2,1)} %collective-permute-done.15.refs_8_.refs_14_), channel_id=1, source_target_pairs={{0,8},{8,16},{16,24},{24,28},{28,20},{20,12},{12,4},{4,0},{1,9},{9... | collective-permute-start | bytes 884744 | tf_op jit(solution)/shard_map/ppermute | solution.py:790
  91.8 17.9 %collective-permute-start.21 = (bf16[96,1536]{1,0:T(8,128)(2,1)}, bf16[96,1536]{1,0:T(8,128)(2,1)}, u32[]{:S(2)}, u32[]{:S(2)}) collective-permute-start(bf16[96,1536]{1,0:T(8,128)(2,1)} %collective-permute-done.18.refs_3_.refs_5_), channel_id=1, source_target_pairs={{0,8},{8,16},{16,24},{24,28},{28,20},{20,12},{12,4},{4,0},{1,9},{9... | collective-permute-start | bytes 884744 | tf_op jit(solution)/shard_map/ppermute | solution.py:790
  109.8 30.8 %collective-permute-start.27 = (bf16[192,1152]{1,0:T(8,128)(2,1)}, bf16[192,1152]{1,0:T(8,128)(2,1)S(1)}, u32[]{:S(2)}, u32[]{:S(2)}) collective-permute-start(bf16[192,1152]{1,0:T(8,128)(2,1)} %get-tuple-element.201), channel_id=1, source_target_pairs={{0,3},{1,2},{2,1},{3,0},{4,7},{5,6},{6,5},{7,4},{8,11},{9,10},{10,... | collective-permute-start | bytes 1327112 | tf_op jit(solution)/shard_map/ppermute | solution.py:727
  110.4 29.4 %collective-permute-start.28 = (bf16[192,768]{1,0:T(8,128)(2,1)S(1)}, bf16[192,768]{1,0:T(8,128)(2,1)S(1)}, u32[]{:S(2)}, u32[]{:S(2)}) collective-permute-start(bf16[192,768]{1,0:T(8,128)(2,1)S(1)} %get-tuple-element.350.wo0), channel_id=1, source_target_pairs={{0,2},{1,3},{2,0},{3,1},{4,6},{5,7},{6,4},{7,5},{8,10},{9,11},{10,... | collective-permute-start | bytes 884744 | tf_op jit(solution)/shard_map/ppermute | solution.py:727
  112.8 27.8 %collective-permute-start.25 = (bf16[96,1536]{1,0:T(8,128)(2,1)}, bf16[96,1536]{1,0:T(8,128)(2,1)S(1)}, u32[]{:S(2)}, u32[]{:S(2)}) collective-permute-start(bf16[96,1536]{1,0:T(8,128)(2,1)} %collective-permute-done.21.refs_4_.refs_6_), channel_id=1, source_target_pairs={{0,8},{8,16},{16,24},{24,28},{28,20},{20,12},{12,4},{4,0},{1,9},{9... | collective-permute-start | bytes 884744 | tf_op jit(solution)/shard_map/ppermute | solution.py:790
  114.4 26.3 %collective-permute-start.26 = (bf16[96,1536]{1,0:T(8,128)(2,1)}, bf16[96,1536]{1,0:T(8,128)(2,1)S(1)}, u32[]{:S(2)}, u32[]{:S(2)}) collective-permute-start(bf16[96,1536]{1,0:T(8,128)(2,1)} %collective-permute-done.22.refs_5_.refs_7_), channel_id=1, source_target_pairs={{8,0},{16,8},{24,16},{28,24},{20,28},{12,20},{4,12},{0,4},{9,1},{1... | collective-permute-start | bytes 884744 | tf_op jit(solution)/shard_map/ppermute | solution.py:794
  141.5 26.1 %collective-permute-start.33 = (bf16[256,768]{1,0:T(8,128)(2,1)S(1)}, bf16[256,768]{1,0:T(8,128)(2,1)S(1)}, u32[]{:S(2)}, u32[]{:S(2)}) collective-permute-start(bf16[256,768]{1,0:T(8,128)(2,1)S(1)} %bitcast.78), channel_id=1, source_target_pairs={{0,1},{1,0},{2,3},{3,2},{4,5},{5,4},{6,7},{7,6},{8,9},{9,8},{10,11... | collective-permute-start | bytes 1179656 | tf_op jit(solution)/shard_map/ppermute | solution.py:727
  166.0 17.5 %collective-permute-start.36 = (bf16[96,1536]{1,0:T(8,128)(2,1)S(1)}, bf16[96,1536]{1,0:T(8,128)(2,1)S(1)}, u32[]{:S(2)}, u32[]{:S(2)}) collective-permute-start(bf16[96,1536]{1,0:T(8,128)(2,1)S(1)} %collective-permute-done.31.refs_8_.refs_10_), channel_id=1, source_target_pairs={{0,8},{8,16},{16,24},{24,28},{28,20},{20,12},{12,4},{4,0},{1,9},{9... | collective-permute-start | bytes 884744 | tf_op jit(solution)/shard_map/ppermute | solution.py:790
  304.0 18.2 %collective-permute-start.42 = (bf16[1024,768]{1,0:T(8,128)(2,1)}, bf16[1024,768]{1,0:T(8,128)(2,1)}, u32[]{:S(2)}, u32[]{:S(2)}) collective-permute-start(bf16[1024,768]{1,0:T(8,128)(2,1)} %get-tuple-element.255.p_ref), channel_id=1, source_target_pairs={{0,1},{1,0},{2,3},{3,2},{4,5},{5,4},{6,7},{7,6},{8,9},{9,8},{10,11... | collective-permute-start | bytes 4718600 | tf_op jit(solution)/shard_map/ppermute | solution.py:727
  392.8 62.3 %collective-permute-start.44 = (bf16[1024,768]{1,0:T(8,128)(2,1)}, bf16[1024,768]{1,0:T(8,128)(2,1)S(1)}, u32[]{:S(2)}, u32[]{:S(2)}) collective-permute-start(bf16[1024,768]{1,0:T(8,128)(2,1)} %get-tuple-element.267.p_ref), channel_id=1, source_target_pairs={{0,1},{1,0},{2,3},{3,2},{4,5},{5,4},{6,7},{7,6},{8,9},{9,8},{10,11... | collective-permute-start | bytes 4718600 | tf_op jit(solution)/shard_map/ppermute | solution.py:727
  398.9 20.0 %collective-permute-start.63 = (bf16[192,384]{1,0:T(8,128)(2,1)S(1)}, bf16[192,384]{1,0:T(8,128)(2,1)S(1)}, u32[]{:S(2)}, u32[]{:S(2)}) collective-permute-start(bf16[192,384]{1,0:T(8,128)(2,1)S(1)} %get-tuple-element.332), channel_id=1, source_target_pairs={{8,0},{16,8},{24,16},{28,24},{20,28},{12,20},{4,12},{0,4},{9,1},{1... | collective-permute-start | bytes 442376 | tf_op jit(solution)/shard_map/ppermute | solution.py:839
  399.3 19.6 %collective-permute-start.49 = (bf16[192,384]{1,0:T(8,128)(2,1)S(1)}, bf16[192,384]{1,0:T(8,128)(2,1)S(1)}, u32[]{:S(2)}, u32[]{:S(2)}) collective-permute-start(bf16[192,384]{1,0:T(8,128)(2,1)S(1)} %get-tuple-element.333), channel_id=1, source_target_pairs={{0,8},{8,16},{16,24},{24,28},{28,20},{20,12},{12,4},{4,0},{1,9},{9... | collective-permute-start | bytes 442376 | tf_op jit(solution)/shard_map/ppermute | solution.py:839
  444.2 92.5 %collective-permute-start.38 = (bf16[1024,768]{1,0:T(8,128)(2,1)}, bf16[1024,768]{1,0:T(8,128)(2,1)}, u32[]{:S(2)}, u32[]{:S(2)}) collective-permute-start(bf16[1024,768]{1,0:T(8,128)(2,1)} %copy-done.56), channel_id=1, source_target_pairs={{0,1},{1,0},{2,3},{3,2},{4,5},{5,4},{6,7},{7,6},{8,9},{9,8},{10,11... | collective-permute-start | bytes 4718600 | tf_op jit(solution)/shard_map/ppermute | solution.py:727
  493.1 20.0 %collective-permute-start.97 = (bf16[192,384]{1,0:T(8,128)(2,1)S(1)}, bf16[192,384]{1,0:T(8,128)(2,1)S(1)}, u32[]{:S(2)}, u32[]{:S(2)}) collective-permute-start(bf16[192,384]{1,0:T(8,128)(2,1)S(1)} %collective-permute-done.96.refs_25_), channel_id=1, source_target_pairs={{8,0},{16,8},{24,16},{28,24},{20,28},{12,20},{4,12},{0,4},{9,1},{1... | collective-permute-start | bytes 442376 | tf_op jit(solution)/shard_map/ppermute | solution.py:845
  496.2 16.9 %collective-permute-start.56 = (bf16[192,384]{1,0:T(8,128)(2,1)S(1)}, bf16[192,384]{1,0:T(8,128)(2,1)S(1)}, u32[]{:S(2)}, u32[]{:S(2)}) collective-permute-start(bf16[192,384]{1,0:T(8,128)(2,1)S(1)} %collective-permute-done.55.refs_2_), channel_id=1, source_target_pairs={{0,8},{8,16},{16,24},{24,28},{28,20},{20,12},{12,4},{4,0},{1,9},{9... | collective-permute-start | bytes 442376 | tf_op jit(solution)/shard_map/ppermute | solution.py:845
  503.1 19.5 %collective-permute-start.70 = (bf16[192,384]{1,0:T(8,128)(2,1)S(1)}, bf16[192,384]{1,0:T(8,128)(2,1)S(1)}, u32[]{:S(2)}, u32[]{:S(2)}) collective-permute-start(bf16[192,384]{1,0:T(8,128)(2,1)S(1)} %collective-permute-done.69.refs_10_), channel_id=1, source_target_pairs={{8,0},{16,8},{24,16},{28,24},{20,28},{12,20},{4,12},{0,4},{9,1},{1... | collective-permute-start | bytes 442376 | tf_op jit(solution)/shard_map/ppermute | solution.py:845
  503.1 19.5 %collective-permute-start.84 = (bf16[192,384]{1,0:T(8,128)(2,1)S(1)}, bf16[192,384]{1,0:T(8,128)(2,1)S(1)}, u32[]{:S(2)}, u32[]{:S(2)}) collective-permute-start(bf16[192,384]{1,0:T(8,128)(2,1)S(1)} %collective-permute-done.83.refs_18_), channel_id=1, source_target_pairs={{0,8},{8,16},{16,24},{24,28},{28,20},{20,12},{12,4},{4,0},{1,9},{9... | collective-permute-start | bytes 442376 | tf_op jit(solution)/shard_map/ppermute | solution.py:845
  513.1 17.5 %collective-permute-start.57 = (bf16[192,384]{1,0:T(8,128)(2,1)S(1)}, bf16[192,384]{1,0:T(8,128)(2,1)S(1)}, u32[]{:S(2)}, u32[]{:S(2)}) collective-permute-start(bf16[192,384]{1,0:T(8,128)(2,1)S(1)} %collective-permute-done.56.refs_3_), channel_id=1, source_target_pairs={{0,8},{8,16},{16,24},{24,28},{28,20},{20,12},{12,4},{4,0},{1,9},{9... | collective-permute-start | bytes 442376 | tf_op jit(solution)/shard_map/ppermute | solution.py:845
  (220 other events, 3366.8 us)
Sparse Core Ops, SparseCore 0:
  391.6 142.5 all-reduce.3

commit v3 on v0

v3 whole, which is shorter than its diff:
```python
import functools
import math

import jax
import jax.numpy as jnp
from jax import lax
from jax.experimental import pallas as pl
from jax.experimental.pallas import tpu as pltpu
from jax.sharding import PartitionSpec as P

HD = 64
branch_scale = 48.0 ** (-0.5)
norm_eps = 1e-05
masked_score = -1e30
log2_e = math.log2(math.e)
MIB = 1 << 20
VMEM = 62
BLK = 256

f32 = jnp.float32
bf16 = jnp.bfloat16
STREAM = bf16

SWAP_CORE = [(s, s ^ 1) for s in range(4)]
SWAP_X = [(s, s ^ 2) for s in range(4)]
SWAP_BOTH = [(s, s ^ 3) for s in range(4)]


def dot_nn(a, b):
    return lax.dot_general(a, b, (((1,), (0,)), ((), ())), preferred_element_type=f32)


def dot_nt(a, b):
    return lax.dot_general(a, b, (((1,), (1,)), ((), ())), preferred_element_type=f32)


def dot_tn(a, b):
    return lax.dot_general(a, b, (((0,), (0,)), ((), ())), preferred_element_type=f32)


def call(body, name, sidx, grid, ins, outs, scratch, flops, vmem, exps=0):
    arrays = [a for a, _, _ in ins]
    in_specs = [
        pl.BlockSpec(memory_space=pl.ANY) if b is None else pl.BlockSpec(b, m) for _, b, m in ins
    ]
    out_specs = [
        pl.BlockSpec(memory_space=pl.ANY) if b is None else pl.BlockSpec(b, m) for _, b, m in outs
    ]
    out_shape = [s for s, _, _ in outs]
    nbytes = sum(a.size * a.dtype.itemsize for a in arrays)
    nbytes += sum(math.prod(s.shape) * s.dtype.itemsize for s in out_shape)
    return pl.pallas_call(
        body,
        name=name,
        grid_spec=pltpu.PrefetchScalarGridSpec(
            num_scalar_prefetch=1,
            grid=grid,
            in_specs=in_specs,
            out_specs=out_specs,
            scratch_shapes=scratch,
        ),
        out_shape=out_shape,
        compiler_params=pltpu.CompilerParams(
            dimension_semantics=("arbitrary",) * len(grid), vmem_limit_bytes=VMEM * MIB
        ),
        cost_estimate=pl.CostEstimate(
            flops=int(flops), bytes_accessed=int(nbytes), transcendentals=int(exps)
        ),
    )(sidx, *arrays)


RING = [0, 2, 4, 6, 7, 5, 3, 1]
RING_NEXT = [(RING[i], RING[(i + 1) % 8]) for i in range(8)]
RING_PREV = [(b, a) for a, b in RING_NEXT]
RING_STEPS = [0, -1, 1, -2, 2, -3, 3, -4]


def ring_place():
    row = lax.axis_index("rows").astype(jnp.int32)
    return jnp.where(row % 2 == 0, row // 2, 7 - row // 2)


def place_index():
    s = lax.axis_index("seq").astype(jnp.int32)
    zero = jnp.int32(0)
    row = lax.axis_index("rows").astype(jnp.int32) if lax.axis_size("rows") == 8 else zero
    place = ring_place() if lax.axis_size("rows") == 8 else zero
    return jnp.stack([s, s // 2, s % 2, place, row % 2, row // 2])


def sds(shape, dtype):
    return jax.ShapeDtypeStruct(shape, dtype)


def whole(block):
    zeros = (0,) * len(block)
    return lambda i, m: zeros


def row_tile(i, m):
    return (i, 0)


def stack_tile(i, m):
    return (i ^ m[0], 0, 0)


def normed(x):
    centre = x - jnp.mean(x, axis=-1, keepdims=True)
    spread = jnp.mean(centre * centre, axis=-1, keepdims=True)
    rstd = lax.rsqrt(spread + norm_eps)
    return centre * rstd, rstd


def norm_back(x, grad, gain):
    unit, rstd = normed(x)
    inner = grad * gain
    mean_inner = jnp.mean(inner, axis=-1, keepdims=True)
    mean_prod = jnp.mean(inner * unit, axis=-1, keepdims=True)
    return rstd * (inner - mean_inner - unit * mean_prod), unit


GAIN_A, GAIN_C, SHIFT_A, SHIFT_C, OUT_A, OUT_M = range(6)


def row_of(ref, k):
    return ref[k : k + 1, :]


def lane_half(shape):
    return lax.broadcasted_iota(jnp.int32, shape, 1) // HD


def block_start(i):
    return BLK * (i * (i + 1) // 2)


class Mover:
    def __init__(self, sems):
        self.sems = sems
        self.used = 0

    def make(self, src, dst):
        cp = pltpu.make_async_copy(src, dst, self.sems.at[self.used])
        self.used += 1
        return cp

    def go(self, src, dst):
        cp = self.make(src, dst)
        cp.start()
        return cp


def wait_all(copies):
    for cp in copies:
        cp.wait()


def tile_of(i):
    return pl.ds(i * BLK, BLK)


def pieces_in(mover, refs, dst, first, rows):
    out = []
    for j, ref in enumerate(refs):
        where = pl.multiple_of((first ^ j) * rows, 16)
        out.append(mover.go(ref, dst.at[pl.ds(where, rows)]))
    return out


def add_up(ref, value, start):
    here = jnp.sum(value, axis=0, keepdims=True)
    if start:
        ref[...] = here
    else:
        ref[...] += here


def back_pair(pair, pairs, tokens, qkv, att, datt, lse, bias, starts, dqkv, dq_acc):
    blocks = tokens // BLK
    half = lane_half((BLK, 2 * HD))
    score_scale = HD ** (-0.5)
    scale = score_scale * log2_e
    pick_row = lax.broadcasted_iota(jnp.int32, (8, 2 * HD), 0)
    pick = jnp.where(lane_half((8, 2 * HD)) == pick_row, 1.0, 0.0)
    prod = datt[pair].astype(f32) * att[pair].astype(f32)
    delta = lax.dot_general(
        pick, prod, (((1,), (1,)), ((), ())), precision=lax.Precision.HIGHEST, preferred_element_type=f32
    )
    for j in range(blocks):
        first = j * BLK
        span = slice(first, first + BLK)
        rest = pl.ds(first, tokens - first)
        kj = qkv[pair + pairs, span, :]
        vj = qkv[pair + 2 * pairs, span, :]
        qq = qkv[pair, rest, :]
        dd = datt[pair, rest, :]
        width = tokens - first
        zero = jnp.zeros_like(kj)
        dks, dvs, dss, khs = [], [], [], []
        for h in range(2):
            kh = jnp.where(half == h, kj, zero)
            vh = jnp.where(half == h, vj, zero)
            t = dot_nt(kh, qq) * scale + bias[:, starts[j] : starts[j] + width]
            p = jnp.exp2(t - lse[pair, h : h + 1, first:])
            dp = dot_nt(vh, dd)
            ds = (p * (dp - delta[h : h + 1, first:])).astype(bf16)
            dvs.append(dot_nn(p.astype(bf16), dd))
            dks.append(dot_nn(ds, qq))
            dss.append(ds)
            khs.append(kh)
        dk = jnp.where(half == 0, dks[0], dks[1]) * score_scale
        dv = jnp.where(half == 0, dvs[0], dvs[1])
        dqkv[pair + pairs, span, :] = dk.astype(bf16)
        dqkv[pair + 2 * pairs, span, :] = dv.astype(bf16)
        dq = dot_tn(jnp.concatenate(dss, axis=0), jnp.concatenate(khs, axis=0))
        if j == 0:
            dq_acc[...] = dq
        else:
            dq_acc[first:, :] += dq
    dqkv[pair] = (dq_acc[...] * score_scale).astype(bf16)


def forward_pair(pair, pairs, blocks, qkv, bias, att, lse):
    half = lane_half((BLK, 2 * HD))
    scale = HD ** (-0.5) * log2_e
    for i in range(blocks):
        width = BLK * (i + 1)
        span = slice(i * BLK, (i + 1) * BLK)
        qb = qkv[pair, span, :]
        kk = qkv[pair + pairs, 0:width, :]
        vv = qkv[pair + 2 * pairs, 0:width, :]
        mixed, logs = [], []
        for h in range(2):
            qh = jnp.where(half == h, qb, jnp.zeros_like(qb))
            t = dot_nt(qh, kk) * scale + bias[:, block_start(i) : block_start(i) + width]
            top = jnp.max(t, axis=-1, keepdims=True)
            p = jnp.exp2(t - top)
            total = jnp.sum(p, axis=-1, keepdims=True)
            o = dot_nn(p.astype(bf16), vv)
            mixed.append(o / total)
            logs.append(jnp.broadcast_to(top + jnp.log2(total), (BLK, 2 * HD)))
        att[pair, span, :] = jnp.where(half == 0, mixed[0], mixed[1]).astype(bf16)
        turned = jnp.transpose(jnp.where(half == 0, logs[0], logs[1]))
        lse[pair, 0:1, span] = turned[0:1, :]
        lse[pair, 1:2, span] = turned[HD : HD + 1, :]


def attn_block_body(l, first, m, *refs):
    count = 1 if first else 3
    sources = refs[:count]
    wo0, wo1, w0, w1, w2, w3 = refs[count : count + 6]
    vec, prev, bias_row, drow, dcol = refs[count + 6 : count + 11]
    refs = refs[count + 11 :]
    if not first:
        x_out, refs = refs[0], refs[1:]
    ln_out, qkv_out, att_out, part_out, lse = refs[:5]
    bufs = refs[5 : 5 + count]
    (wo, w, lns, qkv, att, parts, bias, sems) = refs[5 + count :]
    tokens, d = lns.shape
    blocks = tokens // BLK
    pairs = att.shape[0]
    q = w0.shape[0]
    half = d // 2
    move = Mover(sems)
    c_w = pieces_in(move, (w0, w1, w2, w3), w, m[0], q)
    c_tiles = []
    for t in range(blocks):
        for ref, dst in zip(sources, bufs):
            src = ref.at[t ^ m[0]] if len(ref.shape) == 3 else ref.at[tile_of(t)]
            c_tiles.append(move.go(src, dst.at[tile_of(t)]))
    c_wo = pieces_in(move, (wo0.at[l], wo1), wo, m[1], q)
    for i in range(blocks):
        width = BLK * (i + 1)
        begin = i * BLK
        qpos = begin + lax.broadcasted_iota(jnp.int32, (BLK, width), 0)
        kpos = lax.broadcasted_iota(jnp.int32, (BLK, width), 1)
        same = dcol[begin : begin + BLK, :] == drow[:, :width]
        allowed = (kpos <= qpos) & same
        bias[:, block_start(i) : block_start(i) + width] = jnp.where(allowed, 0.0, masked_score)
    wait_all(c_w)
    c_out = []
    mine = pl.ds(pl.multiple_of(m[1] * half, 128), half)
    for t in range(blocks):
        wait_all(c_tiles[count * t : count * t + count])
        span = tile_of(t)
        if first:
            x = bufs[0][span, :].astype(f32)
        else:
            part = bufs[1][span, :].astype(f32) + bufs[2][span, :].astype(f32) + row_of(prev, OUT_M)
            x = bufs[0][span, :].astype(f32) + branch_scale * part
            bufs[0][span, :] = x.astype(STREAM)
            c_out.append(move.go(bufs[0].at[span], x_out.at[span]))
        unit, _ = normed(x)
        ln = (unit * row_of(vec, GAIN_A) + row_of(vec, SHIFT_A)).astype(bf16)
        lns[span, :] = ln
        c_out.append(move.go(lns.at[span, mine], ln_out.at[span]))
        row = (dot_nn(ln, w[...]) + bias_row[...]).astype(bf16)
        for k in range(3 * pairs):
            cols = slice(k * 2 * HD, (k + 1) * 2 * HD)
            qkv[k, span, :] = row[:, cols]
    for k in range(3 * pairs):
        c_out.append(move.go(qkv.at[k], qkv_out.at[k]))

    @pl.loop(0, pairs)
    def _(pair):
        forward_pair(pair, pairs, blocks, qkv, bias, att, lse)

    for k in range(pairs):
        c_out.append(move.go(att.at[k], att_out.at[k]))
    wait_all(c_wo)
    for t in range(blocks):
        span = tile_of(t)
        row = jnp.concatenate([att[k, span, :] for k in range(pairs)], axis=1)
        parts[span, :] = dot_nn(row, wo[...]).astype(bf16)
        c_out.append(move.go(parts.at[span], part_out.at[span]))
    wait_all(c_out)


def attn_block_forward(sidx, l, source, wo_pieces, pieces, vec, prev, bias, drow, dcol):
    first = len(source) == 1
    q, cols = pieces[0].shape
    d = 4 * q
    tokens = drow.shape[1]
    width = cols // 3
    pairs = width // (2 * HD)
    ins = [(a, None, None) for a in (*source, *wo_pieces, *pieces)]
    ins += [(a, a.shape, whole(a.shape)) for a in (vec, prev, bias, drow, dcol)]
    outs = [] if first else [(sds((tokens, d), STREAM), None, None)]
    outs += [
        (sds((tokens, d // 2), bf16), None, None),
        (sds((3 * pairs, tokens, 2 * HD), bf16), None, None),
        (sds((pairs, tokens, 2 * HD), bf16), None, None),
        (sds((tokens, d), bf16), None, None),
        (sds((pairs, 8, tokens), f32), (pairs, 8, tokens), whole((0, 0, 0))),
    ]
    blocks = tokens // BLK
    scratch = [pltpu.VMEM((tokens, d), a.dtype) for a in source]
    scratch += [
        pltpu.VMEM((width, d), bf16),
        pltpu.VMEM((d, cols), bf16),
        pltpu.VMEM((tokens, d), bf16),
        pltpu.VMEM((3 * pairs, tokens, 2 * HD), bf16),
        pltpu.VMEM((pairs, tokens, 2 * HD), bf16),
        pltpu.VMEM((tokens, d), bf16),
        pltpu.VMEM((BLK, block_start(blocks)), f32),
        pltpu.SemaphoreType.DMA((64,)),
    ]
    return call(
        functools.partial(attn_block_body, l, first),
        "attention_block",
        sidx,
        (1,),
        ins,
        outs,
        scratch,
        4 * tokens * tokens * width + 2 * tokens * d * (cols + width),
        40,
        exps=tokens * tokens * pairs,
    )


def mlp_weights_in(move, l, m, refs, wf, wp):
    if len(refs) == 6:
        first = pieces_in(move, refs[:4], wf, m[0], refs[0].shape[0])
        return first, pieces_in(move, refs[4:], wp, m[1], refs[4].shape[0])
    keep, near, own = refs[0], refs[1], refs[2].at[l]
    far = refs[3:]
    rows = keep.shape[0]
    deep, wide = own.shape
    first = pieces_in(move, (keep, near), wf, m[0], rows)
    second = pieces_in(move, (own,), wp, m[1], deep)
    n = len(far)
    part = far[0].shape[0] // 2
    for ref, t in zip(far, RING_STEPS):
        chunk = (m[3] + t + n) % n
        at = pl.multiple_of((1 - m[1]) * 2 * rows + chunk * part, 16)
        first.append(move.go(ref.at[pl.ds(0, part)], wf.at[pl.ds(at, part)]))
        for side in range(2):
            at = pl.multiple_of((1 - m[1]) * deep + side * (deep // 2) + chunk * part, 16)
            src = ref.at[pl.ds(part, part), pl.ds(side * wide, wide)]
            second.append(move.go(src, wp.at[pl.ds(at, part)]))
    return first, second


def gelu_and_slope(pre):
    root = math.sqrt(2.0 / math.pi)
    sq = pre * pre
    gate = 0.5 * jnp.tanh(pre * (root + root * 0.044715 * sq)) + 0.5
    rise = pre * (2.0 * root + 6.0 * root * 0.044715 * sq)
    return pre * gate, gate + gate * ((1.0 - gate) * rise)


def mlp_block_body(l, ahead, back, count, m, *refs):
    take = lambda k: (refs[:k], refs[k:])
    vec = prev = fcb = None
    sources, refs = take(3 if ahead else 0)
    (cot,), refs = take(1) if ahead and back else ((None,), refs)
    grads, refs = take(4 if back and not ahead else 0)
    (slope_in, act_in, ln_in), refs = take(3) if back and not ahead else ((None,) * 3, refs)
    weights, refs = take(count)
    if ahead:
        (vec, fcb), refs = take(2)
    else:
        (vec,), refs = take(1)
    if ahead:
        (mid_out, part_out), refs = take(2)
        if back:
            (own_out,), refs = take(1)
        else:
            (ln_out, act_out, slope_out), refs = take(3)
    if back:
        if not ahead:
            (g_out,), refs = take(1)
        (back_out, mine, other, send_mine, send_other, sum_mlp, sum_pre), refs = take(7)
        if not ahead:
            (sum_gain, sum_shift), refs = take(2)
    b0, b1, b2, b3, wf, wp, lns, act, slope, dmlp, sems = refs
    tokens, d = b1.shape
    blocks = tokens // BLK
    hidden = wf.shape[1]
    q = d // 4
    move = Mover(sems)
    c_tiles = []
    if ahead:
        loads = list(zip(sources, (b0, b1, b2))) + ([(cot, b3)] if back else [])
    else:
        loads = list(zip(grads, (b0, b1, b2, b3)))
    c_wp = []
    if ahead:
        c_wf, c_wp = mlp_weights_in(move, l, m, weights, wf, wp)
    for t in range(blocks):
        for ref, dst in loads:
            src = ref.at[t ^ m[0]] if len(ref.shape) == 3 else ref.at[tile_of(t)]
            c_tiles.append(move.go(src, dst.at[tile_of(t)]))
    if not ahead:
        c_wf, c_wp = mlp_weights_in(move, l, m, weights, wf, wp)
        c_slope = [move.go(slope_in.at[tile_of(t)], slope.at[tile_of(t)]) for t in range(blocks)]
        c_late = [move.go(act_in, act.at[:, pl.ds(0, act_in.shape[1])]), move.go(ln_in, lns.at[:, pl.ds(0, d // 2)])]
    c_out = []
    n = len(loads)
    wide = hidden // 2
    for t in range(blocks):
        wait_all(c_tiles[n * t : n * t + n])
        span = tile_of(t)
        if ahead:
            part = b1[span, :].astype(f32) + b2[span, :].astype(f32) + row_of(vec, OUT_A)
            mid = b0[span, :].astype(f32) + branch_scale * part
            b0[span, :] = mid.astype(b0.dtype)
            c_out.append(move.go(b0.at[span], mid_out.at[span]))
            if back:

                @pl.when(m[0] == t)
                def _():
                    own_out[...] = mid

            unit, _ = normed(mid)
            ln = (unit * row_of(vec, GAIN_C) + row_of(vec, SHIFT_C)).astype(bf16)
            lns[span, :] = ln
            if t == 0:
                wait_all(c_wf)
            value, rise = gelu_and_slope(dot_nn(ln, wf[...]) + fcb[...])
            low = value.astype(bf16)
            act[span, :] = low
            if not back:
                slope[span, :] = rise.astype(bf16)
                cols = pl.ds(pl.multiple_of(m[1] * (d // 2), 128), d // 2)
                c_out.append(move.go(lns.at[span, cols], ln_out.at[span]))
                cols = pl.ds(pl.multiple_of(m[1] * wide, 128), wide)
                c_out.append(move.go(act.at[span, cols], act_out.at[span]))
                c_out.append(move.go(slope.at[span], slope_out.at[span]))
            if t == 0:
                wait_all(c_wp)
            b1[span, :] = dot_nn(low, wp[...]).astype(bf16)
            c_out.append(move.go(b1.at[span], part_out.at[span]))
        if back:
            if ahead:
                g = b3[span, :].astype(f32)
            else:
                if t == 0:
                    wait_all(c_wp)
                wait_all(c_slope[t : t + 1])
                rise = slope[span, :].astype(f32)
                grad = b2[span, :].astype(f32) + b3[span, :].astype(f32)
                part, unit = norm_back(b1[span, :].astype(f32), grad, row_of(vec, GAIN_A))
                add_up(sum_gain, grad * unit, t == 0)
                add_up(sum_shift, grad, t == 0)
                g = b0[span, :].astype(f32) + part
                b0[span, :] = g.astype(b0.dtype)
                c_out.append(move.go(b0.at[span], g_out.at[span]))
            low = (branch_scale * g).astype(bf16)
            dmlp[span, :] = low
            add_up(sum_mlp, low.astype(f32), t == 0)
            dpre = (dot_nt(low, wp[...]) * rise).astype(bf16)
            slope[span, :] = dpre
            add_up(sum_pre, dpre.astype(f32), t == 0)
            if t == 0 and not ahead:
                wait_all(c_wf)
            b2[span, :] = dot_nt(dpre, wf[...]).astype(bf16)
            c_out.append(move.go(b2.at[span], back_out.at[span]))
    if back:
        y = m[4]
        if not ahead:
            wait_all(c_late)
            turned = jnp.transpose(act[:, 0:wide])
        else:
            turned = jnp.transpose(jnp.where(m[1] == 0, act[:, 0:wide], act[:, wide:]))
        grad = dot_nn(turned, dmlp[...]).astype(bf16)
        h = grad.shape[0] // 2
        mine[0:h, :] = jnp.where(y == 0, grad[:h], grad[h:])
        other[0:h, :] = jnp.where(y == 0, grad[h:], grad[:h])
        half = d // 2
        if not ahead:
            turned = jnp.transpose(lns[:, 0:half])
        else:
            turned = jnp.transpose(jnp.where(m[1] == 0, lns[:, 0:half], lns[:, half:]))
        sides = [dot_nn(turned, slope[:, i * d : (i + 1) * d]).astype(bf16) for i in range(2)]
        for here, there, i in ((mine, send_mine, 0), (other, send_other, 1)):
            side = jnp.where(y == i, sides[0], sides[1])
            here[h : h + q, :] = jnp.where(m[2] == 0, side[:q], side[q:])
            there[...] = jnp.where(m[2] == 0, side[q:], side[:q])
    wait_all(c_out)


def mlp_block(sidx, l, vec, weights, ahead=None, back=None, fcb=None):
    d = vec.shape[1]
    if ahead is not None:
        tokens = ahead[1].shape[0]
        hidden = fcb.shape[1]
        sources = list(ahead) + ([back[0]] if back else [])
        types = [STREAM if ahead[0].ndim == 2 else ahead[0].dtype, bf16, bf16, bf16]
        vectors_in = [vec, fcb]
    else:
        tokens, hidden = back[4].shape
        sources = list(back)
        types = [back[0].dtype, back[1].dtype, bf16, bf16]
        vectors_in = [vec]
    q = d // 4
    ins = [(a, None, None) for a in sources + list(weights)]
    ins += [(a, a.shape, whole(a.shape)) for a in vectors_in]
    stay = lambda shape, dtype: (sds(shape, dtype), shape, whole(shape))
    away = lambda shape, dtype: (sds(shape, dtype), None, None)
    outs = []
    if ahead is not None:
        outs += [away((tokens, d), STREAM), away((tokens, d), bf16)]
        if back:
            outs += [stay((BLK, d), f32)]
        else:
            outs += [
                away((tokens, d // 2), bf16),
                away((tokens, hidden // 2), bf16),
                away((tokens, hidden), bf16),
            ]
    if back:
        if ahead is None:
            outs += [away((tokens, d), back[0].dtype)]
        outs += [away((tokens, d), bf16)]
        outs += [stay((3 * q, d), bf16)] * 2 + [stay((q, d), bf16)] * 2
        outs += [stay((1, d), f32), stay((1, hidden), f32)]
        if ahead is None:
            outs += [stay((1, d), f32)] * 2
    scratch = [pltpu.VMEM((tokens, d), t) for t in types]
    scratch += [
        pltpu.VMEM((d, hidden), bf16),
        pltpu.VMEM((hidden, d), bf16),
        pltpu.VMEM((tokens, d), bf16),
        pltpu.VMEM((tokens, hidden), bf16),
        pltpu.VMEM((tokens, hidden), bf16),
        pltpu.VMEM((tokens, d), bf16),
        pltpu.SemaphoreType.DMA((96,)),
    ]
    return call(
        functools.partial(mlp_block_body, l, ahead is not None, bool(back), len(weights)),
        "mlp_block" + ("_forward" if ahead is not None else "") + ("_backward" if back else ""),
        sidx,
        (1,),
        ins,
        outs,
        scratch,
        (4 * bool(ahead is not None) + 8 * bool(back)) * tokens * d * hidden,
        48,
        exps=tokens * hidden,
    )


def attn_block_back_body(l, m, *refs):
    (g_in, mid_in, p_in, r_in, wo0, wo1, qkv_in, att_in, ln_in, w0, w1, w2, w3) = refs[:13]
    (vec, drow, dcol, lse) = refs[13:17]
    (gm_out, part_out, mine, other, send_mine, send_other) = refs[17:23]
    (sum_attn, sum_gain, sum_shift, sum_qkv) = refs[23:27]
    (gs, mids, ps, rs, wo, qkv, att, lns, w, dattn, datt, dqkv, bias, dq_acc, sems) = refs[27:]
    tokens, d = mids.shape
    blocks = tokens // BLK
    pairs = att.shape[0]
    q = w0.shape[0]
    move = Mover(sems)
    c_wo = pieces_in(move, (wo0.at[l], wo1), wo, m[1], q)
    c_tiles = []
    loads = [(g_in, gs), (mid_in, mids), (p_in, ps), (r_in, rs)]
    for t in range(blocks):
        for ref, dst in loads:
            src = ref.at[t ^ m[0]] if len(ref.shape) == 3 else ref.at[tile_of(t)]
            c_tiles.append(move.go(src, dst.at[tile_of(t)]))
    c_qkv = [move.go(qkv_in, qkv), move.go(att_in, att)]
    c_w = pieces_in(move, (w0, w1, w2, w3), w, m[0], q)
    half = d // 2
    c_ln = [move.go(ln_in, lns)]

    starts = [sum(tokens - BLK * a for a in range(j)) for j in range(blocks)]
    for j in range(blocks):
        width = tokens - j * BLK
        first = j * BLK
        kpos = lax.broadcasted_iota(jnp.int32, (BLK, width), 0)
        qpos = lax.broadcasted_iota(jnp.int32, (BLK, width), 1)
        same = dcol[first : first + BLK, :] == drow[:, first:]
        allowed = (kpos <= qpos) & same
        bias[:, starts[j] : starts[j] + width] = jnp.where(allowed, 0.0, masked_score)

    wait_all(c_wo)
    c_out = []
    for t in range(blocks):
        wait_all(c_tiles[4 * t : 4 * t + 4])
        span = tile_of(t)
        grad = ps[span, :].astype(f32) + rs[span, :].astype(f32)
        part, unit = norm_back(mids[span, :].astype(f32), grad, row_of(vec, GAIN_C))
        add_up(sum_gain, grad * unit, t == 0)
        add_up(sum_shift, grad, t == 0)
        gm = gs[span, :].astype(f32) + part
        gs[span, :] = gm.astype(gs.dtype)
        c_out.append(move.go(gs.at[span], gm_out.at[span]))
        low = (branch_scale * gm).astype(bf16)
        dattn[span, :] = low
        add_up(sum_attn, low.astype(f32), t == 0)
        heads = dot_nt(low, wo[...]).astype(bf16)
        for k in range(pairs):
            datt[k, span, :] = heads[:, k * 2 * HD : (k + 1) * 2 * HD]

    wait_all(c_qkv)

    @pl.loop(0, pairs)
    def _(pair):
        back_pair(pair, pairs, tokens, qkv, att, datt, lse, bias, starts, dqkv, dq_acc)

    wait_all(c_w)
    for t in range(blocks):
        span = tile_of(t)
        row = jnp.concatenate([dqkv[k, span, :] for k in range(3 * pairs)], axis=1)
        ps[span, :] = dot_nt(row, w[...]).astype(bf16)
        c_out.append(move.go(ps.at[span], part_out.at[span]))
        add_up(sum_qkv, row.astype(f32), t == 0)

    wait_all(c_ln)
    quart = q // 2
    y = m[4]
    turned = jnp.concatenate([jnp.transpose(att[k]) for k in range(pairs)], axis=0)
    left = jnp.where(m[1] == 0, turned[:q], turned[q : 2 * q])
    g_o = dot_nn(left, dattn[...]).astype(bf16)
    for i in range(2):
        cols = slice(i * half, (i + 1) * half)
        a, b = g_o[:quart, cols], g_o[quart:, cols]
        mine[i * quart : (i + 1) * quart, :] = jnp.where(y == 0, a, b)
        other[i * quart : (i + 1) * quart, :] = jnp.where(y == 0, b, a)
    turned = jnp.transpose(lns[...])
    for p in range(3):
        right = jnp.concatenate([dqkv[p * pairs + k] for k in range(pairs)], axis=1)
        grad = dot_nn(turned, right).astype(bf16)
        keep = jnp.where(m[2] == 0, grad[:q], grad[q:])
        send = jnp.where(m[2] == 0, grad[q:], grad[:q])
        at = (2 + p) * quart
        mine[at : at + quart, :] = jnp.where(y == 0, keep[:quart], keep[quart:])
        other[at : at + quart, :] = jnp.where(y == 0, keep[quart:], keep[:quart])
        at = p * quart
        send_mine[at : at + quart, :] = jnp.where(y == 0, send[:quart], send[quart:])
        send_other[at : at + quart, :] = jnp.where(y == 0, send[quart:], send[:quart])
    wait_all(c_out)


def attn_block_backward(sidx, l, g, mid, part, recv, wo_pieces, qkv, att, ln_a, pieces, vec, drow, dcol, lse):
    tokens, d = mid.shape
    q, cols = pieces[0].shape
    width = cols // 3
    pairs = width // (2 * HD)
    ins = [(a, None, None) for a in (g, mid, part, recv, *wo_pieces, qkv, att, ln_a, *pieces)]
    ins += [(a, a.shape, whole(a.shape)) for a in (vec, drow, dcol, lse)]
    stay = lambda shape, dtype: (sds(shape, dtype), shape, whole(shape))
    outs = [
        (sds((tokens, d), STREAM), None, None),
        (sds((tokens, d), bf16), None, None),
        stay((5 * q // 2, width), bf16),
        stay((5 * q // 2, width), bf16),
        stay((3 * q // 2, width), bf16),
        stay((3 * q // 2, width), bf16),
        stay((1, d), f32),
        stay((1, d), f32),
        stay((1, d), f32),
        stay((1, cols), f32),
    ]
    blocks = tokens // BLK
    wide = (tokens, 2 * HD)
    scratch = [
        pltpu.VMEM((tokens, d), g.dtype),
        pltpu.VMEM((tokens, d), mid.dtype),
        pltpu.VMEM((tokens, d), bf16),
        pltpu.VMEM((tokens, d), bf16),
        pltpu.VMEM((width, d), bf16),
        pltpu.VMEM((3 * pairs,) + wide, bf16),
        pltpu.VMEM((pairs,) + wide, bf16),
        pltpu.VMEM((tokens, d // 2), bf16),
        pltpu.VMEM((d, cols), bf16),
        pltpu.VMEM((tokens, d), bf16),
        pltpu.VMEM((pairs,) + wide, bf16),
        pltpu.VMEM((3 * pairs,) + wide, bf16),
        pltpu.VMEM((BLK, block_start(blocks)), f32),
        pltpu.VMEM(wide, f32),
        pltpu.SemaphoreType.DMA((64,)),
    ]
    return call(
        functools.partial(attn_block_back_body, l),
        "attention_block_backward",
        sidx,
        (1,),
        ins,
        outs,
        scratch,
        10 * tokens * tokens * width,
        48,
        exps=tokens * tokens * pairs,
    )


def add_rows(ref, value, start):
    @pl.when(start)
    def _():
        ref[...] = jnp.zeros_like(ref)

    ref[...] += jnp.sum(value, axis=0, keepdims=True)


def input_back_body(m, gm_ref, x_ref, p_ref, r_ref, vec, out_ref, sum_gain, sum_shift):
    tile = pl.program_id(0)
    grad = p_ref[...].astype(f32) + r_ref[...].astype(f32)
    part, unit = norm_back(x_ref[0].astype(f32), grad, row_of(vec, GAIN_A))
    add_rows(sum_gain, grad * unit, tile == 0)
    add_rows(sum_shift, grad, tile == 0)

    @pl.when(tile == m[0])
    def _():
        out_ref[...] = gm_ref[...].astype(f32) + part


def input_backward(sidx, gm, x, part, recv, vec):
    tokens, depth = gm.shape
    tile = (BLK, depth)
    ins = [(gm, tile, row_tile), (x, (1, BLK, depth), stack_tile)]
    ins += [(a, tile, row_tile) for a in (part, recv)]
    ins.append((vec, vec.shape, whole(vec.shape)))
    outs = [(sds((BLK, depth), f32), tile, whole((0, 0)))]
    outs += [(sds((1, depth), f32), (1, depth), whole((0, 0)))] * 2
    return call(input_back_body, "input_backward", sidx, (tokens // BLK,), ins, outs, [], tokens * depth, 16)


def swap(a, perm):
    return lax.ppermute(a, "seq", perm)


def split_body(m, qkv_ref, fc_ref, o_ref, qkv_keep, qkv_send, fc_keep, fc_send, o_out):
    core = m[2]
    o_out[...] = o_ref[0]
    q = qkv_ref.shape[1]
    pair = 2 * q
    for p in range(3):
        own, other = [], []
        for xside in range(2):
            col = (2 * p + xside) * pair
            both = qkv_ref[0, :, col : col + pair]
            own.append(jnp.where(core == 0, both[:, :q], both[:, q:]))
            other.append(jnp.where(core == 0, both[:, q:], both[:, :q]))
        qkv_keep[:, p * pair : (p + 1) * pair] = jnp.concatenate(own, axis=1)
        qkv_send[:, p * pair : (p + 1) * pair] = jnp.concatenate(other, axis=1)
    d = fc_ref.shape[2] // 4
    for xside in range(2):
        one = fc_ref[0, :, 2 * xside * d : (2 * xside + 1) * d]
        two = fc_ref[0, :, (2 * xside + 1) * d : (2 * xside + 2) * d]
        fc_keep[:, xside * d : (xside + 1) * d] = jnp.where(core == 0, one, two)
        fc_send[:, xside * d : (xside + 1) * d] = jnp.where(core == 0, two, one)


def split_columns(sidx, w_qkv, w_fc, w_o, l):
    _, rows, cols = w_qkv.shape
    hidden = w_fc.shape[2]
    at = lambda i, m: (l, 0, 0)
    depth = w_o.shape[2]
    ins = [(w_qkv, (1, rows, cols), at), (w_fc, (1, rows, hidden), at), (w_o, (1, rows, depth), at)]
    outs = []
    for width in (cols // 2, cols // 2, hidden // 2, hidden // 2, depth):
        outs.append((sds((rows, width), bf16), (rows, width), whole((0, 0))))
    return call(split_body, "split_columns", sidx, (1,), ins, outs, [], rows * cols, 16)


def column_pieces(keep, send):
    return [keep, swap(send, SWAP_CORE), swap(keep, SWAP_X), swap(send, SWAP_BOTH)]


def row_pieces(w):
    return [w, swap(w, SWAP_X)]


def far_piece_body(l, m, keep, near, proj, out, sems):
    part = out.shape[0] // 2
    wide = proj.shape[2]
    deep = proj.shape[1] // 2
    place = m[3]
    at = pl.multiple_of((place % 4) * part, 16)
    own = place // 4 == m[2]
    first = pltpu.make_async_copy(keep.at[pl.ds(at, part)], out.at[pl.ds(0, part)], sems.at[0])
    second = pltpu.make_async_copy(near.at[pl.ds(at, part)], out.at[pl.ds(0, part)], sems.at[0])
    lows = []
    for side in range(2):
        at = pl.multiple_of(side * deep + place * part, 16)
        dst = out.at[pl.ds(part, part), pl.ds(side * wide, wide)]
        lows.append(pltpu.make_async_copy(proj.at[l, pl.ds(at, part)], dst, sems.at[1 + side]))
    for cp in lows:
        cp.start()

    @pl.when(own)
    def _():
        first.start()
        first.wait()

    @pl.when(jnp.logical_not(own))
    def _():
        second.start()
        second.wait()

    for cp in lows:
        cp.wait()


def far_piece(sidx, keep, near, w_proj, l):
    shape = (keep.shape[0] // 2, keep.shape[1])
    ins = [(a, None, None) for a in (keep, near, w_proj)]
    outs = [(sds(shape, bf16), shape, whole(shape))]
    return call(
        functools.partial(far_piece_body, l),
        "far_piece",
        sidx,
        (1,),
        ins,
        outs,
        [pltpu.SemaphoreType.DMA((3,))],
        0,
        16,
    )[0]


def mlp_pieces(sidx, keep, send, w_proj, l, direct):
    if direct:
        return column_pieces(keep, send) + row_pieces(w_proj[l]), None
    near = swap(send, SWAP_CORE)
    mine = swap(far_piece(sidx, keep, near, w_proj, l), SWAP_X)
    return [keep, near, w_proj], [mine]


def ring_pass(held, t):
    if held is None:
        return []
    on = lax.ppermute(held[max(0, len(held) - 2)], "rows", RING_NEXT)
    if t == 4:
        new = [on]
    else:
        new = [on, lax.ppermute(held[-1], "rows", RING_PREV)]
    held += new
    return new


def gather_rows(a):
    near = swap(a, SWAP_CORE)
    far = swap(a, SWAP_X)
    return jnp.stack([a, near, far, swap(far, SWAP_CORE)])


SWAP_Y = [(r, r ^ 1) for r in range(8)]
SWAP_Z = [None] + [[(r, r ^ (2 * d)) for r in range(8)] for d in range(1, 4)]


def sum_y_body(m, mine, got, recv, got_recv, *refs):
    outs, full = refs[:-1], refs[-1]
    cut = mine.shape[0]
    full[0:cut, :] = (mine[...].astype(f32) + got[...].astype(f32)).astype(bf16)
    full[cut:, :] = (recv[...].astype(f32) + got_recv[...].astype(f32)).astype(bf16)
    rows = outs[0].shape[0]
    for d, out in enumerate(outs):
        out[...] = full[pl.ds(pl.multiple_of((m[5] ^ d) * rows, 16), rows), :]


def sum_y(sidx, mine, got, recv, got_recv):
    rows, d = mine.shape[0] + recv.shape[0], mine.shape[1]
    ins = [(a, a.shape, whole(a.shape)) for a in (mine, got, recv, got_recv)]
    outs = [(sds((rows // 4, d), bf16), (rows // 4, d), whole((0, 0)))] * 4
    scratch = [pltpu.VMEM((rows, d), bf16)]
    return call(sum_y_body, "sum_y", sidx, (1,), ins, outs, scratch, rows * d, 16)


class RowSum:
    def __init__(self, sidx, mine, other, send_mine, send_other):
        recv, recv_other = swap(send_mine, SWAP_CORE), swap(send_other, SWAP_CORE)
        self.sidx = sidx
        self.shape = (4, (mine.shape[0] + recv.shape[0]) // 4, mine.shape[1])
        self.direct = lax.axis_size("rows") != 8
        self.got = [None] * 4
        if self.direct:
            halves = [jnp.concatenate([mine, recv]), jnp.concatenate([other, recv_other])]
            self.held = [t.reshape(self.shape) for t in lax.psum(halves, "rows")]
        else:
            far = [lax.ppermute(a, "rows", SWAP_Y) for a in (other, recv_other)]
            self.held = [mine, far[0], recv, far[1]]

    def split(self):
        if not self.direct:
            self.held = list(sum_y(self.sidx, *self.held))

    def scatter(self, *steps):
        for d in steps:
            if not self.direct:
                self.got[d] = lax.ppermute(self.held[d], "rows", SWAP_Z[d])

    def total(self):
        if not self.direct:
            terms = [self.held[0]] + self.got[1:]
            self.held = [sum(a.astype(f32) for a in terms).astype(bf16)]
            self.got = [None] * 4

    def gather(self, *steps):
        for d in steps:
            if not self.direct:
                self.got[d] = lax.ppermute(self.held[0], "rows", SWAP_Z[d])

    def gather_y(self):
        if not self.direct:
            near = jnp.concatenate([self.held[0]] + self.got[1:]).reshape(self.shape)
            self.held = [near, lax.ppermute(near, "rows", SWAP_Y)]

    def state(self):
        return self.held, self.got

    def restore(self, state):
        self.held, self.got = list(state[0]), list(state[1])


def halves(m, near, far):
    def quarter(k):
        a, b = near[k ^ m[5]].astype(f32), far[k ^ m[5]].astype(f32)
        return jnp.where(m[4] == 0, a, b), jnp.where(m[4] == 0, b, a)

    return [quarter(k) for k in range(4)]


def finish_mlp_body(m, near, far, *refs):
    out_fc, out_proj = refs[-2:]
    q, d = near.shape[1:]
    parts = halves(m, near, far)
    for h in range(2):
        for k in range(2):
            at = (2 * h + k) * q
            out_proj[0, at : at + q, :] = parts[k][h]
        for c in range(2):
            col = (2 * h + c) * d
            out_fc[0, :, col : col + d] = jnp.where(m[2] == c, parts[2][h], parts[3][h])


def finish_attn_body(m, near, far, *refs):
    out_qkv, out_o = refs[-2:]
    rows, width = near.shape[1:]
    n = rows // 2
    q = width // 2
    parts = halves(m, near, far)
    for h in range(2):
        span = slice(h * n, (h + 1) * n)
        bits = [p for k in range(4) for p in (parts[k][h][:n], parts[k][h][n:])]
        out_o[0, span, 0:width] = bits[0]
        out_o[0, span, width:] = bits[1]
        for p in range(3):
            keep, recv = bits[2 + p], bits[5 + p]
            for xside in range(2):
                a = keep[:, xside * q : (xside + 1) * q]
                b = recv[:, xside * q : (xside + 1) * q]
                col = (2 * p + xside) * width
                out_qkv[0, span, col : col + width] = jnp.concatenate(
                    [jnp.where(m[2] == 0, a, b), jnp.where(m[2] == 0, b, a)], axis=1
                )


def finish(body, name, sidx, l, layers, held, before, shapes):
    args = list(held)
    in_specs = [pl.BlockSpec(a.shape, lambda i, m: (0, 0, 0)) for a in held]
    aliases = {}
    if before is not None:
        aliases = {1 + len(args) + k: k for k in range(len(before))}
        args += list(before)
        in_specs += [pl.BlockSpec(memory_space=pl.ANY)] * len(before)
    size = sum(math.prod(sh) for sh in shapes)
    return pl.pallas_call(
        body,
        name=name,
        grid_spec=pltpu.PrefetchScalarGridSpec(
            num_scalar_prefetch=1,
            grid=(1,),
            in_specs=in_specs,
            out_specs=[pl.BlockSpec((1,) + sh, lambda i, m: (l, 0, 0)) for sh in shapes],
        ),
        out_shape=[sds((layers,) + sh, f32) for sh in shapes],
        input_output_aliases=aliases,
        compiler_params=pltpu.CompilerParams(vmem_limit_bytes=VMEM * MIB),
        cost_estimate=pl.CostEstimate(flops=size, bytes_accessed=6 * size, transcendentals=0),
    )(sidx, *args)


def double_sum(a):
    n = lax.axis_size("rows")
    if n & (n - 1):
        return lax.psum(a, "rows")
    step = 1
    while step < n:
        a = a + lax.ppermute(a, "rows", [(r, r ^ step) for r in range(n)])
        step *= 2
    return a


def vectors_body(m, near, far, wide, qkv_bias, fcb):
    layers = near.shape[1]
    q = near.shape[3]
    for l in range(layers):
        full = []
        for k in range(4):
            core = (k % 2) ^ m[2]
            full.append(jnp.where(m[1] == k // 2, near[core, l], far[core, l]).astype(f32))
        every = jnp.concatenate(full, axis=1)
        wide[l, 0:4, :] = every[0:4]
        wide[l, 4:6, :] = every[6:8]
        wide[l, 6:8, :] = jnp.zeros((2, 4 * q), f32)
        here = [jnp.where(m[2] == 0, full[2 * xside], full[2 * xside + 1]) for xside in range(2)]
        pick = lambda r: [a[r : r + 1] for a in here]
        none = jnp.zeros((1, 2 * q), f32)
        qkv_bias[l] = jnp.concatenate(pick(4) + [none] + pick(5), axis=1)
        rest = [a[r : r + 1] for a in here for r in range(8, a.shape[0])]
        fcb[l] = jnp.concatenate(rest, axis=1)


def vectors(sidx, norm_gain, norm_bias, qv_bias, out_bias, fc_bias):
    layers, _, q = norm_gain.shape
    mine = jnp.concatenate(
        [norm_gain, norm_bias, qv_bias, out_bias, fc_bias.reshape(layers, -1, q)], axis=1
    )
    near = jnp.stack([mine, swap(mine, SWAP_CORE)])
    far = swap(near, SWAP_X)
    ins = [(a, a.shape, whole(a.shape)) for a in (near, far)]
    hidden = 2 * fc_bias.shape[1]
    outs = []
    for shape in ((layers, 8, 4 * q), (layers, 1, 6 * q), (layers, 1, hidden)):
        outs.append((sds(shape, f32), shape, whole(shape)))
    return call(vectors_body, "vectors", sidx, (1,), ins, outs, [], near.size, 16)


def on_device(
    block_input,
    output_cotangent,
    doc_ids,
    w_qkv,
    w_o,
    w_fc,
    w_proj,
    norm_gain,
    norm_bias,
    qv_bias,
    out_bias,
    fc_bias,
):
    sidx = place_index()
    s, xi, core = sidx[0], sidx[1], sidx[2]
    layers = w_qkv.shape[0]
    quarter = w_qkv.shape[1]
    tokens = doc_ids.shape[1]
    drow = doc_ids
    dcol = doc_ids.reshape(tokens, 1)

    def pin(outs, *groups):
        flat, tree = jax.tree.flatten((outs, groups))
        outs, groups = jax.tree.unflatten(tree, lax.optimization_barrier(flat))
        return (outs,) + tuple(groups)

    few = lax.axis_size("rows") != 8
    xs = gather_rows(block_input[0])
    wq, wo, wm, far = [], [], [], [None] * layers
    source = (w_qkv, w_fc, w_o)
    for l in range(layers):
        keep, send, fc_keep, fc_send, o = split_columns(sidx, *source, l)
        fixed, moved = mlp_pieces(sidx, fc_keep, fc_send, w_proj, l, few or l > 0)
        wm.append(fixed)
        far[l] = moved
        wq.append(column_pieces(keep, send))
        wo.append([w_o, swap(o, SWAP_X)])
        if moved is not None:
            source, far[l] = pin(source, moved)
    wide, qkv_bias, fcb = vectors(sidx, norm_gain, norm_bias, qv_bias, out_bias, fc_bias)
    cot = gather_rows(output_cotangent[0])

    ring_pass(far[0], 1)
    ring_pass(far[0], 2)
    ring_pass(far[0], 3)
    xs, far[0], wq[0] = pin(xs, far[0], wq[0])
    outs = attn_block_forward(sidx, 0, (xs,), wo[0], wq[0], wide[0], wide[0], qkv_bias[0], drow, dcol)
    ring_pass(far[0], 4)
    outs, far[0], wq[1] = pin(outs, far[0], wq[1])
    ln_a, qkv, att, part, lse = outs
    save_a = [(xs, ln_a, qkv, att, lse)]
    recv = swap(part, SWAP_CORE)
    outs = mlp_block(sidx, 0, wide[0], wm[0] + (far[0] or []), ahead=(xs, part, recv), fcb=fcb[0])
    outs, wo[1], wm[1][2], cot = pin(outs, wo[1], wm[1][2], cot)
    mid, part, ln_c, act, slope = outs
    save_m = (ln_c, act, slope)
    mids = [mid]
    recv = swap(part, SWAP_CORE)
    outs = attn_block_forward(
        sidx, 1, (mid, part, recv), wo[1], wq[1], wide[1], wide[0], qkv_bias[1], drow, dcol
    )
    outs, wm[1] = pin(outs, wm[1])
    x, ln_a, qkv, att, part, lse = outs
    save_a.append((x, ln_a, qkv, att, lse))
    recv = swap(part, SWAP_CORE)
    outs = mlp_block(sidx, 1, wide[1], wm[1], ahead=(x, part, recv), back=(cot,), fcb=fcb[1])
    mid, part, own_mid, part_b, *pack, sum_mlp, sum_pre = outs
    mids.append(mid)

    quarter_of = lambda a: lax.dynamic_slice_in_dim(a[0], s * quarter, quarter)
    own_q = lambda a, at: lax.dynamic_slice_in_dim(a[0], at + xi * quarter, quarter)
    own_h = lambda a: lax.dynamic_slice_in_dim(a[0], xi * (a.shape[1] // 2), a.shape[1] // 2)
    grads = [None] * layers
    norm_a = [None] * layers

    recv = swap(part_b, SWAP_CORE)
    up_m = RowSum(sidx, *pack)
    outs = attn_block_backward(sidx, 1, cot, mids[1], part_b, recv, wo[1], *save_a[1][2:4], save_a[1][1], wq[1], wide[1], drow, dcol, save_a[1][4])
    outs, up_m.held = pin(outs, up_m.held)
    gm, part_b, *pack, sum_attn, gain_c, shift_c, sum_qkv = outs
    grads[1] = [own_q(sum_qkv, 0), own_q(sum_qkv, 4 * quarter), quarter_of(sum_attn), quarter_of(sum_mlp), own_h(sum_pre), quarter_of(gain_c), quarter_of(shift_c)]
    up_m.split()
    up_a = RowSum(sidx, *pack)
    recv = swap(part_b, SWAP_CORE)
    recv, up_m.held = pin(recv, up_m.held)
    up_m.scatter(2, 1)

    outs = mlp_block(sidx, 0, wide[1], wm[0] + (far[0] or []), back=(gm, save_a[1][0], part_b, recv, save_m[2], save_m[1], save_m[0]))
    outs, up_m.got, up_a.held = pin(outs, up_m.got, up_a.held)
    g, part_b, *pack, sum_mlp, sum_pre, gain_a, shift_a = outs
    norm_a[1] = (gain_a, shift_a)
    up_m.scatter(3)
    up_a.split()
    up_a.scatter(2, 3, 1)
    low_m = RowSum(sidx, *pack)
    recv = swap(part_b, SWAP_CORE)
    recv, up_a.held = pin(recv, up_a.held)

    outs = attn_block_backward(sidx, 0, g, mids[0], part_b, recv, wo[0], *save_a[0][2:4], save_a[0][1], wq[0], wide[0], drow, dcol, save_a[0][4])
    outs, up_m.got, up_a.got, low_m.held = pin(outs, up_m.got, up_a.got, low_m.held)
    gm, part_b, *pack, sum_attn, gain_c, shift_c, sum_qkv = outs
    grads[0] = [own_q(sum_qkv, 0), own_q(sum_qkv, 4 * quarter), quarter_of(sum_attn), quarter_of(sum_mlp), own_h(sum_pre), quarter_of(gain_c), quarter_of(shift_c)]
    low_a = RowSum(sidx, *pack)
    up_m.total()
    up_m.gather(2, 3, 1)
    low_m.split()
    low_m.scatter(2, 3, 1)
    up_a.total()
    up_a.gather(2, 3, 1)
    recv = swap(part_b, SWAP_CORE)
    grad_input, gain_a, shift_a = input_backward(sidx, gm, xs, part_b, recv, wide[0])
    norm_a[0] = (gain_a, shift_a)
    low_a.split()
    low_a.scatter(2, 3, 1)
    up_m.gather_y()
    up_a.gather_y()
    low_m.total()
    low_m.gather(2, 3, 1)
    low_a.total()
    low_a.gather(2, 3, 1)
    low_m.gather_y()
    low_a.gather_y()

    recv = swap(part, SWAP_CORE)
    at = s * block_input.shape[1]
    own = lambda a: lax.dynamic_slice_in_dim(a, at, block_input.shape[1]).astype(f32)
    result = own_mid + branch_scale * (own(part) + own(recv) + wide[layers - 1][OUT_M])

    d = 4 * quarter
    outs_m, outs_a = None, None
    for l, sums_m, sums_a in ((1, up_m, up_a), (0, low_m, low_a)):
        outs_m = finish(
            finish_mlp_body, "unpack_mlp", sidx, l, layers, sums_m.held, outs_m, [(quarter, 4 * d), (d, d)]
        )
        outs_a = finish(
            finish_attn_body, "unpack_attn", sidx, l, layers, sums_a.held, outs_a, [(quarter, 3 * d), (quarter, d)]
        )
    out_fc, out_proj = outs_m
    out_qkv, out_o = outs_a

    small = []
    for l in range(layers):
        qb, vb, ob, mb, fb, gain_c, shift_c = grads[l]
        small.append(
            jnp.concatenate(
                [quarter_of(norm_a[l][0]), gain_c, quarter_of(norm_a[l][1]), shift_c, qb, vb, ob, mb, fb]
            )
        )
    small = double_sum(jnp.stack(small))
    pair = lambda k: small[:, k * quarter : (k + 2) * quarter].reshape(layers, 2, quarter)
    return (
        result[None],
        grad_input[None],
        out_qkv,
        out_o,
        out_fc,
        out_proj,
        pair(0),
        pair(2),
        pair(4),
        pair(6),
        small[:, 8 * quarter :],
    )


def solution(mesh):
    in_specs = (
        P("rows", "seq", None),
        P("rows", "seq", None),
        P("rows", None),
        P(None, "seq", None),
        P(None, "seq", None),
        P(None, "seq", None),
        P(None, "seq", None),
        P(None, None, "seq"),
        P(None, None, "seq"),
        P(None, None, "seq"),
        P(None, None, "seq"),
        P(None, "seq"),
    )
    out_specs = (
        P("rows", "seq", None),
        P("rows", "seq", None),
        P(None, "seq", None),
        P(None, "seq", None),
        P(None, "seq", None),
        P(None, "seq", None),
        P(None, None, "seq"),
        P(None, None, "seq"),
        P(None, None, "seq"),
        P(None, None, "seq"),
        P(None, "seq"),
    )
    return jax.shard_map(
        on_device, mesh=mesh, in_specs=in_specs, out_specs=out_specs, check_vma=False
    )
```

time: 1470 us -> 515 us (0.35)
  waiting for transfers between devices: 702 us -> 165 us
  matrix products: 242 us -> 0 us
  Pallas kernels: 0 us -> 215 us
  blocking collectives: 179 us -> 0 us
  local copies, waits for them, and re-layouts: 184 us -> 24.3 us
  other arithmetic: 83.4 us -> 12.8 us
  starting transfers between devices: 35.6 us -> 86.4 us
  loops' own time: 16.5 us -> 0 us
  between operations: 17.1 us -> 1.87 us
    psum x1 -> x0, waiting for transfers between devices: 408 us -> none  [layer_backward(): lax.psum((qkv_share, wo_share, fc_share, proj_share, gain_share, shift_sh...]
    dot_general x58 -> x0, matrix products: 218 us -> none  [the longest x10 41.7 us: matmul(): return jnp.dot(left, right, preferred_element_type=jnp.float32)]
    pallas_call x0 -> x20, Pallas kernels: none -> 215 us  [the longest x16 198 us: call(): pl.pallas_call(body, name=name, grid_spec=pltpu.PrefetchScalarGridSpec(nu...]
    ppermute x0 -> x84, waiting for transfers between devices: none -> 165 us  [the longest x38 57.4 us: swap(): return lax.ppermute(a, 'seq', perm)]
    reduce_scatter x8 -> x0, waiting for transfers between devices: 159 us -> none  [the longest x2 95 us: layer_backward(): lax.psum_scatter(grad_w_proj.astype(jnp.bfloat16), 'seq', scatter_dimensi...]
    all_gather x10 -> x0, blocking collectives: 111 us -> none  [the longest x2 39.5 us: fetch_params(): lax.all_gather(out_bias[layer_index], 'seq', axis=1, tiled=True)]
    unnamed x33 -> x0, waiting for transfers between devices: 105 us -> none
    ppermute x0 -> x84, starting transfers between devices: none -> 86.4 us  [the longest x12 24.6 us: gather(): self.got[d] = lax.ppermute(self.held[0], 'rows', SWAP_Z[d])]
  transfers between devices with their start and end apart: 34 -> 84, of which waited for: 15 -> 25; matrix products, arithmetic and copies ran while one was open for 28% -> 6% of each run, Pallas kernels for 0% -> 35%
where the time goes in v3:
time: 515 us; the launch traced here: 506 us
  Pallas kernels  215 us (42%)
  waiting for transfers between devices  165 us (32%)
  starting transfers between devices  86.4 us (17%)
  local copies, waits for them, and re-layouts  24.3 us (5%)
  other arithmetic  12.8 us (2%)
    pallas_call x16, Pallas kernels, call(): pl.pallas_call(body, name=name, grid_spec=pltpu.PrefetchScalarGridSpec(nu...  198 us
    ppermute x38, waiting for transfers between devices, swap(): return lax.ppermute(a, 'seq', perm)  57.4 us
    ppermute x4, waiting for transfers between devices, gather_y(): self.held = [near, lax.ppermute(near, 'rows', SWAP_Y)]  35 us
    ppermute x12, waiting for transfers between devices, scatter(): self.got[d] = lax.ppermute(self.held[d], 'rows', SWAP_Z[d])  34.1 us
    ppermute x12, waiting for transfers between devices, gather(): self.got[d] = lax.ppermute(self.held[0], 'rows', SWAP_Z[d])  26 us
    ppermute x12, starting transfers between devices, gather(): self.got[d] = lax.ppermute(self.held[0], 'rows', SWAP_Z[d])  24.6 us
    ppermute x38, starting transfers between devices, swap(): return lax.ppermute(a, 'seq', perm)  19.6 us
    ppermute x12, starting transfers between devices, scatter(): self.got[d] = lax.ppermute(self.held[d], 'rows', SWAP_Z[d])  18.5 us
  transfers between devices with their start and end apart: 84, of which 25 were waited for; matrix products, arithmetic and copies ran while one was open for 6% of the time, Pallas kernels for 35%

profile of v3, /device:TPU:0, one launch (start us, length us, event | category | flops | bytes accessed | tf_op | source)
XLA Modules:
  0.0 505.8 jit_solution(3353546693749734377)
XLA Ops:
  1.3 4.4 split_columns.2
  14.3 7.6 %collective-permute-done.4.refs_6_.refs_10_ = bf16[96,1536]{1,0:T(8,128)(2,1)} collective-permute-done((bf16[96,1536]{1,0:T(8,128)(2,1)}, bf16[96,1536]{1,0:T(8,128)(2,1)}, u32[]{:S(2)}, u32[]{:S(2)}) %collective-permute-start.4) | collective-permute-done | bytes 294944 | tf_op jit(solution)/shard_map/ppermute | solution.py:763
  27.7 16.2 %collective-permute-done.16.far = bf16[2,2,12,192]{3,2,1,0:T(8,128)(2,1)S(1)} collective-permute-done((bf16[2,2,12,192]{3,2,1,0:T(8,128)(2,1)S(1)}, bf16[2,2,12,192]{3,2,1,0:T(8,128)(2,1)S(1)}, u32[]{:S(2)}, u32[]{:S(2)}) %collective-permute-start.16) | collective-permute-done | bytes 18464 | tf_op jit(solution)/shard_map/ppermute | solution.py:763
  54.6 7.3 %collective-permute-done.13.refs_6_.refs_12_ = bf16[192,1152]{1,0:T(8,128)(2,1)} collective-permute-done((bf16[192,1152]{1,0:T(8,128)(2,1)}, bf16[192,1152]{1,0:T(8,128)(2,1)}, u32[]{:S(2)}, u32[]{:S(2)}) %collective-permute-start.13) | collective-permute-done | bytes 442400 | tf_op jit(solution)/shard_map/ppermute | solution.py:763
  64.5 4.4 split_columns.3
  73.8 20.8 %attention_block.2 = (bf16[1024,384]{1,0:T(8,128)(2,1)}, bf16[9,1024,128]{2,1,0:T(8,128)(2,1)}, bf16[3,1024,128]{2,1,0:T(8,128)(2,1)}, bf16[1024,768]{1,0:T(8,128)(2,1)}, f32[3,8,1024]{2,1,0:T(8,128)}) custom-call(s32[6]{0:T(128)} %stack.69.m, bf16[4,256,768]{2,1,0:T(8,128)(2,1)} %pad_maximum_fusion.refs_0_.x_ref, bf16[2,192,768]{2,1,0:T(8,128)(2,1)} %refs_4_.2, ...), custom_call_target="tpu_custom_call" | custom-call | flops 4026531840 | bytes 9892352 | tf_op jit(solution)/shard_map/attention_block/pallas_call | solution.py:52
  97.2 9.9 %collective-permute-done.25 = bf16[256,768]{1,0:T(8,128)(2,1)S(1)} collective-permute-done((bf16[256,768]{1,0:T(8,128)(2,1)S(1)}, bf16[256,768]{1,0:T(8,128)(2,1)S(1)}, u32[]{:S(2)}, u32[]{:S(2)}) %collective-permute-start.25) | collective-permute-done | bytes 393248 | tf_op jit(solution)/shard_map/ppermute | solution.py:763
  112.7 15.1 %mlp_block_forward.1 = (bf16[1024,768]{1,0:T(8,128)(2,1)}, bf16[1024,768]{1,0:T(8,128)(2,1)}, bf16[1024,384]{1,0:T(8,128)(2,1)}, bf16[1024,768]{1,0:T(8,128)(2,1)}, bf16[1024,1536]{1,0:T(8,128)(2,1)}) custom-call(s32[6]{0:T(128)} %stack.69.m, bf16[4,256,768]{2,1,0:T(8,128)(2,1)} %pad_maximum_fusion.refs_0_.x_ref, ...), custom_call_target="tpu_custom_call" | custom-call | flops 4831838208 | bytes 19298304 | tf_op jit(solution)/shard_map/mlp_block_forward/pallas_call | solution.py:52
  134.4 32.7 %attention_block.3 = (bf16[1024,768]{1,0:T(8,128)(2,1)}, bf16[1024,384]{1,0:T(8,128)(2,1)}, bf16[9,1024,128]{2,1,0:T(8,128)(2,1)}, bf16[3,1024,128]{2,1,0:T(8,12...) custom-call(s32[6]{0:T(128)} %stack.69.m, bf16[1024,768]{1,0:T(8,128)(2,1)} %get-tuple-element.265.refs_0_.refs_1_, ...), custom_call_target="tpu_custom_call" | custom-call | flops 4026531840 | bytes 14610944 | tf_op jit(solution)/shard_map/attention_block/pallas_call | solution.py:52
  167.2 5.6 %collective-permute-done.29.refs_7_ = bf16[192,1536]{1,0:T(8,128)(2,1)} collective-permute-done((bf16[192,1536]{1,0:T(8,128)(2,1)S(1)}, bf16[192,1536]{1,0:T(8,128)(2,1)}, u32[]{:S(2)}, u32[]{:S(2)}) %collective-permute-start.29) | collective-permute-done | bytes 589856 | tf_op jit(solution)/shard_map/ppermute | solution.py:763
  173.1 3.4 collective-permute-done.31.refs_2_
  177.6 24.0 %mlp_block_forward_backward.1 = (bf16[1024,768]{1,0:T(8,128)(2,1)}, bf16[1024,768]{1,0:T(8,128)(2,1)}, f32[256,768]{1,0:T(8,128)}, bf16[1024,768]{1,0:T(8,128)(2...) custom-call(s32[6]{0:T(128)} %stack.69.m, ...), custom_call_target="tpu_custom_call" | custom-call | flops 14495514624 | bytes 18914304 | tf_op jit(solution)/shard_map/mlp_block_forward_backward/pallas_call | solution.py:52
  206.2 25.6 %attention_block_backward.2 = (bf16[1024,768]{1,0:T(8,128)(2,1)}, bf16[1024,768]{1,0:T(8,128)(2,1)}, bf16[480,384]{1,0:T(8,128)(2,1)}, bf16[480,384]{1,0:T(8,128...) custom-call(s32[6]{0:T(128)} %stack.69.m, ...), custom_call_target="tpu_custom_call" | custom-call | flops 4026531840 | bytes 17348096 | tf_op jit(solution)/shard_map/attention_block_backward/pallas_call | solution.py:52
  234.1 3.9 sum_y.4
  242.5 20.2 %mlp_block_backward.1 = (bf16[1024,768]{1,0:T(8,128)(2,1)}, bf16[1024,768]{1,0:T(8,128)(2,1)}, bf16[576,768]{1,0:T(8,128)(2,1)}, bf16[576,768]{1,0:T(8,128)(2,1)...) custom-call(s32[6]{0:T(128)} %stack.69.m, ...), custom_call_target="tpu_custom_call" | custom-call | flops 9663676416 | bytes 23239680 | tf_op jit(solution)/shard_map/mlp_block_backward/pallas_call | solution.py:52
  271.5 3.4 collective-permute-start.48
  280.1 25.7 %attention_block_backward.3 = (bf16[1024,768]{1,0:T(8,128)(2,1)}, bf16[1024,768]{1,0:T(8,128)(2,1)}, bf16[480,384]{1,0:T(8,128)(2,1)}, bf16[480,384]{1,0:T(8,128...) custom-call(s32[6]{0:T(128)} %stack.69.m, ...), custom_call_target="tpu_custom_call" | custom-call | flops 4026531840 | bytes 17348096 | tf_op jit(solution)/shard_map/attention_block_backward/pallas_call | solution.py:52
  309.4 9.5 %collective-permute-start.67 = (bf16[192,384]{1,0:T(8,128)(2,1)S(1)}, bf16[192,384]{1,0:T(8,128)(2,1)}, u32[]{:S(2)}, u32[]{:S(2)}) collective-permute-start(bf16[192,384]{1,0:T(8,128)(2,1)S(1)} %add_convert_fusion.2), channel_id=1, source_target_pairs={{0,16},{4,20},{8,24},{12,28},{16,0},{20,4},{24,8},{28,12},{1,17},{... | collective-permute-start | bytes 442376 | tf_op jit(solution)/shard_map/ppermute | solution.py:936
  320.4 3.9 sum_y.7
  324.3 3.0 collective-permute-start.70
  335.7 3.6 collective-permute-done.70
  339.3 26.5 %collective-permute-done.71 = bf16[192,768]{1,0:T(8,128)(2,1)S(1)} collective-permute-done((bf16[192,768]{1,0:T(8,128)(2,1)}, bf16[192,768]{1,0:T(8,128)(2,1)S(1)}, u32[]{:S(2)}, u32[]{:S(2)}) %collective-permute-start.71) | collective-permute-done | bytes 294944 | tf_op jit(solution)/shard_map/ppermute | solution.py:925
  370.7 20.4 %collective-permute-done.78 = bf16[192,768]{1,0:T(8,128)(2,1)S(1)} collective-permute-done((bf16[192,768]{1,0:T(8,128)(2,1)S(1)}, bf16[192,768]{1,0:T(8,128)(2,1)S(1)}, u32[]{:S(2)}, u32[]{:S(2)}) %collective-permute-start.78) | collective-permute-done | bytes 294944 | tf_op jit(solution)/shard_map/ppermute | solution.py:936
  391.1 5.9 %collective-permute-start.73 = (bf16[192,768]{1,0:T(8,128)(2,1)S(1)}, bf16[192,768]{1,0:T(8,128)(2,1)}, u32[]{:S(2)}, u32[]{:S(2)}) collective-permute-start(bf16[192,768]{1,0:T(8,128)(2,1)S(1)} %add_convert_fusion.1), channel_id=1, source_target_pairs={{0,8},{4,12},{8,0},{12,4},{16,24},{20,28},{24,16},{28,20},{1,9},{5... | collective-permute-start | bytes 884744 | tf_op jit(solution)/shard_map/ppermute | solution.py:936
  414.7 6.5 %input_backward.1 = (f32[256,768]{1,0:T(8,128)}, f32[1,768]{1,0:T(1,128)}, f32[1,768]{1,0:T(1,128)}) custom-call(s32[6]{0:T(128)} %stack.69.m, bf16[1024,768]{1,0:T(8,128)(2,1)} %get-tuple-element.374.gm_ref, bf16[4,256,768]{2,1,0:T(8,128)(2,1)} %pad_maximum_fusion.refs_0_.x_ref, bf16[1024,768]{1,0:T(8,128)(2,1)} %get-tuple-element.375.p_ref, ...), custom_call_target="tpu_custom_call" | custom-call | flops 786432 | bytes 7108608 | tf_op jit(solution)/shard_map/input_backward/pallas_call | solution.py:52
  428.1 7.6 %collective-permute-done.81 = f32[2,2304]{1,0:T(2,128)S(1)} collective-permute-done((f32[2,2304]{1,0:T(2,128)S(1)}, f32[2,2304]{1,0:T(2,128)S(1)}, u32[]{:S(2)}, u32[]{:S(2)}) %collective-permute-start.81) | collective-permute-done | bytes 18464 | tf_op jit(solution)/shard_map/ppermute | solution.py:1024
  442.4 3.7 collective-permute-done.82
  452.4 3.7 unpack_attn.2
  456.1 32.2 %collective-permute-done.65.far = bf16[4,192,384]{2,1,0:T(8,128)(2,1)} collective-permute-done((bf16[4,192,384]{2,1,0:T(8,128)(2,1)S(1)}, bf16[4,192,384]{2,1,0:T(8,128)(2,1)}, u32[]{:S(2)}, u32[]{:S(2)}) %collective-permute-start.65) | collective-permute-done | bytes 589856 | tf_op jit(solution)/shard_map/ppermute | solution.py:941
  488.4 3.7 unpack_attn.3
  492.1 5.0 unpack_mlp.2
  500.4 5.0 unpack_mlp.3
  (289 shorter events, 133.7 us)
Async XLA Ops:
  23.7 27.1 %collective-permute-start.12 = (bf16[192,1152]{1,0:T(8,128)(2,1)S(1)}, bf16[192,1152]{1,0:T(8,128)(2,1)}, u32[]{:S(2)}, u32[]{:S(2)}) collective-permute-start(bf16[192,1152]{1,0:T(8,128)(2,1)S(1)} %copy-done.39), channel_id=1, source_target_pairs={{0,2},{1,3},{2,0},{3,1},{4,6},{5,7},{6,4},{7,5},{8,10},{9,11},{10,... | collective-permute-start | bytes 1327112 | tf_op jit(solution)/shard_map/ppermute | solution.py:763
  68.8 25.8 %collective-permute-start.20 = (bf16[192,1152]{1,0:T(8,128)(2,1)}, bf16[192,1152]{1,0:T(8,128)(2,1)S(1)}, u32[]{:S(2)}, u32[]{:S(2)}) collective-permute-start(bf16[192,1152]{1,0:T(8,128)(2,1)} %get-tuple-element.247), channel_id=1, source_target_pairs={{0,3},{1,2},{2,1},{3,0},{4,7},{5,6},{6,5},{7,4},{8,11},{9,10},{10,... | collective-permute-start | bytes 1327112 | tf_op jit(solution)/shard_map/ppermute | solution.py:763
  69.4 25.3 %collective-permute-start.18 = (bf16[192,1152]{1,0:T(8,128)(2,1)}, bf16[192,1152]{1,0:T(8,128)(2,1)}, u32[]{:S(2)}, u32[]{:S(2)}) collective-permute-start(bf16[192,1152]{1,0:T(8,128)(2,1)} %get-tuple-element.247), channel_id=1, source_target_pairs={{0,1},{1,0},{2,3},{3,2},{4,5},{5,4},{6,7},{7,6},{8,9},{9,8},{10,11... | collective-permute-start | bytes 1327112 | tf_op jit(solution)/shard_map/ppermute | solution.py:763
  70.4 24.2 %collective-permute-start.19 = (bf16[192,1152]{1,0:T(8,128)(2,1)}, bf16[192,1152]{1,0:T(8,128)(2,1)}, u32[]{:S(2)}, u32[]{:S(2)}) collective-permute-start(bf16[192,1152]{1,0:T(8,128)(2,1)} %get-tuple-element.269.refs_5_.refs_9_), channel_id=1, source_target_pairs={{0,2},{1,3},{2,0},{3,1},{4,6},{5,7},{6,4},{7,5},{8,10},{9,11},{10,... | collective-permute-start | bytes 1327112 | tf_op jit(solution)/shard_map/ppermute | solution.py:763
  132.0 35.2 %collective-permute-start.30 = (bf16[768,768]{1,0:T(8,128)(2,1)S(1)}, bf16[768,768]{1,0:T(8,128)(2,1)}, u32[]{:S(2)}, u32[]{:S(2)}) collective-permute-start(bf16[768,768]{1,0:T(8,128)(2,1)S(1)} %slice_bitcast_fusion.refs_8_), channel_id=1, source_target_pairs={{0,2},{1,3},{2,0},{3,1},{4,6},{5,7},{6,4},{7,5},{8,10},{9,11},{10,... | collective-permute-start | bytes 3538952 | tf_op jit(solution)/shard_map/ppermute | solution.py:763
  133.5 39.3 %collective-permute-start.29 = (bf16[192,1536]{1,0:T(8,128)(2,1)S(1)}, bf16[192,1536]{1,0:T(8,128)(2,1)}, u32[]{:S(2)}, u32[]{:S(2)}) collective-permute-start(bf16[192,1536]{1,0:T(8,128)(2,1)S(1)} %copy-done.38), channel_id=1, source_target_pairs={{0,3},{1,2},{2,1},{3,0},{4,7},{5,6},{6,5},{7,4},{8,11},{9,10},{10,... | collective-permute-start | bytes 1769480 | tf_op jit(solution)/shard_map/ppermute | solution.py:763
  134.0 38.9 %collective-permute-start.28 = (bf16[192,1536]{1,0:T(8,128)(2,1)S(1)}, bf16[192,1536]{1,0:T(8,128)(2,1)}, u32[]{:S(2)}, u32[]{:S(2)}) collective-permute-start(bf16[192,1536]{1,0:T(8,128)(2,1)S(1)} %copy-done.38), channel_id=1, source_target_pairs={{0,1},{1,0},{2,3},{3,2},{4,5},{5,4},{6,7},{7,6},{8,9},{9,8},{10,11... | collective-permute-start | bytes 1769480 | tf_op jit(solution)/shard_map/ppermute | solution.py:763
  201.8 30.0 %collective-permute-start.34 = (bf16[576,768]{1,0:T(8,128)(2,1)}, bf16[576,768]{1,0:T(8,128)(2,1)S(1)}, u32[]{:S(2)}, u32[]{:S(2)}) collective-permute-start(bf16[576,768]{1,0:T(8,128)(2,1)} %get-tuple-element.309), channel_id=1, source_target_pairs={{0,4},{4,0},{8,12},{12,8},{16,20},{20,16},{24,28},{28,24},{1,5},{5... | collective-permute-start | bytes 2654216 | tf_op jit(solution)/shard_map/ppermute | solution.py:915
  202.4 29.4 %collective-permute-start.35 = (bf16[192,768]{1,0:T(8,128)(2,1)}, bf16[192,768]{1,0:T(8,128)(2,1)S(1)}, u32[]{:S(2)}, u32[]{:S(2)}) collective-permute-start(bf16[192,768]{1,0:T(8,128)(2,1)} %get-tuple-element.310), channel_id=1, source_target_pairs={{0,1},{1,0},{2,3},{3,2},{4,5},{5,4},{6,7},{7,6},{8,9},{9,8},{10,11... | collective-permute-start | bytes 884744 | tf_op jit(solution)/shard_map/ppermute | solution.py:763
  205.7 26.1 %collective-permute-start.37 = (bf16[192,768]{1,0:T(8,128)(2,1)S(1)}, bf16[192,768]{1,0:T(8,128)(2,1)S(1)}, u32[]{:S(2)}, u32[]{:S(2)}) collective-permute-start(bf16[192,768]{1,0:T(8,128)(2,1)S(1)} %collective-permute-done.36), channel_id=1, source_target_pairs={{0,4},{4,0},{8,12},{12,8},{16,20},{20,16},{24,28},{28,24},{1,5},{5... | collective-permute-start | bytes 884744 | tf_op jit(solution)/shard_map/ppermute | solution.py:915
  232.4 30.2 %collective-permute-start.42 = (bf16[288,384]{1,0:T(8,128)(2,1)}, bf16[288,384]{1,0:T(8,128)(2,1)}, u32[]{:S(2)}, u32[]{:S(2)}) collective-permute-start(bf16[288,384]{1,0:T(8,128)(2,1)} %get-tuple-element.340), channel_id=1, source_target_pairs={{0,1},{1,0},{2,3},{3,2},{4,5},{5,4},{6,7},{7,6},{8,9},{9,8},{10,11... | collective-permute-start | bytes 663560 | tf_op jit(solution)/shard_map/ppermute | solution.py:763
  232.5 30.1 %collective-permute-start.41 = (bf16[480,384]{1,0:T(8,128)(2,1)}, bf16[480,384]{1,0:T(8,128)(2,1)S(1)}, u32[]{:S(2)}, u32[]{:S(2)}) collective-permute-start(bf16[480,384]{1,0:T(8,128)(2,1)} %get-tuple-element.339), channel_id=1, source_target_pairs={{0,4},{4,0},{8,12},{12,8},{16,20},{20,16},{24,28},{28,24},{1,5},{5... | collective-permute-start | bytes 1105928 | tf_op jit(solution)/shard_map/ppermute | solution.py:915
  237.9 24.8 %collective-permute-start.44 = (bf16[288,384]{1,0:T(8,128)(2,1)}, bf16[288,384]{1,0:T(8,128)(2,1)S(1)}, u32[]{:S(2)}, u32[]{:S(2)}) collective-permute-start(bf16[288,384]{1,0:T(8,128)(2,1)} %collective-permute-done.43), channel_id=1, source_target_pairs={{0,4},{4,0},{8,12},{12,8},{16,20},{20,16},{24,28},{28,24},{1,5},{5... | collective-permute-start | bytes 663560 | tf_op jit(solution)/shard_map/ppermute | solution.py:915
  238.4 24.3 %collective-permute-start.39 = (bf16[192,768]{1,0:T(8,128)(2,1)}, bf16[192,768]{1,0:T(8,128)(2,1)S(1)}, u32[]{:S(2)}, u32[]{:S(2)}) collective-permute-start(bf16[192,768]{1,0:T(8,128)(2,1)} %get-tuple-element.336), channel_id=1, source_target_pairs={{0,8},{4,12},{8,0},{12,4},{16,24},{20,28},{24,16},{28,20},{1,9},{5... | collective-permute-start | bytes 884744 | tf_op jit(solution)/shard_map/ppermute | solution.py:925
  263.6 42.3 %collective-permute-start.50 = (bf16[576,768]{1,0:T(8,128)(2,1)}, bf16[576,768]{1,0:T(8,128)(2,1)S(1)}, u32[]{:S(2)}, u32[]{:S(2)}) collective-permute-start(bf16[576,768]{1,0:T(8,128)(2,1)} %get-tuple-element.371), channel_id=1, source_target_pairs={{0,4},{4,0},{8,12},{12,8},{16,20},{20,16},{24,28},{28,24},{1,5},{5... | collective-permute-start | bytes 2654216 | tf_op jit(solution)/shard_map/ppermute | solution.py:915
  271.5 34.3 %collective-permute-start.48 = (bf16[192,384]{1,0:T(8,128)(2,1)}, bf16[192,384]{1,0:T(8,128)(2,1)S(1)}, u32[]{:S(2)}, u32[]{:S(2)}) collective-permute-start(bf16[192,384]{1,0:T(8,128)(2,1)} %get-tuple-element.350), channel_id=1, source_target_pairs={{0,16},{4,20},{8,24},{12,28},{16,0},{20,4},{24,8},{28,12},{1,17},{... | collective-permute-start | bytes 442376 | tf_op jit(solution)/shard_map/ppermute | solution.py:925
  277.2 28.7 %collective-permute-start.49 = (bf16[192,384]{1,0:T(8,128)(2,1)}, bf16[192,384]{1,0:T(8,128)(2,1)}, u32[]{:S(2)}, u32[]{:S(2)}) collective-permute-start(bf16[192,384]{1,0:T(8,128)(2,1)} %get-tuple-element.351), channel_id=1, source_target_pairs={{0,24},{4,28},{8,16},{12,20},{16,8},{20,12},{24,0},{28,4},{1,25},{... | collective-permute-start | bytes 442376 | tf_op jit(solution)/shard_map/ppermute | solution.py:925
  279.6 26.2 %collective-permute-start.51 = (bf16[192,768]{1,0:T(8,128)(2,1)}, bf16[192,768]{1,0:T(8,128)(2,1)S(1)}, u32[]{:S(2)}, u32[]{:S(2)}) collective-permute-start(bf16[192,768]{1,0:T(8,128)(2,1)} %get-tuple-element.372), channel_id=1, source_target_pairs={{0,1},{1,0},{2,3},{3,2},{4,5},{5,4},{6,7},{7,6},{8,9},{9,8},{10,11... | collective-permute-start | bytes 884744 | tf_op jit(solution)/shard_map/ppermute | solution.py:763
  279.7 26.2 %collective-permute-start.53 = (bf16[192,768]{1,0:T(8,128)(2,1)}, bf16[192,768]{1,0:T(8,128)(2,1)S(1)}, u32[]{:S(2)}, u32[]{:S(2)}) collective-permute-start(bf16[192,768]{1,0:T(8,128)(2,1)} %collective-permute-done.52), channel_id=1, source_target_pairs={{0,4},{4,0},{8,12},{12,8},{16,20},{20,16},{24,28},{28,24},{1,5},{5... | collective-permute-start | bytes 884744 | tf_op jit(solution)/shard_map/ppermute | solution.py:915
  306.5 106.1 %collective-permute-start.54 = (bf16[1024,768]{1,0:T(8,128)(2,1)}, bf16[1024,768]{1,0:T(8,128)(2,1)}, u32[]{:S(2)}, u32[]{:S(2)}) collective-permute-start(bf16[1024,768]{1,0:T(8,128)(2,1)} %get-tuple-element.375.p_ref), channel_id=1, source_target_pairs={{0,1},{1,0},{2,3},{3,2},{4,5},{5,4},{6,7},{7,6},{8,9},{9,8},{10,11... | collective-permute-start | bytes 4718600 | tf_op jit(solution)/shard_map/ppermute | solution.py:763
  329.5 36.3 %collective-permute-start.71 = (bf16[192,768]{1,0:T(8,128)(2,1)}, bf16[192,768]{1,0:T(8,128)(2,1)S(1)}, u32[]{:S(2)}, u32[]{:S(2)}) collective-permute-start(bf16[192,768]{1,0:T(8,128)(2,1)} %get-tuple-element.399), channel_id=1, source_target_pairs={{0,16},{4,20},{8,24},{12,28},{16,0},{20,4},{24,8},{28,12},{1,17},{... | collective-permute-start | bytes 884744 | tf_op jit(solution)/shard_map/ppermute | solution.py:925
  330.4 36.2 %collective-permute-start.72 = (bf16[192,768]{1,0:T(8,128)(2,1)}, bf16[192,768]{1,0:T(8,128)(2,1)S(1)}, u32[]{:S(2)}, u32[]{:S(2)}) collective-permute-start(bf16[192,768]{1,0:T(8,128)(2,1)} %get-tuple-element.400), channel_id=1, source_target_pairs={{0,24},{4,28},{8,16},{12,20},{16,8},{20,12},{24,0},{28,4},{1,25},{... | collective-permute-start | bytes 884744 | tf_op jit(solution)/shard_map/ppermute | solution.py:925
  334.1 34.4 %collective-permute-start.79 = (bf16[192,768]{1,0:T(8,128)(2,1)S(1)}, bf16[192,768]{1,0:T(8,128)(2,1)S(1)}, u32[]{:S(2)}, u32[]{:S(2)}) collective-permute-start(bf16[192,768]{1,0:T(8,128)(2,1)S(1)} %add_convert_fusion), channel_id=1, source_target_pairs={{0,24},{4,28},{8,16},{12,20},{16,8},{20,12},{24,0},{28,4},{1,25},{... | collective-permute-start | bytes 884744 | tf_op jit(solution)/shard_map/ppermute | solution.py:936
  339.3 51.8 %collective-permute-start.78 = (bf16[192,768]{1,0:T(8,128)(2,1)S(1)}, bf16[192,768]{1,0:T(8,128)(2,1)S(1)}, u32[]{:S(2)}, u32[]{:S(2)}) collective-permute-start(bf16[192,768]{1,0:T(8,128)(2,1)S(1)} %add_convert_fusion), channel_id=1, source_target_pairs={{0,16},{4,20},{8,24},{12,28},{16,0},{20,4},{24,8},{28,12},{1,17},{... | collective-permute-start | bytes 884744 | tf_op jit(solution)/shard_map/ppermute | solution.py:936
  365.8 25.3 %collective-permute-start.77 = (bf16[192,768]{1,0:T(8,128)(2,1)S(1)}, bf16[192,768]{1,0:T(8,128)(2,1)S(1)}, u32[]{:S(2)}, u32[]{:S(2)}) collective-permute-start(bf16[192,768]{1,0:T(8,128)(2,1)S(1)} %add_convert_fusion), channel_id=1, source_target_pairs={{0,8},{4,12},{8,0},{12,4},{16,24},{20,28},{24,16},{28,20},{1,9},{5... | collective-permute-start | bytes 884744 | tf_op jit(solution)/shard_map/ppermute | solution.py:936
  366.6 31.2 %collective-permute-start.55 = (bf16[480,384]{1,0:T(8,128)(2,1)S(1)}, bf16[480,384]{1,0:T(8,128)(2,1)S(1)}, u32[]{:S(2)}, u32[]{:S(2)}) collective-permute-start(bf16[480,384]{1,0:T(8,128)(2,1)S(1)} %copy-done.41), channel_id=1, source_target_pairs={{0,4},{4,0},{8,12},{12,8},{16,20},{20,16},{24,28},{28,24},{1,5},{5... | collective-permute-start | bytes 1105928 | tf_op jit(solution)/shard_map/ppermute | solution.py:915
  368.5 38.9 %collective-permute-start.75 = (bf16[192,768]{1,0:T(8,128)(2,1)S(1)}, bf16[192,768]{1,0:T(8,128)(2,1)S(1)}, u32[]{:S(2)}, u32[]{:S(2)}) collective-permute-start(bf16[192,768]{1,0:T(8,128)(2,1)S(1)} %add_convert_fusion.1), channel_id=1, source_target_pairs={{0,24},{4,28},{8,16},{12,20},{16,8},{20,12},{24,0},{28,4},{1,25},{... | collective-permute-start | bytes 884744 | tf_op jit(solution)/shard_map/ppermute | solution.py:936
  403.8 43.7 %collective-permute-start.32 = (bf16[1024,768]{1,0:T(8,128)(2,1)}, bf16[1024,768]{1,0:T(8,128)(2,1)}, u32[]{:S(2)}, u32[]{:S(2)}) collective-permute-start(bf16[1024,768]{1,0:T(8,128)(2,1)} %get-tuple-element.291), channel_id=1, source_target_pairs={{0,1},{1,0},{2,3},{3,2},{4,5},{5,4},{6,7},{7,6},{8,9},{9,8},{10,11... | collective-permute-start | bytes 4718600 | tf_op jit(solution)/shard_map/ppermute | solution.py:763
  407.4 84.7 %collective-permute-start.80 = (bf16[4,192,768]{2,1,0:T(8,128)(2,1)}, bf16[4,192,768]{2,1,0:T(8,128)(2,1)}, u32[]{:S(2)}, u32[]{:S(2)}) collective-permute-start(bf16[4,192,768]{2,1,0:T(8,128)(2,1)} %bitcast.29.near), channel_id=1, source_target_pairs={{0,4},{4,0},{8,12},{12,8},{16,20},{20,16},{24,28},{28,24},{1,5},{5... | collective-permute-start | bytes 3538952 | tf_op jit(solution)/shard_map/ppermute | solution.py:941
  439.2 61.2 %collective-permute-start.76 = (bf16[4,192,768]{2,1,0:T(8,128)(2,1)S(1)}, bf16[4,192,768]{2,1,0:T(8,128)(2,1)}, u32[]{:S(2)}, u32[]{:S(2)}) collective-permute-start(bf16[4,192,768]{2,1,0:T(8,128)(2,1)S(1)} %bitcast.54), channel_id=1, source_target_pairs={{0,4},{4,0},{8,12},{12,8},{16,20},{20,16},{24,28},{28,24},{1,5},{5... | collective-permute-start | bytes 3538952 | tf_op jit(solution)/shard_map/ppermute | solution.py:941
  446.1 42.3 %collective-permute-start.65 = (bf16[4,192,384]{2,1,0:T(8,128)(2,1)S(1)}, bf16[4,192,384]{2,1,0:T(8,128)(2,1)}, u32[]{:S(2)}, u32[]{:S(2)}) collective-permute-start(bf16[4,192,384]{2,1,0:T(8,128)(2,1)S(1)} %bitcast.56), channel_id=1, source_target_pairs={{0,4},{4,0},{8,12},{12,8},{16,20},{20,16},{24,28},{28,24},{1,5},{5... | collective-permute-start | bytes 1769480 | tf_op jit(solution)/shard_map/ppermute | solution.py:941
  447.4 49.6 %collective-permute-start.83 = (f32[2,2304]{1,0:T(2,128)S(1)}, f32[2,2304]{1,0:T(2,128)S(1)}, u32[]{:S(2)}, u32[]{:S(2)}) collective-permute-start(f32[2,2304]{1,0:T(2,128)S(1)} %fusion.4), channel_id=1, source_target_pairs={{0,16},{4,20},{8,24},{12,28},{16,0},{20,4},{24,8},{28,12},{1,17},{... | collective-permute-start | bytes 55304 | tf_op jit(solution)/shard_map/ppermute | solution.py:1024
  (96 other events, 1254.3 us)
